TPU v7x, 128 devices: a whole 4x4x4 slice. The times are simulated.
128 devices in a mesh: dp: 8 (over y_hi, x), cuts: 16 (over z, y_lo, core).
Axes of the slice: x: 4, y: 4 (y_hi: 2, y_lo: 2; y = y_hi * 2 + y_lo), z: 4, core: 2. Of those that a mesh axis runs over, the one named last changes fastest.
Arguments:
- feat_table: bfloat16 [1024, 131072], P('cuts', 'dp'), may hold values from -6 to 6
- self_one: int32 [32768], P('dp'), may hold values from 0 to 16383
- near_one: int32 [5, 32768], P(None, 'dp'), may hold values from 0 to 16383
- self_two: int32 [16384], P(('dp', 'cuts')), may hold values from 0 to 255
- near_two: int32 [10, 16384], P(None, ('dp', 'cuts')), may hold values from 0 to 255
- self_three: int32 [4096], P(('dp', 'cuts')), may hold values from 0 to 127
- near_three: int32 [15, 4096], P(None, ('dp', 'cuts')), may hold values from 0 to 127
- targets: int32 [4096, 112], P(('dp', 'cuts')), may hold values 0 or 1
- seed_count: int32 [128], replicated, may hold values from 8 to 32, as said below
- w_one: bfloat16 [2, 1024, 512], P(None, 'cuts'), may hold values from -0.1875 to 0.1875
- bias_one: float32 [512], replicated, may hold values from -3 to 3
- w_two: bfloat16 [2, 512, 512], replicated, may hold values from -0.25 to 0.25
- bias_two: float32 [512], replicated, may hold values from -3 to 3
- w_three: bfloat16 [2, 512, 112], replicated, may hold values from -0.25 to 0.25
- bias_three: float32 [112], replicated, may hold values from -4 to 4
Outputs:
- grad_one: float32 [2, 1024, 512], P(None, 'cuts')
- grad_bias_one: float32 [512], replicated
- grad_two: float32 [2, 512, 512], replicated
- grad_bias_two: float32 [512], replicated
- grad_three: float32 [2, 512, 112], replicated
- grad_bias_three: float32 [112], replicated
Inputs may be any that keep to these rules, and one draw needn't show every extreme that they name: `seed_count`: one owner has all 32 seeds live; the others have at least a quarter of them.
All inputs are finite; a program needn't handle non-finite values. No bound on the sum of `targets` on one device may be relied on, other than what follows from the above.
Results may differ from a plain program's by a relative error of at most 0.0065.
Values may be sent and summed in bfloat16 or wider, within the bound.
No kernel may reach another device: no remote copies, remote signals or barrier semaphores. Data moves between devices by JAX's collectives and lax.ppermute only.
A program may use at most 64 MiB of HBM per device.

v0:
```python
import jax
import jax.numpy as jnp
from jax import lax
from jax.sharding import PartitionSpec as P


def gelu_tanh(values):
    return jax.nn.gelu(values, approximate=True)


def gelu_back(pre_act, upstream):
    return jax.vjp(gelu_tanh, pre_act)[1](upstream)[0]


def lead_dot(first_mat, second_mat):
    return lax.dot_general(
        first_mat, second_mat, (((0,), (0,)), ((), ())), preferred_element_type=jnp.float32
    )


def plain_dot(first_mat, second_mat):
    return jnp.dot(first_mat, second_mat, preferred_element_type=jnp.float32)


def back_dot(first_mat, second_mat):
    return lax.dot_general(
        first_mat, second_mat, (((1,), (1,)), ((), ())), preferred_element_type=jnp.float32
    )


def gather_mean(row_table, near_ids):
    fan_count = near_ids.shape[0]
    running_sum = jnp.zeros((near_ids.shape[1], row_table.shape[1]), jnp.float32)
    for offset in range(fan_count):
        running_sum = running_sum + row_table[near_ids[offset]].astype(jnp.float32)
    return (running_sum / fan_count).astype(jnp.bfloat16)


def spread_back(row_total, self_ids, near_ids, self_grad, near_grad):
    result = jnp.zeros((row_total, self_grad.shape[1]), jnp.float32).at[self_ids].add(self_grad)
    for offset in range(near_ids.shape[0]):
        result = result.at[near_ids[offset]].add(near_grad)
    return result


def owner_pass(
    hidden_one,
    self_two,
    near_two,
    self_three,
    near_three,
    targets,
    live_mask,
    loss_scale,
    w_two,
    bias_two,
    w_three,
    bias_three,
):
    self_mid = hidden_one[self_two]
    near_mid = gather_mean(hidden_one, near_two)
    pre_two = plain_dot(self_mid, w_two[0]) + plain_dot(near_mid, w_two[1]) + bias_two
    hidden_two = gelu_tanh(pre_two).astype(jnp.bfloat16)
    self_top = hidden_two[self_three]
    near_top = gather_mean(hidden_two, near_three)
    logits = plain_dot(self_top, w_three[0]) + plain_dot(near_top, w_three[1]) + bias_three
    logit_grad = (
        (jax.nn.sigmoid(logits) - targets.astype(jnp.float32)) * (live_mask[:, None] * loss_scale)
    ).astype(jnp.bfloat16)
    grad_three = jnp.stack([lead_dot(self_top, logit_grad), lead_dot(near_top, logit_grad)])
    bias_grad_three = jnp.sum(logit_grad.astype(jnp.float32), axis=0)
    hidden_grad_two = spread_back(
        hidden_two.shape[0],
        self_three,
        near_three,
        back_dot(logit_grad, w_three[0]),
        back_dot(logit_grad, w_three[1]) / near_three.shape[0],
    )
    pre_grad_two = gelu_back(pre_two, hidden_grad_two).astype(jnp.bfloat16)
    grad_two = jnp.stack([lead_dot(self_mid, pre_grad_two), lead_dot(near_mid, pre_grad_two)])
    bias_grad_two = jnp.sum(pre_grad_two.astype(jnp.float32), axis=0)
    hidden_grad_one = spread_back(
        hidden_one.shape[0],
        self_two,
        near_two,
        back_dot(pre_grad_two, w_two[0]),
        back_dot(pre_grad_two, w_two[1]) / near_two.shape[0],
    )
    return (hidden_grad_one, grad_two, bias_grad_two, grad_three, bias_grad_three)


def local(
    feat_table,
    self_one,
    near_one,
    self_two,
    near_two,
    self_three,
    near_three,
    targets,
    seed_count,
    w_one,
    bias_one,
    w_two,
    bias_two,
    w_three,
    bias_three,
):
    cut_count = lax.axis_size("cuts")
    column_count = feat_table.shape[0]
    self_feat = jnp.take(feat_table, self_one, axis=1)
    running_sum = jnp.zeros((column_count, self_one.shape[0]), jnp.float32)
    for offset in range(near_one.shape[0]):
        running_sum = running_sum + jnp.take(feat_table, near_one[offset], axis=1).astype(
            jnp.float32
        )
    near_feat = (running_sum / near_one.shape[0]).astype(jnp.bfloat16)
    owner_index = lax.axis_index("dp") * cut_count + lax.axis_index("cuts")
    live_mask = (jnp.arange(self_three.shape[0]) < seed_count[owner_index]).astype(jnp.float32)
    loss_scale = 1.0 / jnp.sqrt(jnp.sum(seed_count).astype(jnp.float32))
    self_part = self_feat
    near_part = near_feat
    pre_one = (
        lax.psum_scatter(
            lead_dot(self_part, w_one[0]) + lead_dot(near_part, w_one[1]),
            "cuts",
            scatter_dimension=0,
            tiled=True,
        )
        + bias_one
    )
    hidden_one = gelu_tanh(pre_one).astype(jnp.bfloat16)
    hidden_grad, grad_two, bias_grad_two, grad_three, bias_grad_three = owner_pass(
        hidden_one,
        self_two,
        near_two,
        self_three,
        near_three,
        targets,
        live_mask,
        loss_scale,
        w_two,
        bias_two,
        w_three,
        bias_three,
    )
    pre_grad_one = gelu_back(pre_one, hidden_grad).astype(jnp.bfloat16)
    block_rows = lax.all_gather(pre_grad_one, "cuts", axis=0, tiled=True)
    self_part = self_feat
    near_part = near_feat
    grad_one_part = jnp.stack([plain_dot(self_part, block_rows), plain_dot(near_part, block_rows)])
    grad_one = lax.psum(grad_one_part, "dp")
    bias_grad_one = jnp.sum(pre_grad_one.astype(jnp.float32), axis=0)
    layer_sums = lax.psum(
        (grad_two, bias_grad_two, grad_three, bias_grad_three, bias_grad_one), ("dp", "cuts")
    )
    return (grad_one, layer_sums[4], layer_sums[0], layer_sums[1], layer_sums[2], layer_sums[3])


def solution(mesh):
    return jax.shard_map(
        local,
        mesh=mesh,
        in_specs=(
            P("cuts", "dp"),
            P("dp"),
            P(None, "dp"),
            P(("dp", "cuts")),
            P(None, ("dp", "cuts")),
            P(("dp", "cuts")),
            P(None, ("dp", "cuts")),
            P(("dp", "cuts"), None),
            P(),
            P(None, "cuts", None),
            P(),
            P(),
            P(),
            P(),
            P(),
        ),
        out_specs=(P(None, "cuts", None), P(), P(), P(), P(), P()),
        check_vma=False,
    )
```

profile of v0, /device:TPU:1, one launch (start us, length us, event | category | flops | bytes accessed | tf_op | source)
XLA Modules:
  0.0 595.7 jit_solution(13698020155040161216)
XLA Ops:
  7.2 1.3 fusion.89
  10.1 4.8 copy.21
  14.9 13.8 %gather_fusion.28 = bf16[4096,64]{1,0:T(8,128)(2,1)S(1)} fusion(bf16[64,16384]{0,1:T(8,128)(2,1)} %copy.21, s32[4096]{0:T(1024)S(1)} %fusion.55), kind=kCustom, calls=%fused_computation.1.clone | custom fusion | bytes 1064960 | tf_op jit(solution)/shard_map/jit(_take)/gather | solution.py:114
  28.6 17.0 %gather_fusion.29 = bf16[4096,64]{1,0:T(8,128)(2,1)} fusion(bf16[64,16384]{0,1:T(8,128)(2,1)} %copy.21, s32[4096]{0:T(1024)S(1)} %fusion.56), kind=kCustom, calls=%fused_computation.2.clone | custom fusion | bytes 1064960 | tf_op jit(solution)/shard_map/jit(_take)/gather | solution.py:114
  45.6 17.0 %gather_fusion.30 = bf16[4096,64]{1,0:T(8,128)(2,1)} fusion(bf16[64,16384]{0,1:T(8,128)(2,1)} %copy.21, s32[4096]{0:T(1024)S(1)} %fusion.57), kind=kCustom, calls=%fused_computation.3.clone | custom fusion | bytes 1064960 | tf_op jit(solution)/shard_map/jit(_take)/gather | solution.py:114
  62.6 16.9 %gather_fusion.31 = bf16[4096,64]{1,0:T(8,128)(2,1)} fusion(bf16[64,16384]{0,1:T(8,128)(2,1)} %copy.21, s32[4096]{0:T(1024)S(1)} %fusion.58), kind=kCustom, calls=%fused_computation.4.clone | custom fusion | bytes 1064960 | tf_op jit(solution)/shard_map/jit(_take)/gather | solution.py:114
  79.5 17.1 %gather_fusion.32 = bf16[4096,64]{1,0:T(8,128)(2,1)} fusion(bf16[64,16384]{0,1:T(8,128)(2,1)} %copy.21, s32[4096]{0:T(1024)S(1)} %fusion.59), kind=kCustom, calls=%fused_computation.5.clone | custom fusion | bytes 1064960 | tf_op jit(solution)/shard_map/jit(_take)/gather | solution.py:114
  96.6 13.8 %gather_fusion.27 = bf16[4096,64]{1,0:T(8,128)(2,1)S(1)} fusion(bf16[64,16384]{0,1:T(8,128)(2,1)} %copy.21, s32[4096]{0:T(1024)S(1)} %fusion.54), kind=kCustom, calls=%fused_computation.clone | custom fusion | bytes 1064960 | tf_op jit(solution)/shard_map/jit(_take)/gather | solution.py:111
  110.4 1.3 fusion.10
  112.6 3.9 multiply_convert_fusion
  116.5 4.4 convolution_add_fusion
  130.8 89.7 %reduce-scatter.2.cloned.1.call-done = f32[256,512]{1,0:T(8,128)} async-done(((f32[4096,512]{1,0:T(8,128)}), f32[256,512]{1,0:T(8,128)}) %reduce-scatter.2.cloned.1.call-update) | async-done | bytes 524304 | tf_op jit(solution)/shard_map/reduce_scatter | solution.py:124
  220.5 1.2 multiply_convert_fusion.1
  221.7 1.5 gather_fusion.4
  223.2 1.5 gather_fusion.5
  224.7 1.5 gather_fusion.6
  226.2 1.5 gather_fusion.7
  227.7 1.5 gather_fusion.8
  229.2 1.5 gather_fusion.9
  230.7 1.5 gather_fusion.10
  232.4 1.5 gather_fusion.1
  233.9 1.5 gather_fusion.2
  235.4 1.5 gather_fusion.3
  238.1 1.5 multiply_convert_fusion.3
  239.7 1.7 multiply_convert_fusion.2
  241.4 1.3 gather_fusion.13
  242.7 1.3 gather_fusion.14
  244.1 1.3 gather_fusion.15
  245.4 1.4 gather_fusion.16
  246.8 1.3 gather_fusion.17
  248.1 1.3 gather_fusion.18
  249.5 1.3 gather_fusion.19
  250.8 1.4 gather_fusion.20
  252.2 1.3 gather_fusion.21
  253.5 1.3 gather_fusion.22
  254.9 1.3 gather_fusion.23
  256.2 1.4 gather_fusion.24
  257.6 1.3 gather_fusion.25
  258.9 1.4 gather_fusion.26
  261.5 1.2 gather_fusion.11
  264.9 1.6 convert_reduce_fusion.2
  284.5 1.7 convert_reduce_fusion.1
  286.5 1.3 convolution_multiply_fusion
  287.9 1.8 scatter_custom_fusion.16
  289.7 1.7 scatter_fusion.15
  291.4 1.7 scatter_fusion.16
  293.1 1.6 scatter_fusion.17
  294.7 1.6 scatter_fusion.18
  296.3 1.6 scatter_fusion.19
  297.8 1.6 scatter_fusion.20
  299.4 1.6 scatter_fusion.21
  301.0 1.6 scatter_fusion.22
  302.6 1.6 scatter_fusion.23
  304.2 1.6 scatter_fusion.24
  305.8 2.1 convert_reduce_fusion
  309.9 1.5 pad_maximum_fusion
  311.5 34.9 %all-gather.2.cloned.1.call-done = bf16[4096,512]{1,0:T(8,128)(2,1)} async-done(((bf16[256,512]{1,0:T(8,128)(2,1)}), bf16[4096,512]{1,0:T(8,128)(2,1)}) %all-gather.2.cloned.1.call-update) | async-done | bytes 4194320 | tf_op jit(solution)/shard_map/all_gather | solution.py:148
  346.4 3.2 convolution_bitcast_fusion.4
  349.9 1.5 convolution_bitcast_fusion.5
  352.2 65.3 %all-reduce = (f32[512]{0:T(512)}, f32[512]{0:T(512)}, f32[112]{0:T(128)}) all-reduce(f32[512]{0:T(512)S(1)} %get-tuple-element.14, f32[512]{0:T(512)S(1)} %copy-done.16, f32[112]{0:T(128)S(1)} %copy-done.60), channel_id=1, replica_groups=mesh['dp'=8,'cuts'=16] {'dp','cuts'}, use_global_device_ids=true, to_apply=%region_31.33 | all-reduce | flops 1136 | bytes 9088 | tf_op jit(solution)/shard_map/psum | solution.py:154
  417.4 85.9 %all-reduce.7.cloned.1.call-done = (f32[2,512,512]{2,1,0:T(8,128)}, f32[2,512,112]{1,2,0:T(8,128)}) async-done(((f32[2,512,512]{2,1,0:T(8,128)}, f32[2,512,112]{1,2,0:T(8,128)}), (f32[2,512,512]{2,1,0:T(8,128)}, f32[2,512,112]{1,2,0:T(8,128)})) %all-reduce.7.cloned.1.call-update) | async-done | bytes 2555920 | tf_op jit(solution)/shard_map/psum | solution.py:154
  503.3 80.4 %all-reduce.5.cloned.1.call-done = f32[2,64,512]{2,1,0:T(8,128)} async-done(((f32[2,64,512]{2,1,0:T(8,128)}), f32[2,64,512]{2,1,0:T(8,128)}) %all-reduce.5.cloned.1.call-update) | async-done | bytes 262160 | tf_op jit(solution)/shard_map/psum | solution.py:152
  583.7 1.7 copy.55
  585.3 3.1 copy.56
  (201 shorter events, 37.6 us)
Async XLA Ops:
  7.2 213.3 %reduce-scatter.2.cloned.1.call-start = ((), (), s32[]{:S(2)}) async-start(), calls=%async_computation.1 | async-start | bytes 8912896 | tf_op jit(solution)/shard_map/reduce_scatter | solution.py:124
  79.5 30.9 %copy-start.12 = (bf16[2,64,512]{2,1,0:T(8,128)(2,1)S(1)}, bf16[2,64,512]{2,1,0:T(8,128)(2,1)}, u32[]{:S(2)}) copy-start(bf16[2,64,512]{2,1,0:T(8,128)(2,1)} %param.26) | copy-start | bytes 393220
  110.4 1.4 copy-start.2
  110.4 1.5 copy-start.3
  110.4 1.8 copy-start.4
  110.4 2.1 copy-start.5
  120.9 0.7 copy-start.62
  120.9 3.7 copy-start.63
  120.9 4.3 copy-start.17
  120.9 4.9 copy-start.64
  121.0 4.9 copy-start.58
  121.0 99.5 %copy-start.15 = (f32[512]{0:T(512)S(1)}, f32[512]{0:T(512)}, u32[]{:S(2)}) copy-start(f32[512]{0:T(512)} %param.27) | copy-start | bytes 6148
  121.0 225.4 %all-gather.2.cloned.1.call-start = ((), (), s32[]{:S(2)}) async-start(), calls=%async_computation.2 | async-start | bytes 4456448 | tf_op jit(solution)/shard_map/all_gather | solution.py:148
  124.7 107.6 %copy-start.59 = (s32[128]{0:T(128)}, s32[128]{0:T(128)S(1)}, u32[]{:S(2)}) copy-start(s32[128]{0:T(128)S(1)} %compare_select_fusion.32) | copy-start | bytes 1540
  125.3 106.9 %copy-start.36 = (s32[32]{0:T(128)}, s32[32]{0:T(128)S(1)}, u32[]{:S(2)}) copy-start(s32[32]{0:T(128)S(1)} %get-tuple-element.34) | copy-start | bytes 388
  125.3 106.9 %copy-start.38 = (s32[32]{0:T(128)}, s32[32]{0:T(128)S(1)}, u32[]{:S(2)}) copy-start(s32[32]{0:T(128)S(1)} %get-tuple-element.35) | copy-start | bytes 388
  125.3 106.9 %copy-start.40 = (s32[32]{0:T(128)}, s32[32]{0:T(128)S(1)}, u32[]{:S(2)}) copy-start(s32[32]{0:T(128)S(1)} %get-tuple-element.22) | copy-start | bytes 388
  125.3 106.9 %copy-start.42 = (s32[32]{0:T(128)}, s32[32]{0:T(128)S(1)}, u32[]{:S(2)}) copy-start(s32[32]{0:T(128)S(1)} %get-tuple-element.23) | copy-start | bytes 388
  125.3 106.9 %copy-start.44 = (s32[32]{0:T(128)}, s32[32]{0:T(128)S(1)}, u32[]{:S(2)}) copy-start(s32[32]{0:T(128)S(1)} %get-tuple-element.24) | copy-start | bytes 388
  125.4 106.9 %copy-start.46 = (s32[32]{0:T(128)}, s32[32]{0:T(128)S(1)}, u32[]{:S(2)}) copy-start(s32[32]{0:T(128)S(1)} %get-tuple-element.25) | copy-start | bytes 388
  125.4 106.9 %copy-start.48 = (s32[32]{0:T(128)}, s32[32]{0:T(128)S(1)}, u32[]{:S(2)}) copy-start(s32[32]{0:T(128)S(1)} %get-tuple-element.26) | copy-start | bytes 388
  125.4 106.9 %copy-start.50 = (s32[32]{0:T(128)}, s32[32]{0:T(128)S(1)}, u32[]{:S(2)}) copy-start(s32[32]{0:T(128)S(1)} %get-tuple-element.27) | copy-start | bytes 388
  125.4 106.9 %copy-start.51 = (s32[32]{0:T(128)}, s32[32]{0:T(128)S(1)}, u32[]{:S(2)}) copy-start(s32[32]{0:T(128)S(1)} %get-tuple-element.28) | copy-start | bytes 388
  125.4 106.9 %copy-start.52 = (s32[32]{0:T(128)}, s32[32]{0:T(128)S(1)}, u32[]{:S(2)}) copy-start(s32[32]{0:T(128)S(1)} %get-tuple-element.29) | copy-start | bytes 388
  125.4 106.9 %copy-start.53 = (s32[32]{0:T(128)}, s32[32]{0:T(128)S(1)}, u32[]{:S(2)}) copy-start(s32[32]{0:T(128)S(1)} %get-tuple-element.30) | copy-start | bytes 388
  125.4 106.9 %copy-start.54 = (s32[32]{0:T(128)}, s32[32]{0:T(128)S(1)}, u32[]{:S(2)}) copy-start(s32[32]{0:T(128)S(1)} %get-tuple-element.31) | copy-start | bytes 388
  125.4 106.9 %copy-start.55 = (s32[32]{0:T(128)}, s32[32]{0:T(128)S(1)}, u32[]{:S(2)}) copy-start(s32[32]{0:T(128)S(1)} %get-tuple-element.32) | copy-start | bytes 388
  125.4 106.9 %copy-start.56 = (s32[32]{0:T(128)}, s32[32]{0:T(128)S(1)}, u32[]{:S(2)}) copy-start(s32[32]{0:T(128)S(1)} %get-tuple-element.33) | copy-start | bytes 388
  125.9 106.5 %copy-start.61 = (s32[32]{0:T(128)}, s32[32]{0:T(128)S(1)}, u32[]{:S(2)}) copy-start(s32[32]{0:T(128)S(1)} %compare_select_fusion.31) | copy-start | bytes 388
  126.0 0.6 copy-start.28
  126.0 0.6 copy-start.22
  126.0 0.6 copy-start.18
  126.0 0.6 copy-start.20
  126.0 106.4 %copy-start.34 = (s32[128]{0:T(128)}, s32[128]{0:T(128)S(1)}, u32[]{:S(2)}) copy-start(s32[128]{0:T(128)S(1)} %get-tuple-element.43) | copy-start | bytes 1540
  126.0 106.4 %copy-start.35 = (s32[128]{0:T(128)}, s32[128]{0:T(128)S(1)}, u32[]{:S(2)}) copy-start(s32[128]{0:T(128)S(1)} %get-tuple-element.36) | copy-start | bytes 1540
  227.7 10.1 %copy-start.1 = (bf16[2,512,512]{2,1,0:T(8,128)(2,1)S(1)}, bf16[2,512,512]{2,1,0:T(8,128)(2,1)}, u32[]{:S(2)}) copy-start(bf16[2,512,512]{2,1,0:T(8,128)(2,1)} %param.28) | copy-start | bytes 3145732
  237.9 24.9 %copy-start.6 = (bf16[128,512]{1,0:T(8,128)(2,1)}, bf16[128,512]{1,0:T(8,128)(2,1)S(1)}, u32[]{:S(2)}) copy-start(bf16[128,512]{1,0:T(8,128)(2,1)S(1)} %gather_fusion) | copy-start | bytes 393220
  239.7 27.9 %copy-start.8 = (bf16[128,512]{1,0:T(8,128)(2,1)}, bf16[128,512]{1,0:T(8,128)(2,1)S(1)}, u32[]{:S(2)}) copy-start(bf16[128,512]{1,0:T(8,128)(2,1)S(1)} %multiply_convert_fusion.3) | copy-start | bytes 393220
  264.9 1.7 copy-start.13
  269.6 8.4 %copy-start.49 = (s32[32]{0:T(128)S(1)}, s32[32]{0:T(128)}, u32[]{:S(2)}) copy-start(s32[32]{0:T(128)} %copy-done.48) | copy-start | bytes 388
  270.6 8.3 %copy-start.47 = (s32[32]{0:T(128)S(1)}, s32[32]{0:T(128)}, u32[]{:S(2)}) copy-start(s32[32]{0:T(128)} %copy-done.46) | copy-start | bytes 388
  271.7 8.2 %copy-start.45 = (s32[32]{0:T(128)S(1)}, s32[32]{0:T(128)}, u32[]{:S(2)}) copy-start(s32[32]{0:T(128)} %copy-done.44) | copy-start | bytes 388
  272.7 8.0 %copy-start.43 = (s32[32]{0:T(128)S(1)}, s32[32]{0:T(128)}, u32[]{:S(2)}) copy-start(s32[32]{0:T(128)} %copy-done.42) | copy-start | bytes 388
  273.8 7.9 %copy-start.41 = (s32[32]{0:T(128)S(1)}, s32[32]{0:T(128)}, u32[]{:S(2)}) copy-start(s32[32]{0:T(128)} %copy-done.40) | copy-start | bytes 388
  274.8 7.8 %copy-start.39 = (s32[32]{0:T(128)S(1)}, s32[32]{0:T(128)}, u32[]{:S(2)}) copy-start(s32[32]{0:T(128)} %copy-done.38) | copy-start | bytes 388
  275.9 7.7 %copy-start.37 = (s32[32]{0:T(128)S(1)}, s32[32]{0:T(128)}, u32[]{:S(2)}) copy-start(s32[32]{0:T(128)} %copy-done.36) | copy-start | bytes 388
  289.7 3.4 copy-start.33
  291.4 3.3 copy-start.31
  293.1 3.2 copy-start.29
  294.7 3.2 copy-start.27
  296.2 3.2 copy-start.25
  297.8 3.2 copy-start.23
  299.4 3.2 copy-start.21
  301.0 3.2 copy-start.19
  302.6 5.4 copy-start.11
  304.2 4.0 copy-start.14
  304.2 5.1 copy-start.7
  304.2 5.4 copy-start.9
  307.9 195.4 %all-reduce.7.cloned.1.call-start = ((), (), s32[]{:S(2)}) async-start(), calls=%async_computation.4 | async-start | bytes 5111808 | tf_op jit(solution)/shard_map/psum | solution.py:154
  311.4 272.2 %all-reduce.5.cloned.1.call-start = ((), (), s32[]{:S(2)}) async-start(), calls=%async_computation.3 | async-start | bytes 524288 | tf_op jit(solution)/shard_map/psum | solution.py:152
  346.4 3.4 copy-start
  349.9 2.3 copy-start.16
  349.9 2.3 copy-start.60
  503.3 85.1 %copy-start.10 = (f32[2,512,112]{1,2,0:T(8,128)S(1)}, f32[2,512,112]{1,2,0:T(8,128)}, u32[]{:S(2)}) copy-start(f32[2,512,112]{1,2,0:T(8,128)} %get-tuple-element.82) | copy-start | bytes 1376260
  (5 other events, 2.8 us)
Sparse Core Ops, SparseCore 0:
  121.1 99.3 reduce-scatter.1
  308.1 38.3 all-gather.1
  351.9 151.3 all-reduce.6
  506.4 77.2 all-reduce.4
where the time goes:
time: 602 us; the launch traced here: 596 us
  waiting for transfers between devices  291 us (48%)
  local copies, waits for them, and re-layouts  148 us (25%)
  blocking collectives  65.3 us (11%)
  other arithmetic  56.1 us (9%)
  matrix products  19.9 us (3%)
  between operations  15.7 us (3%)
    reduce_scatter x1, waiting for transfers between devices, local(): lax.psum_scatter(lead_dot(self_part, w_one[0]) + lead_dot(near_part, w_on...  89.7 us
    psum x1, waiting for transfers between devices, local(): lax.psum((grad_two, bias_grad_two, grad_three, bias_grad_three, bias_grad...  85.9 us
    gather x5, local copies, waits for them, and re-layouts, local(): jnp.take(feat_table, near_one[offset], axis=1).astype(jnp.float32)  81.7 us
    psum x1, waiting for transfers between devices, local(): grad_one = lax.psum(grad_one_part, 'dp')  80.4 us
    psum x1, blocking collectives, local(): lax.psum((grad_two, bias_grad_two, grad_three, bias_grad_three, bias_grad...  65.3 us
    gather x25, local copies, waits for them, and re-layouts, gather_mean(): running_sum = running_sum + row_table[near_ids[offset]].astype(jnp.float32)  35.1 us
    all_gather x1, waiting for transfers between devices, local(): block_rows = lax.all_gather(pre_grad_one, 'cuts', axis=0, tiled=True)  34.9 us
    scatter-add x25, other arithmetic, spread_back(): result = result.at[near_ids[offset]].add(near_grad)  30.5 us
  transfers between devices with their start and end apart: 4, of which 4 were waited for; matrix products, arithmetic and copies ran while one was open for 3% of the time, Pallas kernels for 0%

commit v1 on v0

v1 whole, which is shorter than its diff:
```python
import functools

import jax
import jax.numpy as jnp
from jax import lax
from jax.experimental import pallas as pl
from jax.experimental.pallas import tpu as pltpu
from jax.sharding import Mesh, PartitionSpec as P

BF16 = jnp.bfloat16
F32 = jnp.float32
VMEM = pltpu.VMEM
SMEM = pltpu.SMEM

LANES = 128
GATHER_UNROLL = 16
ONE_ROWS = 64
TWO_ROWS = 32
TOP_ROWS = 16
LATE_ROWS = TWO_ROWS + TOP_ROWS
CHUNK_ROWS = ONE_ROWS + LATE_ROWS
PEERS = 64

DP = ("y_hi", "x")
CUTS = ("z", "y_lo", "core")
SAME_CORE = ("y_hi", "x", "z", "y_lo")


def dot(first, second, contract=((1,), (0,))):
    return lax.dot_general(first, second, (contract, ((), ())), preferred_element_type=F32)


def lead_dot(first, second):
    return dot(first, second, ((0,), (0,)))


def back_dot(first, second):
    return dot(first, second, ((1,), (1,)))


def exact_dot(picks, values):
    high = values.astype(BF16)
    low = (values - high.astype(F32)).astype(BF16)
    return dot(picks, high) + dot(picks, low)


def gelu_parts(values):
    inner = 0.7978845608028654 * (values + 0.044715 * values * values * values)
    cdf = 0.5 * (1.0 + jnp.tanh(inner))
    return cdf


def gelu_slope(values):
    square = values * values
    tanh = jnp.tanh(0.7978845608028654 * (values + 0.044715 * values * square))
    inner_slope = 0.7978845608028654 * (1.0 + 3.0 * 0.044715 * square)
    return 0.5 * (1.0 + tanh) + 0.5 * values * (1.0 - tanh * tanh) * inner_slope


def vmem(count):
    return [pl.BlockSpec(memory_space=VMEM)] * count


def gather_kernel(feat_ref, self_ref, near_ref, out_ref, table, rows):
    nodes = feat_ref.shape[1]
    targets = out_ref.shape[0]
    fan = near_ref.shape[0] // targets

    @pl.loop(0, nodes // LANES, unroll=4)
    def _(block):
        spot = pl.ds(pl.multiple_of(block * LANES, LANES), LANES)
        part = feat_ref[:, spot].astype(F32)
        table[spot, :] = jnp.concatenate([part, part], axis=0).T

    half = lax.broadcasted_iota(jnp.int32, (1, LANES), 1) < LANES // 2

    @pl.loop(0, targets // GATHER_UNROLL)
    def _(group):
        base = group * GATHER_UNROLL
        for step in range(GATHER_UNROLL):
            spot = base + step
            total = table[pl.ds(near_ref[spot], 1), :]
            for offset in range(1, fan):
                total = total + table[pl.ds(near_ref[offset * targets + spot], 1), :]
            own = table[pl.ds(self_ref[spot], 1), :]
            rows[pl.ds(spot, 1), :] = jnp.where(half, own, total)

    step_rows = 64
    wide_half = lax.broadcasted_iota(jnp.int32, (step_rows, LANES), 1) < LANES // 2

    @pl.loop(0, targets // step_rows)
    def _(group):
        spot = pl.ds(pl.multiple_of(group * step_rows, step_rows), step_rows)
        value = rows[spot, :]
        out_ref[spot, :] = jnp.where(wide_half, value, value / fan).astype(BF16)


def gather_rows(feat_table, self_one, near_one):
    nodes = feat_table.shape[1]
    targets = self_one.shape[0]
    return pl.pallas_call(
        gather_kernel,
        out_shape=jax.ShapeDtypeStruct((targets, LANES), BF16),
        in_specs=[
            pl.BlockSpec(memory_space=VMEM),
            pl.BlockSpec(memory_space=SMEM),
            pl.BlockSpec(memory_space=SMEM),
        ],
        out_specs=pl.BlockSpec(memory_space=VMEM),
        scratch_shapes=[VMEM((nodes, LANES), F32), VMEM((targets, LANES), F32)],
        compiler_params=pltpu.CompilerParams(vmem_limit_bytes=48 << 20),
        cost_estimate=pl.CostEstimate(flops=1 << 27, bytes_accessed=40 << 20, transcendentals=0),
        name="gather_rows",
    )(feat_table, self_one, near_one.reshape(-1))


def owner_kernel(
    place_ref,
    count_ref,
    rows_ref,
    w_one_ref,
    bias_one_ref,
    self_two_ref,
    near_two_ref,
    self_three_ref,
    near_three_ref,
    targets_ref,
    w_two_ref,
    bias_two_ref,
    w_three_ref,
    bias_three_ref,
    keep_ref,
    send_ref,
    pre_one,
    mids,
    tops,
):
    core = place_ref[0]
    owner = place_ref[1]
    cuts, cap, _ = rows_ref.shape
    hidden = w_two_ref.shape[2]
    labels = w_three_ref.shape[2]
    mid_rows = self_two_ref.shape[1]
    seeds = self_three_ref.shape[1]
    fan_two = near_two_ref.shape[0]
    fan_three = near_three_ref.shape[0]

    total = None
    for pair in range(cuts // 2):
        wide = jnp.concatenate([rows_ref[2 * pair], rows_ref[2 * pair + 1]], axis=1)
        part = dot(wide, w_one_ref[pl.ds(pair * 2 * LANES, 2 * LANES), :])
        total = part if total is None else total + part
    pre_one[...] = total + bias_one_ref[...]
    values = pre_one[...]
    hidden_one = (values * gelu_parts(values)).astype(BF16)

    spots = lax.broadcasted_iota(jnp.int32, (cap, mid_rows), 0)
    self_two_t = (spots == self_two_ref[...]).astype(F32)
    near_two_t = jnp.zeros((cap, mid_rows), F32)
    for offset in range(fan_two):
        near_two_t += (spots == near_two_ref[pl.ds(offset, 1), :]).astype(F32)
    self_mid = dot(self_two_t.T.astype(BF16), hidden_one).astype(BF16)
    near_mid = (dot(near_two_t.T.astype(BF16), hidden_one) / fan_two).astype(BF16)
    mids[0] = self_mid
    mids[1] = near_mid
    pre_two = dot(self_mid, w_two_ref[0]) + dot(near_mid, w_two_ref[1]) + bias_two_ref[...]
    hidden_two = (pre_two * gelu_parts(pre_two)).astype(BF16)

    spots = lax.broadcasted_iota(jnp.int32, (mid_rows, seeds), 0)
    self_three_t = (spots == self_three_ref[...]).astype(F32)
    near_three_t = jnp.zeros((mid_rows, seeds), F32)
    for offset in range(fan_three):
        near_three_t += (spots == near_three_ref[pl.ds(offset, 1), :]).astype(F32)
    self_top = dot(self_three_t.T.astype(BF16), hidden_two).astype(BF16)
    near_top = (dot(near_three_t.T.astype(BF16), hidden_two) / fan_three).astype(BF16)
    tops[0] = self_top
    tops[1] = near_top
    logits = dot(self_top, w_three_ref[0]) + dot(near_top, w_three_ref[1]) + bias_three_ref[...]

    live_total = lax.fori_loop(0, count_ref.shape[0], lambda i, t: t + count_ref[i], jnp.int32(0))
    scale = 1.0 / jnp.sqrt(jnp.full((1, labels), live_total, jnp.int32).astype(F32))
    live = lax.broadcasted_iota(jnp.int32, (seeds, labels), 0) < count_ref[owner]
    slope = jax.nn.sigmoid(logits) - targets_ref[...].astype(F32)
    logit_grad = jnp.where(live, slope * scale, 0.0).astype(BF16)

    self_grad = back_dot(logit_grad, w_three_ref[0])
    near_grad = back_dot(logit_grad, w_three_ref[1]) / fan_three
    upstream = exact_dot(self_three_t.astype(BF16), self_grad)
    upstream += exact_dot(near_three_t.astype(BF16), near_grad)
    pre_grad_two = (gelu_slope(pre_two) * upstream).astype(BF16)

    self_grad = back_dot(pre_grad_two, w_two_ref[0])
    near_grad = back_dot(pre_grad_two, w_two_ref[1]) / fan_two
    upstream = exact_dot(self_two_t.astype(BF16), self_grad)
    upstream += exact_dot(near_two_t.astype(BF16), near_grad)
    pre_grad_one = (gelu_slope(pre_one[...]) * upstream).astype(BF16)

    wide_logit = jnp.concatenate([logit_grad, jnp.zeros((seeds, LANES - labels), BF16)], axis=1)
    bias_one = jnp.sum(pre_grad_one.astype(F32), axis=0, keepdims=True)
    bias_two = jnp.sum(pre_grad_two.astype(F32), axis=0, keepdims=True)
    bias_three = jnp.sum(wide_logit.astype(F32), axis=0, keepdims=True)
    tiles = hidden // LANES
    dp_count = PEERS // (cuts // 2)
    share = LANES // dp_count

    for out_ref, side in ((send_ref, 1 - core), (keep_ref, core)):
        for pair in range(cuts // 2):
            block = lead_dot(rows_ref[2 * pair + side], pre_grad_one).astype(BF16)
            for group in range(dp_count):
                for tile in range(tiles):
                    out_ref[group * (cuts // 2) + pair, pl.ds(tile * share, share), :] = block[
                        group * share : (group + 1) * share, tile * LANES : (tile + 1) * LANES
                    ]
        two = lead_dot(mids[side], pre_grad_two)
        top = lead_dot(tops[side], wide_logit)
        count = hidden // PEERS
        first = (side == 0).astype(F32)
        for peer in range(PEERS):
            late = [
                two[peer * count : (peer + 1) * count, tile * LANES : (tile + 1) * LANES]
                for tile in range(tiles)
            ]
            late.append(top[peer * count : (peer + 1) * count, :])
            if peer < tiles:
                spread = slice(peer * LANES, (peer + 1) * LANES)
                lines = [bias_one[:, spread], bias_two[:, spread]]
                lines.append(bias_three if peer == 0 else jnp.zeros((1, LANES), F32))
                lines.append(jnp.zeros((count - 3, LANES), F32))
                late.append(jnp.concatenate(lines, axis=0) * first)
            else:
                late.append(jnp.zeros((count, LANES), F32))
            out_ref[peer, pl.ds(ONE_ROWS, LATE_ROWS), :] = jnp.concatenate(late, axis=0).astype(BF16)


def owner_pass(place, seed_count, rows, w_one, bias_one, self_two, near_two, self_three, near_three,
               targets, w_two, bias_two, w_three, bias_three):
    cap = rows.shape[1]
    hidden = w_two.shape[2]
    chunk = jax.ShapeDtypeStruct((PEERS, CHUNK_ROWS, LANES), BF16)
    return pl.pallas_call(
        owner_kernel,
        out_shape=(chunk, chunk),
        in_specs=[pl.BlockSpec(memory_space=SMEM)] * 2 + vmem(12),
        out_specs=tuple(vmem(2)),
        scratch_shapes=[
            VMEM((cap, hidden), F32),
            VMEM((2, near_two.shape[1], hidden), BF16),
            VMEM((2, near_three.shape[1], hidden), BF16),
        ],
        compiler_params=pltpu.CompilerParams(vmem_limit_bytes=48 << 20),
        cost_estimate=pl.CostEstimate(flops=1 << 31, bytes_accessed=10 << 20, transcendentals=1 << 19),
        name="owner_pass",
    )(
        place, seed_count, rows, w_one, bias_one.reshape(1, -1), self_two.reshape(1, -1), near_two,
        self_three.reshape(1, -1), near_three, targets, w_two, bias_two.reshape(1, -1), w_three,
        bias_three.reshape(1, -1),
    )


def sum_kernel(parts_ref, one_ref, late_ref):
    total = jnp.sum(parts_ref[...].astype(F32), axis=0)
    one_ref[...] = total[:ONE_ROWS].astype(BF16)
    late = total[ONE_ROWS:].astype(BF16)
    for peer in range(PEERS):
        late_ref[peer] = late


def sum_parts(parts):
    return pl.pallas_call(
        sum_kernel,
        out_shape=(
            jax.ShapeDtypeStruct((ONE_ROWS, LANES), BF16),
            jax.ShapeDtypeStruct((PEERS, LATE_ROWS, LANES), BF16),
        ),
        in_specs=vmem(1),
        out_specs=tuple(vmem(2)),
        compiler_params=pltpu.CompilerParams(vmem_limit_bytes=48 << 20),
        name="sum_parts",
    )(parts)


def unpack_kernel(place_ref, one_ref, own_ref, other_ref, grad_one, bias_one, grad_two, bias_two, grad_three, bias_three):
    core = place_ref[0]
    hidden = grad_one.shape[2]
    tiles = hidden // LANES
    groups = one_ref.shape[0]
    share = ONE_ROWS // tiles
    for group in range(groups):
        layer, line = divmod(group * share, grad_one.shape[1])
        for tile in range(tiles):
            grad_one[layer, pl.ds(line, share), pl.ds(tile * LANES, LANES)] = one_ref[
                group, pl.ds(tile * share, share), :
            ].astype(F32)
    count = hidden // PEERS
    labels = grad_three.shape[2]
    for ref, side in ((own_ref, core), (other_ref, 1 - core)):
        for peer in range(PEERS):
            late = ref[peer].astype(F32)
            for tile in range(tiles):
                grad_two[side, pl.ds(peer * count, count), pl.ds(tile * LANES, LANES)] = late[
                    tile * count : (tile + 1) * count
                ]
            grad_three[side, pl.ds(peer * count, count), :] = late[TWO_ROWS : TWO_ROWS + count, :labels]
    line = TWO_ROWS + count
    for peer in range(tiles):
        late = own_ref[peer].astype(F32)[line : line + count] + other_ref[peer].astype(F32)[line : line + count]
        bias_one[:, pl.ds(peer * LANES, LANES)] = late[0:1]
        bias_two[:, pl.ds(peer * LANES, LANES)] = late[1:2]
        if peer == 0:
            bias_three[...] = late[2:3, :labels]


def unpack(place, one, own, other, cut_rows, hidden, labels):
    return pl.pallas_call(
        unpack_kernel,
        out_shape=(
            jax.ShapeDtypeStruct((2, cut_rows, hidden), F32),
            jax.ShapeDtypeStruct((1, hidden), F32),
            jax.ShapeDtypeStruct((2, hidden, hidden), F32),
            jax.ShapeDtypeStruct((1, hidden), F32),
            jax.ShapeDtypeStruct((2, hidden, labels), F32),
            jax.ShapeDtypeStruct((1, labels), F32),
        ),
        in_specs=[pl.BlockSpec(memory_space=SMEM)] + vmem(3),
        out_specs=tuple(vmem(6)),
        compiler_params=pltpu.CompilerParams(vmem_limit_bytes=48 << 20),
        name="unpack",
    )(place, one, own, other)


def exchange(values, axes):
    return lax.all_to_all(values, axes, 0, 0, tiled=True)


def swap_core(values):
    return lax.ppermute(values, "core", [(0, 1), (1, 0)])


def local(
    feat_table,
    self_one,
    near_one,
    self_two,
    near_two,
    self_three,
    near_three,
    targets,
    seed_count,
    w_one,
    bias_one,
    w_two,
    bias_two,
    w_three,
    bias_three,
):
    cut_rows, hidden = w_one.shape[1:]
    labels = w_three.shape[2]
    cuts = lax.axis_size(CUTS)
    owner = lax.axis_index(DP) * cuts + lax.axis_index(CUTS)
    place = jnp.stack([lax.axis_index("core"), owner]).astype(jnp.int32)
    whole_w_one = lax.all_gather(w_one.reshape(-1, hidden), CUTS, axis=0, tiled=True)
    rows = gather_rows(feat_table, self_one, near_one)
    rows = exchange(rows, CUTS).reshape(cuts, -1, LANES)
    keep, send = owner_pass(
        place, seed_count, rows, whole_w_one, bias_one, self_two, near_two, self_three, near_three,
        targets, w_two, bias_two, w_three, bias_three,
    )
    parts = (keep.astype(F32) + swap_core(send).astype(F32)).astype(BF16)
    parts = exchange(parts, SAME_CORE)
    one, late = sum_parts(parts)
    groups = lax.axis_size(DP)
    one = exchange(jnp.broadcast_to(one[None], (groups,) + one.shape), DP)
    own = exchange(late, SAME_CORE)
    other = swap_core(own)
    grad_one, bias_one, grad_two, bias_two, grad_three, bias_three = unpack(
        place, one, own, other, cut_rows, hidden, labels
    )
    return (
        grad_one,
        bias_one.reshape(-1),
        grad_two,
        bias_two.reshape(-1),
        grad_three,
        bias_three.reshape(-1),
    )


def solution(mesh):
    fine = Mesh(mesh.devices.reshape(2, 4, 4, 2, 2), ("y_hi", "x", "z", "y_lo", "core"))
    both = DP + CUTS
    return jax.shard_map(
        local,
        mesh=fine,
        in_specs=(
            P(CUTS, DP),
            P(DP),
            P(None, DP),
            P(both),
            P(None, both),
            P(both),
            P(None, both),
            P(both, None),
            P(),
            P(None, CUTS, None),
            P(),
            P(),
            P(),
            P(),
            P(),
        ),
        out_specs=(P(None, CUTS, None), P(), P(), P(), P(), P()),
        check_vma=False,
    )
```

time: 602 us -> 149 us (0.25)
  waiting for transfers between devices: 291 us -> 19.7 us
  local copies, waits for them, and re-layouts: 148 us -> 4.47 us
  other arithmetic: 56.1 us -> 0.55 us
  Pallas kernels: 0 us -> 35.9 us
  matrix products: 19.9 us -> 0 us
  starting transfers between devices: 0.34 us -> 12.2 us
    psum x2 -> x0, waiting for transfers between devices: 166 us -> none  [the longest x1 85.9 us: local(): lax.psum((grad_two, bias_grad_two, grad_three, bias_grad_three, bias_grad...]
    gather x33 -> x0, local copies, waits for them, and re-layouts: 133 us -> none  [the longest x5 81.7 us: local(): jnp.take(feat_table, near_one[offset], axis=1).astype(jnp.float32)]
    reduce_scatter x1 -> x0, waiting for transfers between devices: 89.7 us -> none  [local(): lax.psum_scatter(lead_dot(self_part, w_one[0]) + lead_dot(near_part, w_on...]
    psum x1 -> x0, blocking collectives: 65.3 us -> none  [local(): lax.psum((grad_two, bias_grad_two, grad_three, bias_grad_three, bias_grad...]
    all_to_all x0 -> x3, blocking collectives: none -> 61.5 us  [exchange(): return lax.all_to_all(values, axes, 0, 0, tiled=True)]
    pallas_call x0 -> x4, Pallas kernels: none -> 35.9 us  [the longest x1 27.1 us: gather_rows(): pl.pallas_call(gather_kernel, out_shape=jax.ShapeDtypeStruct((targets, LA...]
    all_gather x1, waiting for transfers between devices: 34.9 us -> 0.01 us  [local(): lax.all_gather(w_one.reshape(-1, hidden), CUTS, axis=0, tiled=True)]
    scatter-add x27 -> x0, other arithmetic: 33.3 us -> none  [the longest x25 30.5 us: spread_back(): result = result.at[near_ids[offset]].add(near_grad)]
  transfers between devices with their start and end apart: 4 -> 4, of which waited for: 4 -> 2; matrix products, arithmetic and copies ran while one was open for 3% -> 1% of each run, Pallas kernels for 0% -> 18%
where the time goes in v1:
time: 149 us; the launch traced here: 148 us
  blocking collectives  61.5 us (41%)
  Pallas kernels  35.9 us (24%)
  waiting for transfers between devices  19.7 us (13%)
  between operations  14.2 us (10%)
  starting transfers between devices  12.2 us (8%)
  local copies, waits for them, and re-layouts  4.47 us (3%)
    all_to_all x3, blocking collectives, exchange(): return lax.all_to_all(values, axes, 0, 0, tiled=True)  61.5 us
    pallas_call x1, Pallas kernels, gather_rows(): pl.pallas_call(gather_kernel, out_shape=jax.ShapeDtypeStruct((targets, LA...  27.1 us
    all_to_all x1, waiting for transfers between devices, exchange(): return lax.all_to_all(values, axes, 0, 0, tiled=True)  15.6 us
    all_to_all x1, starting transfers between devices, exchange(): return lax.all_to_all(values, axes, 0, 0, tiled=True)  7.99 us
    pallas_call x1, Pallas kernels, owner_pass(): pl.pallas_call(owner_kernel, out_shape=(chunk, chunk), in_specs=[pl.Block...  6.44 us
    ppermute x2, starting transfers between devices, swap_core(): return lax.ppermute(values, 'core', [(0, 1), (1, 0)])  4.23 us
    unnamed x28, local copies, waits for them, and re-layouts  3.51 us
    ppermute x2, waiting for transfers between devices, swap_core(): return lax.ppermute(values, 'core', [(0, 1), (1, 0)])  3.41 us
  transfers between devices with their start and end apart: 4, of which 2 were waited for; matrix products, arithmetic and copies ran while one was open for 1% of the time, Pallas kernels for 18%

profile of v1, /device:TPU:1, one launch (start us, length us, event | category | flops | bytes accessed | tf_op | source)
XLA Modules:
  0.0 148.5 jit_solution(14485188448836421837)
XLA Ops:
  7.2 0.0 all-gather.2.cloned.1.call-start
  7.2 0.7 all-gather.2.cloned.1.call-update
  7.9 0.9 reshape.47.near_ref
  8.9 0.0 copy-start
  8.9 1.6 %copy-done = bf16[64,16384]{1,0:T(8,128)(2,1)S(1)} copy-done((bf16[64,16384]{1,0:T(8,128)(2,1)S(1)}, bf16[64,16384]{1,0:T(8,128)(2,1)}, u32[]{:S(2)}) %copy-start) | copy-done | bytes 2097176
  10.4 0.0 copy-start.1
  10.4 0.7 copy-done.1
  11.2 27.1 %gather_rows.1 = bf16[4096,128]{1,0:T(8,128)(2,1)} custom-call(bf16[64,16384]{1,0:T(8,128)(2,1)S(1)} %copy-done, s32[4096]{0:T(1024)S(1)} %copy-done.1, s32[20480]{0:T(1024)S(1)} %reshape.47.near_ref), custom_call_target="tpu_custom_call" | custom-call | flops 134217728 | bytes 41943040 | tf_op jit(solution)/shard_map/gather_rows/pallas_call | solution.py:101
  38.3 0.0 copy-start.12
  38.3 0.0 copy-start.2
  38.3 0.0 copy-start.3
  38.3 0.0 copy-start.4
  38.3 0.0 copy-start.5
  38.3 0.0 copy-start.6
  38.3 0.0 copy-start.7
  38.3 0.0 copy-start.8
  38.3 0.0 copy-start.9
  38.3 0.0 copy-start.10
  38.3 0.0 copy-start.11
  38.4 8.0 %all-to-all-start = ((bf16[16,256,128]{2,1,0:T(8,128)(2,1)}), bf16[16,256,128]{2,1,0:T(8,128)(2,1)S(1)}, u32[]{:S(2)}, u32[]{:S(2)}) async-start(bf16[16,256,128]{2,1,0:T(8,128)(2,1)} %bitcast.2), calls=%async_computation | async-start | bytes 2097152 | tf_op jit(solution)/shard_map/all_to_all | solution.py:332
  46.3 0.0 copy-done.12
  46.3 0.2 copy.21.w_three_ref
  46.5 0.1 pad_add_fusion.place_ref
  46.6 15.6 %all-to-all-done.rows_ref = bf16[16,256,128]{2,1,0:T(8,128)(2,1)S(1)} async-done(((bf16[16,256,128]{2,1,0:T(8,128)(2,1)}), bf16[16,256,128]{2,1,0:T(8,128)(2,1)S(1)}, u32[]{:S(2)}, u32[]{:S(2)}) %all-to-all-start) | async-done | bytes 1048608 | tf_op jit(solution)/shard_map/all_to_all | solution.py:332
  62.2 0.0 all-gather.2.cloned.1.call-done.w_one_ref
  62.2 0.0 copy-done.2
  62.2 0.0 copy-done.3
  62.2 0.0 copy-done.4
  62.2 0.0 copy-done.5
  62.2 0.0 copy-done.6
  62.2 0.0 copy-done.7
  62.2 0.0 copy-done.8
  62.2 0.0 copy-done.9
  62.2 0.0 copy-done.10
  62.2 0.0 copy-done.11
  62.3 6.4 %owner_pass.1 = (bf16[64,112,128]{2,1,0:T(8,128)(2,1)S(1)}, bf16[64,112,128]{2,1,0:T(8,128)(2,1)S(1)}) custom-call(s32[2]{0:T(128)S(1)} %pad_add_fusion.place_ref, s32[128]{0:T(128)S(1)} %copy-done.8, bf16[16,256,128]{2,1,0:T(8,128)(2,1)S(1)} %all-to-all-done.rows_ref, bf16[2048,512]{1,0:T(8,128)(2,1)} %all-gather.2.cloned.1.call-done.w_one_ref, ...), custom_call_target="tpu_custom_call" | custom-call | flops 2147483648 | bytes 10485760 | tf_op jit(solution)/shard_map/owner_pass/pallas_call | solution.py:240
  68.7 0.9 collective-permute-start
  69.7 3.4 %collective-permute-done = bf16[64,112,128]{2,1,0:T(8,128)(2,1)S(1)} collective-permute-done((bf16[64,112,128]{2,1,0:T(8,128)(2,1)S(1)}, bf16[64,112,128]{2,1,0:T(8,128)(2,1)S(1)}, u32[]{:S(2)}, u32[]{:S(2)}) %collective-permute-start) | collective-permute-done | bytes 1835040 | tf_op jit(solution)/shard_map/ppermute | solution.py:336
  73.1 0.5 add_convert_fusion
  73.5 32.2 %all_to_all.24.parts_ref = bf16[64,112,128]{2,1,0:T(8,128)(2,1)S(1)} all-to-all(bf16[64,112,128]{2,1,0:T(8,128)(2,1)S(1)} %add_convert_fusion), channel_id=1, replica_groups=mesh['y_hi'=2,'x'=4,'z'=4,'y_lo'=2,'core'=2] {'y_hi','x','z','y_lo'}, dimensions={0} | all-to-all | bytes 3670016 | tf_op jit(solution)/shard_map/all_to_all | solution.py:332
  105.8 0.3 sum_parts.1
  106.1 19.2 %all_to_all.25.own_ref = bf16[64,48,128]{2,1,0:T(8,128)(2,1)S(1)} all-to-all(bf16[64,48,128]{2,1,0:T(8,128)(2,1)S(1)} %get-tuple-element.19), channel_id=1, replica_groups=mesh['y_hi'=2,'x'=4,'z'=4,'y_lo'=2,'core'=2] {'y_hi','x','z','y_lo'}, dimensions={0} | all-to-all | bytes 1572864 | tf_op jit(solution)/shard_map/all_to_all | solution.py:332
  125.3 3.3 %collective-permute-start.1 = (bf16[64,48,128]{2,1,0:T(8,128)(2,1)S(1)}, bf16[64,48,128]{2,1,0:T(8,128)(2,1)S(1)}, u32[]{:S(2)}, u32[]{:S(2)}) collective-permute-start(bf16[64,48,128]{2,1,0:T(8,128)(2,1)S(1)} %all_to_all.25.own_ref), channel_id=1, source_target_pairs={{0,1},{1,0},{2,3},{3,2},{4,5},{5,4},{6,7},{7,6},{8,9},{9,8},{10,11... | collective-permute-start | bytes 2359304 | tf_op jit(solution)/shard_map/ppermute | solution.py:336
  128.6 10.0 %all_to_all.26.one_ref = bf16[8,64,128]{2,1,0:T(8,128)(2,1)S(1)} all-to-all(bf16[8,64,128]{2,1,0:T(8,128)(2,1)S(1)} %broadcast_in_dim.2), channel_id=1, replica_groups=mesh['y_hi'=2,'x'=4,'z'=4,'y_lo'=2,'core'=2] {'y_hi','x'}, dimensions={0} | all-to-all | bytes 262144 | tf_op jit(solution)/shard_map/all_to_all | solution.py:332
  138.6 0.0 collective-permute-done.1.other_ref
  138.6 2.1 %unpack.1 = (f32[2,64,512]{2,1,0:T(8,128)}, f32[1,512]{1,0:T(1,128)}, f32[2,512,512]{2,1,0:T(8,128)}, f32[1,512]{1,0:T(1,128)}, f32[2,512,112]{2,1,0:T(8,128)S(1)}, /*index=5*/f32[1,112]{1,0:T(1,128)}) custom-call(s32[2]{0:T(128)S(1)} %pad_add_fusion.place_ref, bf16[8,64,128]{2,1,0:T(8,128)(2,1)S(1)} %all_to_all.26.one_ref, ...), custom_call_target="tpu_custom_call" | custom-call | tf_op jit(solution)/shard_map/unpack/pallas_call | solution.py:314
  140.7 1.0 copy.22
  (1 shorter events, 0.0 us)
Async XLA Ops:
  7.2 55.0 %all-gather.2.cloned.1.call-start = ((), (), s32[]{:S(2)}) async-start(), calls=%async_computation.4 | async-start | bytes 2228224 | tf_op jit(solution)/shard_map/all_gather | solution.py:361
  8.9 1.6 %copy-start = (bf16[64,16384]{1,0:T(8,128)(2,1)S(1)}, bf16[64,16384]{1,0:T(8,128)(2,1)}, u32[]{:S(2)}) copy-start(bf16[64,16384]{1,0:T(8,128)(2,1)} %feat_ref.1) | copy-start | bytes 6291460
  10.4 0.7 copy-start.1
  38.3 8.1 %copy-start.12 = (bf16[2,512,112]{1,2,0:T(8,128)(2,1)S(1)}, bf16[2,512,112]{1,2,0:T(8,128)(2,1)}, u32[]{:S(2)}) copy-start(bf16[2,512,112]{1,2,0:T(8,128)(2,1)} %param.28) | copy-start | bytes 688132
  38.3 23.9 %copy-start.2 = (bf16[2,512,512]{2,1,0:T(8,128)(2,1)S(1)}, bf16[2,512,512]{2,1,0:T(8,128)(2,1)}, u32[]{:S(2)}) copy-start(bf16[2,512,512]{2,1,0:T(8,128)(2,1)} %w_two_ref.1) | copy-start | bytes 3145732
  38.3 23.9 %copy-start.3 = (s32[32,112]{1,0:T(8,128)S(1)}, s32[32,112]{1,0:T(8,128)}, u32[]{:S(2)}) copy-start(s32[32,112]{1,0:T(8,128)} %targets_ref.1) | copy-start | bytes 43012
  38.3 23.9 %copy-start.4 = (s32[10,128]{1,0:T(8,128)S(1)}, s32[10,128]{1,0:T(8,128)}, u32[]{:S(2)}) copy-start(s32[10,128]{1,0:T(8,128)} %near_two_ref.1) | copy-start | bytes 15364
  38.3 23.9 %copy-start.5 = (s32[15,32]{1,0:T(8,128)S(1)}, s32[15,32]{1,0:T(8,128)}, u32[]{:S(2)}) copy-start(s32[15,32]{1,0:T(8,128)} %near_three_ref.1) | copy-start | bytes 5764
  38.3 23.9 %copy-start.6 = (f32[512]{0:T(512)S(1)}, f32[512]{0:T(512)}, u32[]{:S(2)}) copy-start(f32[512]{0:T(512)} %param.25) | copy-start | bytes 6148
  38.3 23.9 %copy-start.7 = (f32[512]{0:T(512)S(1)}, f32[512]{0:T(512)}, u32[]{:S(2)}) copy-start(f32[512]{0:T(512)} %param.27) | copy-start | bytes 6148
  38.3 23.9 %copy-start.8 = (s32[128]{0:T(128)S(1)}, s32[128]{0:T(128)}, u32[]{:S(2)}) copy-start(s32[128]{0:T(128)} %count_ref.1) | copy-start | bytes 1540
  38.3 23.9 %copy-start.9 = (s32[128]{0:T(128)S(1)}, s32[128]{0:T(128)}, u32[]{:S(2)}) copy-start(s32[128]{0:T(128)} %param.18) | copy-start | bytes 1540
  38.3 23.9 %copy-start.10 = (s32[32]{0:T(128)S(1)}, s32[32]{0:T(128)}, u32[]{:S(2)}) copy-start(s32[32]{0:T(128)} %param.20) | copy-start | bytes 388
  38.3 23.9 %copy-start.11 = (f32[112]{0:T(128)S(1)}, f32[112]{0:T(128)}, u32[]{:S(2)}) copy-start(f32[112]{0:T(128)} %param.29) | copy-start | bytes 1348
  38.4 23.8 %all-to-all-start = ((bf16[16,256,128]{2,1,0:T(8,128)(2,1)}), bf16[16,256,128]{2,1,0:T(8,128)(2,1)S(1)}, u32[]{:S(2)}, u32[]{:S(2)}) async-start(bf16[16,256,128]{2,1,0:T(8,128)(2,1)} %bitcast.2), calls=%async_computation | async-start | bytes 2097152 | tf_op jit(solution)/shard_map/all_to_all | solution.py:332
  68.7 4.4 %collective-permute-start = (bf16[64,112,128]{2,1,0:T(8,128)(2,1)S(1)}, bf16[64,112,128]{2,1,0:T(8,128)(2,1)S(1)}, u32[]{:S(2)}, u32[]{:S(2)}) collective-permute-start(bf16[64,112,128]{2,1,0:T(8,128)(2,1)S(1)} %get-tuple-element.17), channel_id=1, source_target_pairs={{0,1},{1,0},{2,3},{3,2},{4,5},{5,4},{6,7},{7,6},{8,9},{9,8},{10,11... | collective-permute-start | bytes 5505032 | tf_op jit(solution)/shard_map/ppermute | solution.py:336
  125.3 13.3 %collective-permute-start.1 = (bf16[64,48,128]{2,1,0:T(8,128)(2,1)S(1)}, bf16[64,48,128]{2,1,0:T(8,128)(2,1)S(1)}, u32[]{:S(2)}, u32[]{:S(2)}) collective-permute-start(bf16[64,48,128]{2,1,0:T(8,128)(2,1)S(1)} %all_to_all.25.own_ref), channel_id=1, source_target_pairs={{0,1},{1,0},{2,3},{3,2},{4,5},{5,4},{6,7},{7,6},{8,9},{9,8},{10,11... | collective-permute-start | bytes 2359304 | tf_op jit(solution)/shard_map/ppermute | solution.py:336
Sparse Core Ops, SparseCore 0:
  9.7 37.8 all-gather.1

commit v2 on v1

v2 whole, which is shorter than its diff:
```python
import jax
import jax.numpy as jnp
from jax import lax
from jax.experimental import pallas as pl
from jax.experimental.pallas import tpu as pltpu
from jax.sharding import Mesh, PartitionSpec as P

BF16 = jnp.bfloat16
F32 = jnp.float32
VMEM = pltpu.VMEM
SMEM = pltpu.SMEM

LANES = 128
GATHER_UNROLL = 16
ONE_ROWS = 64
TWO_ROWS = 32
TOP_ROWS = 8
LATE_ROWS = TWO_ROWS + TOP_ROWS
CHUNK_ROWS = ONE_ROWS + LATE_ROWS
PEERS = 64

DP = ("y_hi", "x")
CUTS = ("z", "y_lo", "core")
CHIPS = ("z", "y_lo")
SAME_CORE = DP + CHIPS


def dot(first, second, contract=((1,), (0,))):
    return lax.dot_general(first, second, (contract, ((), ())), preferred_element_type=F32)


def lead_dot(first, second):
    return dot(first, second, ((0,), (0,)))


def back_dot(first, second):
    return dot(first, second, ((1,), (1,)))


def exact_dot(picks, values):
    high = values.astype(BF16)
    low = (values - high.astype(F32)).astype(BF16)
    return dot(picks, high) + dot(picks, low)


def gelu_cdf(values):
    return 0.5 * (1.0 + jnp.tanh(0.7978845608028654 * (values + 0.044715 * values * values * values)))


def gelu_slope(values):
    square = values * values
    tanh = jnp.tanh(0.7978845608028654 * (values + 0.044715 * values * square))
    inner_slope = 0.7978845608028654 * (1.0 + 3.0 * 0.044715 * square)
    return 0.5 * (1.0 + tanh) + 0.5 * values * (1.0 - tanh * tanh) * inner_slope


def vmem(count):
    return [pl.BlockSpec(memory_space=VMEM)] * count


def gather_kernel(place_ref, own_ref, other_ref, w_one_ref, self_ref, near_ref, out_ref, table, rows):
    core = place_ref[0]
    nodes = own_ref.shape[1]
    targets = self_ref.shape[0]
    fan = near_ref.shape[0] // targets
    chips = out_ref.shape[0]
    cap = targets // (2 * chips)

    @pl.loop(0, nodes // LANES, unroll=4)
    def _(block):
        spot = pl.ds(pl.multiple_of(block * LANES, LANES), LANES)
        part = jnp.concatenate([own_ref[:, spot], other_ref[:, spot]], axis=0).astype(F32)
        table[spot, :] = part.T

    tiles = w_one_ref.shape[1] // LANES
    for tile in range(tiles):
        block = w_one_ref[:, pl.ds(tile * LANES, LANES)]
        for chip in range(chips):
            out_ref[chip, pl.ds(2 * cap + tile * LANES, LANES), :] = block

    @pl.loop(0, chips)
    def _(chip):
        first = (2 * chip + core) * cap

        @pl.loop(0, cap // GATHER_UNROLL)
        def _(group):
            for step in range(GATHER_UNROLL):
                line = group * GATHER_UNROLL + step
                spot = first + line
                total = table[pl.ds(near_ref[spot], 1), :]
                for offset in range(1, fan):
                    total = total + table[pl.ds(near_ref[offset * targets + spot], 1), :]
                rows[pl.ds(line, 1), :] = table[pl.ds(self_ref[spot], 1), :]
                rows[pl.ds(cap + line, 1), :] = total

        out_ref[chip, pl.ds(0, cap), :] = rows[pl.ds(0, cap), :].astype(BF16)
        out_ref[chip, pl.ds(cap, cap), :] = (rows[pl.ds(cap, cap), :] / fan).astype(BF16)


def gather_rows(place, own_table, other_table, w_one, self_one, near_one, chips):
    nodes = own_table.shape[1]
    cap = self_one.shape[0] // (2 * chips)
    chunk = 2 * cap + w_one.shape[0] * w_one.shape[1] // LANES
    return pl.pallas_call(
        gather_kernel,
        out_shape=jax.ShapeDtypeStruct((chips, chunk, LANES), BF16),
        in_specs=[pl.BlockSpec(memory_space=SMEM)] + vmem(3) + [pl.BlockSpec(memory_space=SMEM)] * 2,
        out_specs=pl.BlockSpec(memory_space=VMEM),
        scratch_shapes=[VMEM((nodes, LANES), F32), VMEM((2 * cap, LANES), F32)],
        compiler_params=pltpu.CompilerParams(vmem_limit_bytes=48 << 20),
        cost_estimate=pl.CostEstimate(flops=1 << 27, bytes_accessed=40 << 20, transcendentals=0),
        name="gather_rows",
    )(place, own_table, other_table, w_one, self_one, near_one.reshape(-1))


def owner_kernel(
    place_ref,
    count_ref,
    rows_ref,
    w_other_ref,
    bias_one_ref,
    self_two_ref,
    near_two_ref,
    self_three_ref,
    near_three_ref,
    targets_ref,
    w_two_ref,
    bias_two_ref,
    w_three_ref,
    bias_three_ref,
    keep_ref,
    send_ref,
    pre_one,
    mids,
    tops,
):
    core = place_ref[0]
    owner = place_ref[1]
    chips = rows_ref.shape[0]
    cap, hidden = pre_one.shape
    labels = w_three_ref.shape[1]
    mid_rows = self_two_ref.shape[1]
    seeds = self_three_ref.shape[1]
    fan_two = near_two_ref.shape[0]
    fan_three = near_three_ref.shape[0]
    tiles = hidden // LANES
    half = LANES // 2

    total = None
    for chip in range(chips):
        columns = []
        for tile in range(tiles):
            mine = 2 * cap + tile * LANES
            other = tile * LANES
            columns.append(
                jnp.concatenate(
                    [
                        rows_ref[chip, pl.ds(mine, half), :],
                        w_other_ref[chip, pl.ds(other, half), :],
                        rows_ref[chip, pl.ds(mine + half, half), :],
                        w_other_ref[chip, pl.ds(other + half, half), :],
                    ],
                    axis=0,
                )
            )
        wide = jnp.concatenate([rows_ref[chip, pl.ds(0, cap), :], rows_ref[chip, pl.ds(cap, cap), :]], axis=1)
        part = dot(wide, jnp.concatenate(columns, axis=1))
        total = part if total is None else total + part
    pre_one[...] = total + bias_one_ref[...]
    values = pre_one[...]
    hidden_one = (values * gelu_cdf(values)).astype(BF16)

    spots = lax.broadcasted_iota(jnp.int32, (cap, mid_rows), 0)
    self_two_t = (spots == self_two_ref[...]).astype(F32)
    near_two_t = jnp.zeros((cap, mid_rows), F32)
    for offset in range(fan_two):
        near_two_t += (spots == near_two_ref[pl.ds(offset, 1), :]).astype(F32)
    self_mid = dot(self_two_t.T.astype(BF16), hidden_one).astype(BF16)
    near_mid = (dot(near_two_t.T.astype(BF16), hidden_one) / fan_two).astype(BF16)
    mids[0] = self_mid
    mids[1] = near_mid
    pre_two = dot(self_mid, w_two_ref[0]) + dot(near_mid, w_two_ref[1]) + bias_two_ref[...]
    hidden_two = (pre_two * gelu_cdf(pre_two)).astype(BF16)

    spots = lax.broadcasted_iota(jnp.int32, (mid_rows, seeds), 0)
    self_three_t = (spots == self_three_ref[...]).astype(F32)
    near_three_t = jnp.zeros((mid_rows, seeds), F32)
    for offset in range(fan_three):
        near_three_t += (spots == near_three_ref[pl.ds(offset, 1), :]).astype(F32)
    self_top = dot(self_three_t.T.astype(BF16), hidden_two).astype(BF16)
    near_top = (dot(near_three_t.T.astype(BF16), hidden_two) / fan_three).astype(BF16)
    tops[0] = self_top
    tops[1] = near_top
    logits = back_dot(self_top, w_three_ref[0]) + back_dot(near_top, w_three_ref[1]) + bias_three_ref[...]

    live_total = lax.fori_loop(0, count_ref.shape[0], lambda i, t: t + count_ref[i], jnp.int32(0))
    scale = 1.0 / jnp.sqrt(jnp.full((1, labels), live_total, jnp.int32).astype(F32))
    live = lax.broadcasted_iota(jnp.int32, (seeds, labels), 0) < count_ref[owner]
    slope = jax.nn.sigmoid(logits) - targets_ref[...].astype(F32)
    logit_grad = jnp.where(live, slope * scale, 0.0).astype(BF16)

    self_grad = dot(logit_grad, w_three_ref[0])
    near_grad = dot(logit_grad, w_three_ref[1]) / fan_three
    upstream = exact_dot(self_three_t.astype(BF16), self_grad)
    upstream += exact_dot(near_three_t.astype(BF16), near_grad)
    pre_grad_two = (gelu_slope(pre_two) * upstream).astype(BF16)

    self_grad = back_dot(pre_grad_two, w_two_ref[0])
    near_grad = back_dot(pre_grad_two, w_two_ref[1]) / fan_two
    upstream = exact_dot(self_two_t.astype(BF16), self_grad)
    upstream += exact_dot(near_two_t.astype(BF16), near_grad)
    pre_grad_one = (gelu_slope(pre_one[...]) * upstream).astype(BF16)

    wide_logit = jnp.concatenate([logit_grad, jnp.zeros((seeds, LANES - labels), BF16)], axis=1)
    bias_three = jnp.sum(wide_logit.astype(F32), axis=0, keepdims=True)
    biases = jnp.concatenate(
        [
            jnp.sum(pre_grad_one.astype(F32), axis=0, keepdims=True),
            jnp.sum(pre_grad_two.astype(F32), axis=0, keepdims=True),
            jnp.concatenate([bias_three, jnp.zeros((1, hidden - LANES), F32)], axis=1),
            jnp.zeros((LANES - labels - 3, hidden), F32),
        ],
        axis=0,
    )
    groups = PEERS // chips
    share = LANES // groups
    count = hidden // PEERS

    for chip in range(chips):
        for line in (0, 1):
            block = lead_dot(rows_ref[chip, pl.ds(line * cap, cap), :], pre_grad_one).astype(BF16)
            for out_ref, start in ((keep_ref, 0), (send_ref, half)):
                for group in range(groups // 2):
                    first = start + group * share
                    peer = (line * (groups // 2) + group) * chips + chip
                    for tile in range(tiles):
                        out_ref[peer, pl.ds(tile * share, share), :] = block[
                            first : first + share, tile * LANES : (tile + 1) * LANES
                        ]
    for out_ref, side in ((send_ref, 1 - core), (keep_ref, core)):
        two = lead_dot(mids[side], pre_grad_two)
        top = lead_dot(wide_logit, tops[side])
        top = jnp.concatenate([top[:labels], biases * (side == 0).astype(F32)], axis=0).T
        for peer in range(PEERS):
            late = [
                two[peer * count : (peer + 1) * count, tile * LANES : (tile + 1) * LANES]
                for tile in range(tiles)
            ]
            late.append(top[peer * count : (peer + 1) * count, :])
            out_ref[peer, pl.ds(ONE_ROWS, LATE_ROWS), :] = jnp.concatenate(late, axis=0).astype(BF16)


def owner_pass(place, seed_count, rows, w_other, bias_one, self_two, near_two, self_three, near_three,
               targets, w_two, bias_two, w_three, bias_three, cap):
    hidden = w_two.shape[2]
    chunk = jax.ShapeDtypeStruct((PEERS, CHUNK_ROWS, LANES), BF16)
    return pl.pallas_call(
        owner_kernel,
        out_shape=(chunk, chunk),
        in_specs=[pl.BlockSpec(memory_space=SMEM)] * 2 + vmem(12),
        out_specs=tuple(vmem(2)),
        scratch_shapes=[
            VMEM((cap, hidden), F32),
            VMEM((2, near_two.shape[1], hidden), BF16),
            VMEM((2, near_three.shape[1], hidden), BF16),
        ],
        compiler_params=pltpu.CompilerParams(vmem_limit_bytes=48 << 20),
        cost_estimate=pl.CostEstimate(flops=1 << 31, bytes_accessed=10 << 20, transcendentals=1 << 19),
        name="owner_pass",
    )(
        place, seed_count, rows, w_other, bias_one.reshape(1, -1), self_two.reshape(1, -1), near_two,
        self_three.reshape(1, -1), near_three, targets, w_two, bias_two.reshape(1, -1),
        jnp.transpose(w_three, (0, 2, 1)), bias_three.reshape(1, -1),
    )


def sum_kernel(parts_ref, out_ref):
    total = parts_ref[0].astype(F32)
    for peer in range(1, PEERS):
        total = total + parts_ref[peer].astype(F32)
    total = total.astype(BF16)
    for peer in range(PEERS):
        out_ref[peer] = total


def sum_parts(parts):
    return pl.pallas_call(
        sum_kernel,
        out_shape=jax.ShapeDtypeStruct(parts.shape, BF16),
        in_specs=vmem(1),
        out_specs=pl.BlockSpec(memory_space=VMEM),
        compiler_params=pltpu.CompilerParams(vmem_limit_bytes=48 << 20),
        name="sum_parts",
    )(parts)


def unpack_kernel(place_ref, own_ref, other_ref, grad_one, bias_one, grad_two, bias_two, grad_three, bias_three, top):
    core = place_ref[0]
    chip = place_ref[2]
    hidden = grad_one.shape[2]
    tiles = hidden // LANES
    share = ONE_ROWS // tiles
    groups = 2 * grad_one.shape[1] // share
    chips = PEERS // groups
    for group in range(groups):
        layer, line = divmod(group * share, grad_one.shape[1])
        for tile in range(tiles):
            grad_one[layer, pl.ds(line, share), pl.ds(tile * LANES, LANES)] = own_ref[
                group * chips + chip, pl.ds(tile * share, share), :
            ].astype(F32)
    count = hidden // PEERS
    labels = grad_three.shape[1]
    for ref, start, side in ((own_ref, ONE_ROWS, core), (other_ref, 0, 1 - core)):
        for peer in range(PEERS):
            late = ref[peer, pl.ds(start, LATE_ROWS), :].astype(F32)
            for tile in range(tiles):
                grad_two[side, pl.ds(peer * count, count), pl.ds(tile * LANES, LANES)] = late[
                    tile * count : (tile + 1) * count
                ]
            top[side, pl.ds(peer * count, count), :] = late[TWO_ROWS:]
    for side in (0, 1):
        flipped = top[side].T
        grad_three[side] = flipped[:labels]
        if side == 0:
            bias_one[...] = flipped[labels : labels + 1]
            bias_two[...] = flipped[labels + 1 : labels + 2]
            bias_three[...] = flipped[labels + 2 : labels + 3, :labels]


def unpack(place, own, other, cut_rows, hidden, labels):
    return pl.pallas_call(
        unpack_kernel,
        out_shape=(
            jax.ShapeDtypeStruct((2, cut_rows, hidden), F32),
            jax.ShapeDtypeStruct((1, hidden), F32),
            jax.ShapeDtypeStruct((2, hidden, hidden), F32),
            jax.ShapeDtypeStruct((1, hidden), F32),
            jax.ShapeDtypeStruct((2, labels, hidden), F32),
            jax.ShapeDtypeStruct((1, labels), F32),
        ),
        in_specs=[pl.BlockSpec(memory_space=SMEM)] + vmem(2),
        out_specs=tuple(vmem(6)),
        scratch_shapes=[VMEM((2, hidden, LANES), F32)],
        compiler_params=pltpu.CompilerParams(vmem_limit_bytes=48 << 20),
        name="unpack",
    )(place, own, other)


def exchange(values, axes):
    return lax.all_to_all(values, axes, 0, 0, tiled=True)


def swap_core(values):
    return lax.ppermute(values, "core", [(0, 1), (1, 0)])


def local(
    feat_table,
    self_one,
    near_one,
    self_two,
    near_two,
    self_three,
    near_three,
    targets,
    seed_count,
    w_one,
    bias_one,
    w_two,
    bias_two,
    w_three,
    bias_three,
):
    cut_rows, hidden = w_one.shape[1:]
    labels = w_three.shape[2]
    chips = lax.axis_size(CHIPS)
    cap = self_one.shape[0] // (2 * chips)
    owner = lax.axis_index(DP) * lax.axis_size(CUTS) + lax.axis_index(CUTS)
    place = jnp.stack([lax.axis_index("core"), owner, lax.axis_index(CHIPS)]).astype(jnp.int32)
    other_table = swap_core(feat_table)
    rows = gather_rows(place, feat_table, other_table, w_one.reshape(-1, hidden), self_one, near_one, chips)
    rows = exchange(rows, CHIPS)
    w_other = swap_core(rows[:, 2 * cap :])
    keep, send = owner_pass(
        place, seed_count, rows, w_other, bias_one, self_two, near_two, self_three, near_three,
        targets, w_two, bias_two, w_three, bias_three, cap,
    )
    parts = (keep.astype(F32) + swap_core(send).astype(F32)).astype(BF16)
    sums = sum_parts(exchange(parts, SAME_CORE))
    own = exchange(sums, SAME_CORE)
    other = swap_core(own[:, ONE_ROWS:])
    grad_one, bias_one, grad_two, bias_two, grad_three, bias_three = unpack(
        place, own, other, cut_rows, hidden, labels
    )
    return (
        grad_one,
        bias_one.reshape(-1),
        grad_two,
        bias_two.reshape(-1),
        jnp.transpose(grad_three, (0, 2, 1)),
        bias_three.reshape(-1),
    )


def solution(mesh):
    fine = Mesh(mesh.devices.reshape(2, 4, 4, 2, 2), ("y_hi", "x", "z", "y_lo", "core"))
    both = DP + CUTS
    return jax.shard_map(
        local,
        mesh=fine,
        in_specs=(
            P(CUTS, DP),
            P(DP),
            P(None, DP),
            P(both),
            P(None, both),
            P(both),
            P(None, both),
            P(both, None),
            P(),
            P(None, CUTS, None),
            P(),
            P(),
            P(),
            P(),
            P(),
        ),
        out_specs=(P(None, CUTS, None), P(), P(), P(), P(), P()),
        check_vma=False,
    )
```

time: 149 us -> 142 us (0.953)
  blocking collectives: 61.5 us -> 91.8 us
  between operations: 14.2 us -> 0.83 us
  Pallas kernels: 35.9 us -> 25.7 us
  waiting for transfers between devices: 19.7 us -> 10.2 us
  starting transfers between devices: 12.2 us -> 6.84 us
    all_to_all x3, blocking collectives: 61.5 us -> 91.8 us  [exchange(): return lax.all_to_all(values, axes, 0, 0, tiled=True)]
    all_to_all x1 -> x0, waiting for transfers between devices: 15.6 us -> none  [exchange(): return lax.all_to_all(values, axes, 0, 0, tiled=True)]
    pallas_call x2, Pallas kernels: 27.4 us -> 16.8 us  [the longest x1 16.5 us: gather_rows(): pl.pallas_call(gather_kernel, out_shape=jax.ShapeDtypeStruct((chips, chun...]
    all_to_all x1 -> x0, starting transfers between devices: 7.99 us -> none  [exchange(): return lax.all_to_all(values, axes, 0, 0, tiled=True)]
    ppermute x2 -> x4, waiting for transfers between devices: 3.41 us -> 10.2 us  [swap_core(): return lax.ppermute(values, 'core', [(0, 1), (1, 0)])]
    ppermute x2 -> x4, starting transfers between devices: 4.23 us -> 6.84 us  [swap_core(): return lax.ppermute(values, 'core', [(0, 1), (1, 0)])]
    unnamed x28 -> x32, local copies, waits for them, and re-layouts: 3.51 us -> 4.59 us
  transfers between devices with their start and end apart: 4 -> 4, of which waited for: 2 -> 4; matrix products, arithmetic and copies ran while one was open for 1% -> 1% of each run, Pallas kernels for 18% -> 0%
where the time goes in v2:
time: 142 us
  blocking collectives  91.8 us (65%)
  Pallas kernels  25.7 us (18%)
  waiting for transfers between devices  10.2 us (7%)
  starting transfers between devices  6.84 us (5%)
  local copies, waits for them, and re-layouts  5.67 us (4%)
    all_to_all x3, blocking collectives, exchange(): return lax.all_to_all(values, axes, 0, 0, tiled=True)  91.8 us
    pallas_call x1, Pallas kernels, gather_rows(): pl.pallas_call(gather_kernel, out_shape=jax.ShapeDtypeStruct((chips, chun...  16.5 us
    ppermute x4, waiting for transfers between devices, swap_core(): return lax.ppermute(values, 'core', [(0, 1), (1, 0)])  10.2 us
    ppermute x4, starting transfers between devices, swap_core(): return lax.ppermute(values, 'core', [(0, 1), (1, 0)])  6.84 us
    pallas_call x1, Pallas kernels, owner_pass(): pl.pallas_call(owner_kernel, out_shape=(chunk, chunk), in_specs=[pl.Block...  6.51 us
    unnamed x32, local copies, waits for them, and re-layouts  4.59 us
  transfers between devices with their start and end apart: 4, of which 4 were waited for; matrix products, arithmetic and copies ran while one was open for 1% of the time, Pallas kernels for 0%

profile of v2, /device:TPU:1, one launch (start us, length us, event | category | flops | bytes accessed | tf_op | source)
XLA Modules:
  0.0 141.6 jit_solution(13346020372512211450)
XLA Ops:
  0.6 1.5 %collective-permute-start = (bf16[64,16384]{1,0:T(8,128)(2,1)}, bf16[64,16384]{1,0:T(8,128)(2,1)S(1)}, u32[]{:S(2)}, u32[]{:S(2)}) collective-permute-start(bf16[64,16384]{1,0:T(8,128)(2,1)} %own_ref.1), channel_id=1, source_target_pairs={{0,1},{1,0},{2,3},{3,2},{4,5},{5,4},{6,7},{7,6},{8,9},{9,8},{10,11... | collective-permute-start | bytes 6291464 | tf_op jit(solution)/shard_map/ppermute | solution.py:354
  2.1 0.9 reshape.43.near_ref
  3.1 0.1 pad_add_fusion.place_ref
  3.2 3.0 %collective-permute-done.other_ref = bf16[64,16384]{1,0:T(8,128)(2,1)S(1)} collective-permute-done((bf16[64,16384]{1,0:T(8,128)(2,1)}, bf16[64,16384]{1,0:T(8,128)(2,1)S(1)}, u32[]{:S(2)}, u32[]{:S(2)}) %collective-permute-start) | collective-permute-done | bytes 2097184 | tf_op jit(solution)/shard_map/ppermute | solution.py:354
  6.1 0.0 copy-start.15
  6.1 1.3 copy-done.15
  7.4 0.0 copy-start
  7.5 1.6 %copy-done = bf16[64,16384]{1,0:T(8,128)(2,1)S(1)} copy-done((bf16[64,16384]{1,0:T(8,128)(2,1)S(1)}, bf16[64,16384]{1,0:T(8,128)(2,1)}, u32[]{:S(2)}) %copy-start) | copy-done | bytes 2097176
  9.0 0.0 copy-start.1
  9.0 0.9 copy-done.1
  9.9 0.0 copy-start.2
  9.9 0.7 copy-done.2
  10.7 16.5 %gather_rows.1 = bf16[8,1024,128]{2,1,0:T(8,128)(2,1)S(1)} custom-call(s32[3]{0:T(128)S(1)} %pad_add_fusion.place_ref, bf16[64,16384]{1,0:T(8,128)(2,1)S(1)} %copy-done, bf16[64,16384]{1,0:T(8,128)(2,1)} %copy-done.15, bf16[128,512]{1,0:T(8,128)(2,1)S(1)} %bitcast.14, s32[4096]{0:T(1024)S(1)} %copy-done.2, s32[20480]{0:T(1024)S(1)} %reshape.43.near_ref), custom_call_target="tpu_custom_call" | custom-call | flops 134217728 | bytes 41943040 | tf_op jit(solution)/shard_map/gather_rows/pallas_call | solution.py:104
  27.2 32.0 %all_to_all.15.rows_ref = bf16[8,1024,128]{2,1,0:T(8,128)(2,1)S(1)} all-to-all(bf16[8,1024,128]{2,1,0:T(8,128)(2,1)S(1)} %gather_rows.1), channel_id=1, replica_groups=mesh['y_hi'=2,'x'=4,'z'=4,'y_lo'=2,'core'=2] {'z','y_lo'}, dimensions={0} | all-to-all | bytes 4194304 | tf_op jit(solution)/shard_map/all_to_all | solution.py:350
  59.2 0.0 copy-start.14
  59.2 0.0 copy-start.3
  59.2 0.0 copy-start.4
  59.2 0.0 copy-start.5
  59.2 0.0 copy-start.6
  59.2 0.0 copy-start.7
  59.2 0.0 copy-start.8
  59.2 0.0 copy-start.9
  59.2 0.0 copy-start.10
  59.2 0.0 copy-start.11
  59.3 0.0 copy-start.12
  59.3 0.0 copy-start.13
  59.3 0.1 slice.8
  59.4 1.9 %collective-permute-start.1 = (bf16[8,512,128]{2,1,0:T(8,128)(2,1)S(1)}, bf16[8,512,128]{2,1,0:T(8,128)(2,1)S(1)}, u32[]{:S(2)}, u32[]{:S(2)}) collective-permute-start(bf16[8,512,128]{2,1,0:T(8,128)(2,1)S(1)} %slice.8), channel_id=1, source_target_pairs={{0,1},{1,0},{2,3},{3,2},{4,5},{5,4},{6,7},{7,6},{8,9},{9,8},{10,11... | collective-permute-start | bytes 3145736 | tf_op jit(solution)/shard_map/ppermute | solution.py:354
  61.3 2.3 %collective-permute-done.1.w_other_ref = bf16[8,512,128]{2,1,0:T(8,128)(2,1)S(1)} collective-permute-done((bf16[8,512,128]{2,1,0:T(8,128)(2,1)S(1)}, bf16[8,512,128]{2,1,0:T(8,128)(2,1)S(1)}, u32[]{:S(2)}, u32[]{:S(2)}) %collective-permute-start.1) | collective-permute-done | bytes 1048608 | tf_op jit(solution)/shard_map/ppermute | solution.py:354
  63.5 0.0 copy-done.14
  63.5 0.0 copy-done.3
  63.6 0.0 copy-done.4
  63.6 0.0 copy-done.5
  63.6 0.0 copy-done.6
  63.6 0.0 copy-done.7
  63.6 0.0 copy-done.8
  63.6 0.0 copy-done.9
  63.6 0.0 copy-done.10
  63.6 0.0 copy-done.11
  63.6 0.0 copy-done.12
  63.6 0.0 copy-done.13
  63.6 6.5 %owner_pass.1 = (bf16[64,104,128]{2,1,0:T(8,128)(2,1)S(1)}, bf16[64,104,128]{2,1,0:T(8,128)(2,1)S(1)}) custom-call(s32[3]{0:T(128)S(1)} %pad_add_fusion.place_ref, s32[128]{0:T(128)S(1)} %copy-done.10, bf16[8,1024,128]{2,1,0:T(8,128)(2,1)} %copy-done.14, bf16[8,512,128]{2,1,0:T(8,128)(2,1)S(1)} %collective-permute-done.1.w_other_ref, f32[1,512]{1,0:T(1,128)S(1)} %bitcast.16, ...), custom_call_target="tpu_custom_call" | custom-call | flops 2147483648 | bytes 10485760 | tf_op jit(solution)/shard_map/owner_pass/pallas_call | solution.py:257
  70.2 0.5 collective-permute-start.2
  70.6 3.2 %collective-permute-done.2 = bf16[64,104,128]{2,1,0:T(8,128)(2,1)S(1)} collective-permute-done((bf16[64,104,128]{2,1,0:T(8,128)(2,1)S(1)}, bf16[64,104,128]{2,1,0:T(8,128)(2,1)S(1)}, u32[]{:S(2)}, u32[]{:S(2)}) %collective-permute-start.2) | collective-permute-done | bytes 1703968 | tf_op jit(solution)/shard_map/ppermute | solution.py:354
  73.8 0.4 add_convert_fusion
  74.3 31.3 %all_to_all.16.parts_ref = bf16[64,104,128]{2,1,0:T(8,128)(2,1)S(1)} all-to-all(bf16[64,104,128]{2,1,0:T(8,128)(2,1)S(1)} %add_convert_fusion), channel_id=1, replica_groups=mesh['y_hi'=2,'x'=4,'z'=4,'y_lo'=2,'core'=2] {'y_hi','x','z','y_lo'}, dimensions={0} | all-to-all | bytes 3407872 | tf_op jit(solution)/shard_map/all_to_all | solution.py:350
  105.6 0.3 sum_parts.1
  105.9 28.6 %all_to_all.17.own_ref = bf16[64,104,128]{2,1,0:T(8,128)(2,1)S(1)} all-to-all(bf16[64,104,128]{2,1,0:T(8,128)(2,1)S(1)} %sum_parts.1), channel_id=1, replica_groups=mesh['y_hi'=2,'x'=4,'z'=4,'y_lo'=2,'core'=2] {'y_hi','x','z','y_lo'}, dimensions={0} | all-to-all | bytes 3407872 | tf_op jit(solution)/shard_map/all_to_all | solution.py:350
  134.5 0.1 slice.9
  134.5 3.0 %collective-permute-start.3 = (bf16[64,40,128]{2,1,0:T(8,128)(2,1)S(1)}, bf16[64,40,128]{2,1,0:T(8,128)(2,1)S(1)}, u32[]{:S(2)}, u32[]{:S(2)}) collective-permute-start(bf16[64,40,128]{2,1,0:T(8,128)(2,1)S(1)} %slice.9), channel_id=1, source_target_pairs={{0,1},{1,0},{2,3},{3,2},{4,5},{5,4},{6,7},{7,6},{8,9},{9,8},{10,11... | collective-permute-start | bytes 1966088 | tf_op jit(solution)/shard_map/ppermute | solution.py:354
  137.5 1.7 %collective-permute-done.3.other_ref = bf16[64,40,128]{2,1,0:T(8,128)(2,1)S(1)} collective-permute-done((bf16[64,40,128]{2,1,0:T(8,128)(2,1)S(1)}, bf16[64,40,128]{2,1,0:T(8,128)(2,1)S(1)}, u32[]{:S(2)}, u32[]{:S(2)}) %collective-permute-start.3) | collective-permute-done | bytes 655392 | tf_op jit(solution)/shard_map/ppermute | solution.py:354
  139.2 2.3 %unpack.1 = (f32[2,64,512]{2,1,0:T(8,128)}, f32[1,512]{1,0:T(1,128)}, f32[2,512,512]{2,1,0:T(8,128)}, f32[1,512]{1,0:T(1,128)}, f32[2,112,512]{2,1,0:T(8,128)}, /*index=5*/f32[1,112]{1,0:T(1,128)}) custom-call(s32[3]{0:T(128)S(1)} %pad_add_fusion.place_ref, bf16[64,104,128]{2,1,0:T(8,128)(2,1)S(1)} %all_to_all.17.own_ref, ...), custom_call_target="tpu_custom_call" | custom-call | tf_op jit(solution)/shard_map/unpack/pallas_call | solution.py:331
Async XLA Ops:
  0.6 5.5 %collective-permute-start = (bf16[64,16384]{1,0:T(8,128)(2,1)}, bf16[64,16384]{1,0:T(8,128)(2,1)S(1)}, u32[]{:S(2)}, u32[]{:S(2)}) collective-permute-start(bf16[64,16384]{1,0:T(8,128)(2,1)} %own_ref.1), channel_id=1, source_target_pairs={{0,1},{1,0},{2,3},{3,2},{4,5},{5,4},{6,7},{7,6},{8,9},{9,8},{10,11... | collective-permute-start | bytes 6291464 | tf_op jit(solution)/shard_map/ppermute | solution.py:354
  6.1 1.3 copy-start.15
  7.4 1.6 %copy-start = (bf16[64,16384]{1,0:T(8,128)(2,1)S(1)}, bf16[64,16384]{1,0:T(8,128)(2,1)}, u32[]{:S(2)}) copy-start(bf16[64,16384]{1,0:T(8,128)(2,1)} %own_ref.1) | copy-start | bytes 6291460
  9.0 0.9 copy-start.1
  9.9 0.7 copy-start.2
  59.2 4.4 %copy-start.14 = (bf16[8,1024,128]{2,1,0:T(8,128)(2,1)}, bf16[8,1024,128]{2,1,0:T(8,128)(2,1)S(1)}, u32[]{:S(2)}) copy-start(bf16[8,1024,128]{2,1,0:T(8,128)(2,1)S(1)} %all_to_all.15.rows_ref) | copy-start | bytes 6291460
  59.2 4.4 %copy-start.3 = (bf16[2,512,512]{2,1,0:T(8,128)(2,1)S(1)}, bf16[2,512,512]{2,1,0:T(8,128)(2,1)}, u32[]{:S(2)}) copy-start(bf16[2,512,512]{2,1,0:T(8,128)(2,1)} %w_two_ref.1) | copy-start | bytes 3145732
  59.2 4.4 %copy-start.4 = (bf16[2,512,112]{1,2,0:T(8,128)(2,1)S(1)}, bf16[2,512,112]{1,2,0:T(8,128)(2,1)}, u32[]{:S(2)}) copy-start(bf16[2,512,112]{1,2,0:T(8,128)(2,1)} %param.28) | copy-start | bytes 688132
  59.2 4.4 %copy-start.5 = (s32[32,112]{1,0:T(8,128)S(1)}, s32[32,112]{1,0:T(8,128)}, u32[]{:S(2)}) copy-start(s32[32,112]{1,0:T(8,128)} %targets_ref.1) | copy-start | bytes 43012
  59.2 4.4 %copy-start.6 = (s32[10,128]{1,0:T(8,128)S(1)}, s32[10,128]{1,0:T(8,128)}, u32[]{:S(2)}) copy-start(s32[10,128]{1,0:T(8,128)} %near_two_ref.1) | copy-start | bytes 15364
  59.2 4.4 %copy-start.7 = (s32[15,32]{1,0:T(8,128)S(1)}, s32[15,32]{1,0:T(8,128)}, u32[]{:S(2)}) copy-start(s32[15,32]{1,0:T(8,128)} %near_three_ref.1) | copy-start | bytes 5764
  59.2 4.4 %copy-start.8 = (f32[512]{0:T(512)S(1)}, f32[512]{0:T(512)}, u32[]{:S(2)}) copy-start(f32[512]{0:T(512)} %param.25) | copy-start | bytes 6148
  59.2 4.4 %copy-start.9 = (f32[512]{0:T(512)S(1)}, f32[512]{0:T(512)}, u32[]{:S(2)}) copy-start(f32[512]{0:T(512)} %param.27) | copy-start | bytes 6148
  59.2 4.4 %copy-start.10 = (s32[128]{0:T(128)S(1)}, s32[128]{0:T(128)}, u32[]{:S(2)}) copy-start(s32[128]{0:T(128)} %count_ref.1) | copy-start | bytes 1540
  59.2 4.4 %copy-start.11 = (s32[128]{0:T(128)S(1)}, s32[128]{0:T(128)}, u32[]{:S(2)}) copy-start(s32[128]{0:T(128)} %param.18) | copy-start | bytes 1540
  59.3 4.4 %copy-start.12 = (s32[32]{0:T(128)S(1)}, s32[32]{0:T(128)}, u32[]{:S(2)}) copy-start(s32[32]{0:T(128)} %param.20) | copy-start | bytes 388
  59.3 4.4 %copy-start.13 = (f32[112]{0:T(128)S(1)}, f32[112]{0:T(128)}, u32[]{:S(2)}) copy-start(f32[112]{0:T(128)} %param.29) | copy-start | bytes 1348
  59.4 4.2 %collective-permute-start.1 = (bf16[8,512,128]{2,1,0:T(8,128)(2,1)S(1)}, bf16[8,512,128]{2,1,0:T(8,128)(2,1)S(1)}, u32[]{:S(2)}, u32[]{:S(2)}) collective-permute-start(bf16[8,512,128]{2,1,0:T(8,128)(2,1)S(1)} %slice.8), channel_id=1, source_target_pairs={{0,1},{1,0},{2,3},{3,2},{4,5},{5,4},{6,7},{7,6},{8,9},{9,8},{10,11... | collective-permute-start | bytes 3145736 | tf_op jit(solution)/shard_map/ppermute | solution.py:354
  70.2 3.7 %collective-permute-start.2 = (bf16[64,104,128]{2,1,0:T(8,128)(2,1)S(1)}, bf16[64,104,128]{2,1,0:T(8,128)(2,1)S(1)}, u32[]{:S(2)}, u32[]{:S(2)}) collective-permute-start(bf16[64,104,128]{2,1,0:T(8,128)(2,1)S(1)} %get-tuple-element.15), channel_id=1, source_target_pairs={{0,1},{1,0},{2,3},{3,2},{4,5},{5,4},{6,7},{7,6},{8,9},{9,8},{10,11... | collective-permute-start | bytes 5111816 | tf_op jit(solution)/shard_map/ppermute | solution.py:354
  134.5 4.7 %collective-permute-start.3 = (bf16[64,40,128]{2,1,0:T(8,128)(2,1)S(1)}, bf16[64,40,128]{2,1,0:T(8,128)(2,1)S(1)}, u32[]{:S(2)}, u32[]{:S(2)}) collective-permute-start(bf16[64,40,128]{2,1,0:T(8,128)(2,1)S(1)} %slice.9), channel_id=1, source_target_pairs={{0,1},{1,0},{2,3},{3,2},{4,5},{5,4},{6,7},{7,6},{8,9},{9,8},{10,11... | collective-permute-start | bytes 1966088 | tf_op jit(solution)/shard_map/ppermute | solution.py:354

commit v3 on v2

--- a/solution.py
+++ b/solution.py
@@ -11,7 +11,9 @@
 SMEM = pltpu.SMEM
 
 LANES = 128
+SUB = 8
 GATHER_UNROLL = 16
+TABLE_PIECES = 8
 ONE_ROWS = 64
 TWO_ROWS = 32
 TOP_ROWS = 8
@@ -58,25 +60,43 @@
     return [pl.BlockSpec(memory_space=VMEM)] * count
 
 
-def gather_kernel(place_ref, own_ref, other_ref, w_one_ref, self_ref, near_ref, out_ref, table, rows):
+def gather_kernel(
+    place_ref, own_ref, other_ref, self_ref, near_ref, out_ref, own, other, self_ids, near_ids, table, rows, sems, id_sems
+):
     core = place_ref[0]
     nodes = own_ref.shape[1]
     targets = self_ref.shape[0]
     fan = near_ref.shape[0] // targets
     chips = out_ref.shape[0]
     cap = targets // (2 * chips)
-
-    @pl.loop(0, nodes // LANES, unroll=4)
-    def _(block):
-        spot = pl.ds(pl.multiple_of(block * LANES, LANES), LANES)
-        part = jnp.concatenate([own_ref[:, spot], other_ref[:, spot]], axis=0).astype(F32)
-        table[spot, :] = part.T
-
-    tiles = w_one_ref.shape[1] // LANES
-    for tile in range(tiles):
-        block = w_one_ref[:, pl.ds(tile * LANES, LANES)]
-        for chip in range(chips):
-            out_ref[chip, pl.ds(2 * cap + tile * LANES, LANES), :] = block
+    width = nodes // TABLE_PIECES
+
+    fetches = []
+    for piece in range(TABLE_PIECES):
+        spot = pl.ds(piece * width, width)
+        for slot, (source, held) in enumerate(((own_ref, own), (other_ref, other))):
+            fetch = pltpu.make_async_copy(source.at[:, spot], held.at[:, spot], sems.at[slot, piece])
+            fetch.start()
+            fetches.append(fetch)
+    id_fetches = [
+        pltpu.make_async_copy(self_ref, self_ids, id_sems.at[0]),
+        pltpu.make_async_copy(near_ref, near_ids, id_sems.at[1]),
+    ]
+    for fetch in id_fetches:
+        fetch.start()
+
+    for piece in range(TABLE_PIECES):
+        fetches[2 * piece].wait()
+        fetches[2 * piece + 1].wait()
+
+        @pl.loop(0, width // LANES, unroll=4)
+        def _(block):
+            spot = pl.ds(pl.multiple_of(piece * width + block * LANES, LANES), LANES)
+            part = jnp.concatenate([own[:, spot], other[:, spot]], axis=0).astype(F32)
+            table[spot, :] = part.T
+
+    for fetch in id_fetches:
+        fetch.wait()
 
     @pl.loop(0, chips)
     def _(chip):
@@ -87,36 +107,48 @@
             for step in range(GATHER_UNROLL):
                 line = group * GATHER_UNROLL + step
                 spot = first + line
-                total = table[pl.ds(near_ref[spot], 1), :]
+                total = table[pl.ds(near_ids[spot], 1), :]
                 for offset in range(1, fan):
-                    total = total + table[pl.ds(near_ref[offset * targets + spot], 1), :]
-                rows[pl.ds(line, 1), :] = table[pl.ds(self_ref[spot], 1), :]
+                    total = total + table[pl.ds(near_ids[offset * targets + spot], 1), :]
+                rows[pl.ds(line, 1), :] = table[pl.ds(self_ids[spot], 1), :]
                 rows[pl.ds(cap + line, 1), :] = total
 
         out_ref[chip, pl.ds(0, cap), :] = rows[pl.ds(0, cap), :].astype(BF16)
         out_ref[chip, pl.ds(cap, cap), :] = (rows[pl.ds(cap, cap), :] / fan).astype(BF16)
 
 
-def gather_rows(place, own_table, other_table, w_one, self_one, near_one, chips):
-    nodes = own_table.shape[1]
-    cap = self_one.shape[0] // (2 * chips)
-    chunk = 2 * cap + w_one.shape[0] * w_one.shape[1] // LANES
+def gather_rows(place, own_table, other_table, self_one, near_one, chips):
+    features, nodes = own_table.shape
+    targets = self_one.shape[0]
+    near_one = near_one.reshape(-1)
+    cap = targets // (2 * chips)
+    anywhere = pl.BlockSpec(memory_space=pl.ANY)
     return pl.pallas_call(
         gather_kernel,
-        out_shape=jax.ShapeDtypeStruct((chips, chunk, LANES), BF16),
-        in_specs=[pl.BlockSpec(memory_space=SMEM)] + vmem(3) + [pl.BlockSpec(memory_space=SMEM)] * 2,
+        out_shape=jax.ShapeDtypeStruct((chips, 2 * cap, LANES), BF16),
+        in_specs=[pl.BlockSpec(memory_space=SMEM)] + [anywhere] * 4,
         out_specs=pl.BlockSpec(memory_space=VMEM),
-        scratch_shapes=[VMEM((nodes, LANES), F32), VMEM((2 * cap, LANES), F32)],
+        scratch_shapes=[
+            VMEM((features, nodes), BF16),
+            VMEM((features, nodes), BF16),
+            SMEM(self_one.shape, jnp.int32),
+            SMEM(near_one.shape, jnp.int32),
+            VMEM((nodes, LANES), F32),
+            VMEM((2 * cap, LANES), F32),
+            pltpu.SemaphoreType.DMA((2, TABLE_PIECES)),
+            pltpu.SemaphoreType.DMA((2,)),
+        ],
         compiler_params=pltpu.CompilerParams(vmem_limit_bytes=48 << 20),
         cost_estimate=pl.CostEstimate(flops=1 << 27, bytes_accessed=40 << 20, transcendentals=0),
         name="gather_rows",
-    )(place, own_table, other_table, w_one, self_one, near_one.reshape(-1))
+    )(place, own_table, other_table, self_one, near_one)
 
 
 def owner_kernel(
     place_ref,
     count_ref,
     rows_ref,
+    w_own_ref,
     w_other_ref,
     bias_one_ref,
     self_two_ref,
@@ -148,23 +180,9 @@
 
     total = None
     for chip in range(chips):
-        columns = []
-        for tile in range(tiles):
-            mine = 2 * cap + tile * LANES
-            other = tile * LANES
-            columns.append(
-                jnp.concatenate(
-                    [
-                        rows_ref[chip, pl.ds(mine, half), :],
-                        w_other_ref[chip, pl.ds(other, half), :],
-                        rows_ref[chip, pl.ds(mine + half, half), :],
-                        w_other_ref[chip, pl.ds(other + half, half), :],
-                    ],
-                    axis=0,
-                )
-            )
+        depth = [ref[chip, pl.ds(line * half, half), :] for line in (0, 1) for ref in (w_own_ref, w_other_ref)]
         wide = jnp.concatenate([rows_ref[chip, pl.ds(0, cap), :], rows_ref[chip, pl.ds(cap, cap), :]], axis=1)
-        part = dot(wide, jnp.concatenate(columns, axis=1))
+        part = dot(wide, jnp.concatenate(depth, axis=0))
         total = part if total is None else total + part
     pre_one[...] = total + bias_one_ref[...]
     values = pre_one[...]
@@ -222,21 +240,22 @@
         ],
         axis=0,
     )
-    groups = PEERS // chips
-    share = LANES // groups
     count = hidden // PEERS
 
-    for chip in range(chips):
-        for line in (0, 1):
-            block = lead_dot(rows_ref[chip, pl.ds(line * cap, cap), :], pre_grad_one).astype(BF16)
-            for out_ref, start in ((keep_ref, 0), (send_ref, half)):
-                for group in range(groups // 2):
-                    first = start + group * share
-                    peer = (line * (groups // 2) + group) * chips + chip
-                    for tile in range(tiles):
-                        out_ref[peer, pl.ds(tile * share, share), :] = block[
-                            first : first + share, tile * LANES : (tile + 1) * LANES
-                        ]
+    for pair in range(chips // 2):
+        sides = []
+        for chip in (2 * pair, 2 * pair + 1):
+            blocks = [lead_dot(rows_ref[chip, pl.ds(line * cap, cap), :], pre_grad_one) for line in (0, 1)]
+            sides.append(
+                [jnp.concatenate([block[start : start + half] for block in blocks], axis=0) for start in (0, half)]
+            )
+        for out_ref, side in ((keep_ref, 0), (send_ref, 1)):
+            for peer in range(PEERS):
+                line, tile = divmod(peer, tiles)
+                cell = [
+                    both[side][line * SUB : (line + 1) * SUB, tile * LANES : (tile + 1) * LANES] for both in sides
+                ]
+                out_ref[peer, pl.ds(pair * 2 * SUB, 2 * SUB), :] = jnp.concatenate(cell, axis=0).astype(BF16)
     for out_ref, side in ((send_ref, 1 - core), (keep_ref, core)):
         two = lead_dot(mids[side], pre_grad_two)
         top = lead_dot(wide_logit, tops[side])
@@ -250,14 +269,14 @@
             out_ref[peer, pl.ds(ONE_ROWS, LATE_ROWS), :] = jnp.concatenate(late, axis=0).astype(BF16)
 
 
-def owner_pass(place, seed_count, rows, w_other, bias_one, self_two, near_two, self_three, near_three,
+def owner_pass(place, seed_count, rows, w_own, w_other, bias_one, self_two, near_two, self_three, near_three,
                targets, w_two, bias_two, w_three, bias_three, cap):
     hidden = w_two.shape[2]
     chunk = jax.ShapeDtypeStruct((PEERS, CHUNK_ROWS, LANES), BF16)
     return pl.pallas_call(
         owner_kernel,
         out_shape=(chunk, chunk),
-        in_specs=[pl.BlockSpec(memory_space=SMEM)] * 2 + vmem(12),
+        in_specs=[pl.BlockSpec(memory_space=SMEM)] * 2 + vmem(13),
         out_specs=tuple(vmem(2)),
         scratch_shapes=[
             VMEM((cap, hidden), F32),
@@ -268,7 +287,7 @@
         cost_estimate=pl.CostEstimate(flops=1 << 31, bytes_accessed=10 << 20, transcendentals=1 << 19),
         name="owner_pass",
     )(
-        place, seed_count, rows, w_other, bias_one.reshape(1, -1), self_two.reshape(1, -1), near_two,
+        place, seed_count, rows, w_own, w_other, bias_one.reshape(1, -1), self_two.reshape(1, -1), near_two,
         self_three.reshape(1, -1), near_three, targets, w_two, bias_two.reshape(1, -1),
         jnp.transpose(w_three, (0, 2, 1)), bias_three.reshape(1, -1),
     )
@@ -278,15 +297,18 @@
     total = parts_ref[0].astype(F32)
     for peer in range(1, PEERS):
         total = total + parts_ref[peer].astype(F32)
-    total = total.astype(BF16)
-    for peer in range(PEERS):
-        out_ref[peer] = total
+    late = total[ONE_ROWS:]
+    chips = ONE_ROWS // SUB
+    for chip in range(chips):
+        block = jnp.concatenate([total[chip * SUB : (chip + 1) * SUB], late], axis=0).astype(BF16)
+        for group in range(PEERS // chips):
+            out_ref[group * chips + chip] = block
 
 
 def sum_parts(parts):
     return pl.pallas_call(
         sum_kernel,
-        out_shape=jax.ShapeDtypeStruct(parts.shape, BF16),
+        out_shape=jax.ShapeDtypeStruct((PEERS, SUB + LATE_ROWS, LANES), BF16),
         in_specs=vmem(1),
         out_specs=pl.BlockSpec(memory_space=VMEM),
         compiler_params=pltpu.CompilerParams(vmem_limit_bytes=48 << 20),
@@ -296,28 +318,22 @@
 
 def unpack_kernel(place_ref, own_ref, other_ref, grad_one, bias_one, grad_two, bias_two, grad_three, bias_three, top):
     core = place_ref[0]
-    chip = place_ref[2]
-    hidden = grad_one.shape[2]
+    cut_rows, hidden = grad_one.shape[1:]
     tiles = hidden // LANES
-    share = ONE_ROWS // tiles
-    groups = 2 * grad_one.shape[1] // share
-    chips = PEERS // groups
-    for group in range(groups):
-        layer, line = divmod(group * share, grad_one.shape[1])
-        for tile in range(tiles):
-            grad_one[layer, pl.ds(line, share), pl.ds(tile * LANES, LANES)] = own_ref[
-                group * chips + chip, pl.ds(tile * share, share), :
-            ].astype(F32)
     count = hidden // PEERS
     labels = grad_three.shape[1]
-    for ref, start, side in ((own_ref, ONE_ROWS, core), (other_ref, 0, 1 - core)):
+    for ref, side in ((own_ref, core), (other_ref, 1 - core)):
         for peer in range(PEERS):
-            late = ref[peer, pl.ds(start, LATE_ROWS), :].astype(F32)
+            cells = ref[peer].astype(F32)
+            if ref is own_ref:
+                line, tile = divmod(peer, tiles)
+                layer, line = divmod(line * SUB, cut_rows)
+                grad_one[layer, pl.ds(line, SUB), pl.ds(tile * LANES, LANES)] = cells[:SUB]
             for tile in range(tiles):
-                grad_two[side, pl.ds(peer * count, count), pl.ds(tile * LANES, LANES)] = late[
-                    tile * count : (tile + 1) * count
+                grad_two[side, pl.ds(peer * count, count), pl.ds(tile * LANES, LANES)] = cells[
+                    SUB + tile * count : SUB + (tile + 1) * count
                 ]
-            top[side, pl.ds(peer * count, count), :] = late[TWO_ROWS:]
+            top[side, pl.ds(peer * count, count), :] = cells[SUB + TWO_ROWS :]
     for side in (0, 1):
         flipped = top[side].T
         grad_three[side] = flipped[:labels]
@@ -376,19 +392,21 @@
     chips = lax.axis_size(CHIPS)
     cap = self_one.shape[0] // (2 * chips)
     owner = lax.axis_index(DP) * lax.axis_size(CUTS) + lax.axis_index(CUTS)
-    place = jnp.stack([lax.axis_index("core"), owner, lax.axis_index(CHIPS)]).astype(jnp.int32)
+    place = jnp.stack([lax.axis_index("core"), owner]).astype(jnp.int32)
     other_table = swap_core(feat_table)
-    rows = gather_rows(place, feat_table, other_table, w_one.reshape(-1, hidden), self_one, near_one, chips)
+    w_own = exchange(jnp.broadcast_to(w_one.reshape(1, -1, hidden), (chips, 2 * cut_rows, hidden)), CHIPS)
+    rows = gather_rows(place, feat_table, other_table, self_one, near_one, chips)
+    w_own, rows = lax.optimization_barrier((w_own, rows))
+    w_other = swap_core(w_own)
     rows = exchange(rows, CHIPS)
-    w_other = swap_core(rows[:, 2 * cap :])
     keep, send = owner_pass(
-        place, seed_count, rows, w_other, bias_one, self_two, near_two, self_three, near_three,
+        place, seed_count, rows, w_own, w_other, bias_one, self_two, near_two, self_three, near_three,
         targets, w_two, bias_two, w_three, bias_three, cap,
     )
     parts = (keep.astype(F32) + swap_core(send).astype(F32)).astype(BF16)
     sums = sum_parts(exchange(parts, SAME_CORE))
     own = exchange(sums, SAME_CORE)
-    other = swap_core(own[:, ONE_ROWS:])
+    other = swap_core(own)
     grad_one, bias_one, grad_two, bias_two, grad_three, bias_three = unpack(
         place, own, other, cut_rows, hidden, labels
     )

time: 142 us -> 118 us (0.83)
  blocking collectives: 91.8 us -> 70.4 us
  starting transfers between devices: 6.84 us -> 12.9 us
  waiting for transfers between devices: 10.2 us -> 5.35 us
  local copies, waits for them, and re-layouts: 5.67 us -> 2.24 us
    all_to_all x3, blocking collectives: 91.8 us -> 70.4 us  [exchange(): return lax.all_to_all(values, axes, 0, 0, tiled=True)]
    all_to_all x0 -> x1, starting transfers between devices: none -> 6.13 us  [exchange(): return lax.all_to_all(values, axes, 0, 0, tiled=True)]
    ppermute x4, waiting for transfers between devices: 10.2 us -> 5.35 us  [swap_core(): return lax.ppermute(values, 'core', [(0, 1), (1, 0)])]
    unnamed x32 -> x28, local copies, waits for them, and re-layouts: 4.59 us -> 0.08 us
    broadcast_in_dim x0 -> x1, local copies, waits for them, and re-layouts: none -> 2.11 us  [local(): jnp.broadcast_to(w_one.reshape(1, -1, hidden), (chips, 2 * cut_rows, hidd...]
  transfers between devices with their start and end apart: 4 -> 5, of which waited for: 4 -> 2; matrix products, arithmetic and copies ran while one was open for 1% -> 2% of each run, Pallas kernels for 0% -> 13%
where the time goes in v3:
time: 118 us
  blocking collectives  70.4 us (60%)
  Pallas kernels  25.8 us (22%)
  starting transfers between devices  12.9 us (11%)
  waiting for transfers between devices  5.35 us (5%)
  local copies, waits for them, and re-layouts  2.24 us (2%)
    all_to_all x3, blocking collectives, exchange(): return lax.all_to_all(values, axes, 0, 0, tiled=True)  70.4 us
    pallas_call x1, Pallas kernels, gather_rows(): pl.pallas_call(gather_kernel, out_shape=jax.ShapeDtypeStruct((chips, 2 *...  15.9 us
    pallas_call x1, Pallas kernels, owner_pass(): pl.pallas_call(owner_kernel, out_shape=(chunk, chunk), in_specs=[pl.Block...  7.17 us
    ppermute x4, starting transfers between devices, swap_core(): return lax.ppermute(values, 'core', [(0, 1), (1, 0)])  6.75 us
    all_to_all x1, starting transfers between devices, exchange(): return lax.all_to_all(values, axes, 0, 0, tiled=True)  6.13 us
    ppermute x4, waiting for transfers between devices, swap_core(): return lax.ppermute(values, 'core', [(0, 1), (1, 0)])  5.35 us
    pallas_call x1, Pallas kernels, unpack(): pl.pallas_call(unpack_kernel, out_shape=(jax.ShapeDtypeStruct((2, cut_row...  2.37 us
  transfers between devices with their start and end apart: 5, of which 2 were waited for; matrix products, arithmetic and copies ran while one was open for 2% of the time, Pallas kernels for 13%

profile of v3, /device:TPU:1, one launch (start us, length us, event | category | flops | bytes accessed | tf_op | source)
XLA Modules:
  0.0 118.1 jit_solution(2120268965418966916)
XLA Ops:
  0.6 0.0 copy-start.13
  0.6 1.5 %collective-permute-start = (bf16[64,16384]{1,0:T(8,128)(2,1)}, bf16[64,16384]{1,0:T(8,128)(2,1)}, u32[]{:S(2)}, u32[]{:S(2)}) collective-permute-start(bf16[64,16384]{1,0:T(8,128)(2,1)} %own_ref.1), channel_id=1, source_target_pairs={{0,1},{1,0},{2,3},{3,2},{4,5},{5,4},{6,7},{7,6},{8,9},{9,8},{10,11... | collective-permute-start | bytes 6291464 | tf_op jit(solution)/shard_map/ppermute | solution.py:370
  2.1 0.0 copy-start
  2.1 0.0 copy-start.1
  2.1 2.1 %broadcast_in_dim.8 = bf16[8,128,512]{2,1,0:T(8,128)(2,1)} broadcast(bf16[128,512]{1,0:T(8,128)(2,1)} %bitcast.19), dimensions={1,2} | broadcast | bytes 1179648 | tf_op jit(solution)/shard_map/broadcast_in_dim | solution.py:397
  4.3 6.1 %all-to-all-start = ((bf16[8,128,512]{2,1,0:T(8,128)(2,1)}), bf16[8,128,512]{2,1,0:T(8,128)(2,1)}, u32[]{:S(2)}, u32[]{:S(2)}) async-start(bf16[8,128,512]{2,1,0:T(8,128)(2,1)} %broadcast_in_dim.8), calls=%async_computation | async-start | bytes 2097152 | tf_op jit(solution)/shard_map/all_to_all | solution.py:366
  10.4 0.0 copy-done.13
  10.5 0.1 pad_add_fusion.place_ref
  10.5 0.0 collective-permute-done.other_ref
  10.5 0.0 copy-done
  10.5 0.0 copy-done.1
  10.6 15.9 %gather_rows.1 = bf16[8,512,128]{2,1,0:T(8,128)(2,1)S(1)} custom-call(s32[2]{0:T(128)S(1)} %pad_add_fusion.place_ref, bf16[64,16384]{1,0:T(8,128)(2,1)S(1)} %copy-done, bf16[64,16384]{1,0:T(8,128)(2,1)} %collective-permute-done.other_ref, s32[4096]{0:T(1024)S(1)} %copy-done.1, s32[20480]{0:T(1024)S(1)} %reshape.41.near_ref), custom_call_target="tpu_custom_call" | custom-call | flops 134217728 | bytes 41943040 | tf_op jit(solution)/shard_map/gather_rows/pallas_call | solution.py:126
  26.5 0.0 copy-start.2
  26.5 0.0 copy-start.3
  26.5 0.0 copy-start.4
  26.5 0.0 copy-start.5
  26.5 0.0 copy-start.6
  26.6 0.0 copy-start.7
  26.6 0.0 copy-start.8
  26.6 0.0 copy-start.9
  26.6 0.0 copy-start.10
  26.6 0.0 copy-start.11
  26.6 0.0 copy-start.12
  26.6 0.0 all-to-all-done.w_own_ref
  26.6 0.5 collective-permute-start.1
  27.2 20.4 %all_to_all.20.rows_ref = bf16[8,512,128]{2,1,0:T(8,128)(2,1)S(1)} all-to-all(bf16[8,512,128]{2,1,0:T(8,128)(2,1)S(1)} %gather_rows.1), channel_id=1, replica_groups=mesh['y_hi'=2,'x'=4,'z'=4,'y_lo'=2,'core'=2] {'z','y_lo'}, dimensions={0} | all-to-all | bytes 2097152 | tf_op jit(solution)/shard_map/all_to_all | solution.py:366
  47.6 0.0 collective-permute-done.1.w_other_ref
  47.6 0.0 copy-done.2
  47.6 0.0 copy-done.3
  47.6 0.0 copy-done.4
  47.6 0.0 copy-done.5
  47.6 0.0 copy-done.6
  47.7 0.0 copy-done.7
  47.7 0.0 copy-done.8
  47.7 0.0 copy-done.9
  47.7 0.0 copy-done.10
  47.7 0.0 copy-done.11
  47.7 0.0 copy-done.12
  47.7 7.2 %owner_pass.1 = (bf16[64,104,128]{2,1,0:T(8,128)(2,1)S(1)}, bf16[64,104,128]{2,1,0:T(8,128)(2,1)}) custom-call(s32[2]{0:T(128)S(1)} %pad_add_fusion.place_ref, s32[128]{0:T(128)S(1)} %copy-done.9, bf16[8,512,128]{2,1,0:T(8,128)(2,1)S(1)} %all_to_all.20.rows_ref, bf16[8,128,512]{2,1,0:T(8,128)(2,1)} %all-to-all-done.w_own_ref, ...), custom_call_target="tpu_custom_call" | custom-call | flops 2147483648 | bytes 10485760 | tf_op jit(solution)/shard_map/owner_pass/pallas_call | solution.py:276
  54.9 1.3 %collective-permute-start.2 = (bf16[64,104,128]{2,1,0:T(8,128)(2,1)}, bf16[64,104,128]{2,1,0:T(8,128)(2,1)S(1)}, u32[]{:S(2)}, u32[]{:S(2)}) collective-permute-start(bf16[64,104,128]{2,1,0:T(8,128)(2,1)} %get-tuple-element.19), channel_id=1, source_target_pairs={{0,1},{1,0},{2,3},{3,2},{4,5},{5,4},{6,7},{7,6},{8,9},{9,8},{10,11... | collective-permute-start | bytes 5111816 | tf_op jit(solution)/shard_map/ppermute | solution.py:370
  56.2 3.4 %collective-permute-done.2 = bf16[64,104,128]{2,1,0:T(8,128)(2,1)S(1)} collective-permute-done((bf16[64,104,128]{2,1,0:T(8,128)(2,1)}, bf16[64,104,128]{2,1,0:T(8,128)(2,1)S(1)}, u32[]{:S(2)}, u32[]{:S(2)}) %collective-permute-start.2) | collective-permute-done | bytes 1703968 | tf_op jit(solution)/shard_map/ppermute | solution.py:370
  59.6 0.4 add_convert_fusion
  60.0 31.3 %all_to_all.21.parts_ref = bf16[64,104,128]{2,1,0:T(8,128)(2,1)S(1)} all-to-all(bf16[64,104,128]{2,1,0:T(8,128)(2,1)S(1)} %add_convert_fusion), channel_id=1, replica_groups=mesh['y_hi'=2,'x'=4,'z'=4,'y_lo'=2,'core'=2] {'y_hi','x','z','y_lo'}, dimensions={0} | all-to-all | bytes 3407872 | tf_op jit(solution)/shard_map/all_to_all | solution.py:366
  91.3 0.3 sum_parts.1
  91.6 18.8 %all_to_all.22.own_ref = bf16[64,48,128]{2,1,0:T(8,128)(2,1)S(1)} all-to-all(bf16[64,48,128]{2,1,0:T(8,128)(2,1)S(1)} %sum_parts.1), channel_id=1, replica_groups=mesh['y_hi'=2,'x'=4,'z'=4,'y_lo'=2,'core'=2] {'y_hi','x','z','y_lo'}, dimensions={0} | all-to-all | bytes 1572864 | tf_op jit(solution)/shard_map/all_to_all | solution.py:366
  110.4 3.4 %collective-permute-start.3 = (bf16[64,48,128]{2,1,0:T(8,128)(2,1)S(1)}, bf16[64,48,128]{2,1,0:T(8,128)(2,1)S(1)}, u32[]{:S(2)}, u32[]{:S(2)}) collective-permute-start(bf16[64,48,128]{2,1,0:T(8,128)(2,1)S(1)} %all_to_all.22.own_ref), channel_id=1, source_target_pairs={{0,1},{1,0},{2,3},{3,2},{4,5},{5,4},{6,7},{7,6},{8,9},{9,8},{10,11... | collective-permute-start | bytes 2359304 | tf_op jit(solution)/shard_map/ppermute | solution.py:370
  113.8 1.9 %collective-permute-done.3.other_ref = bf16[64,48,128]{2,1,0:T(8,128)(2,1)S(1)} collective-permute-done((bf16[64,48,128]{2,1,0:T(8,128)(2,1)S(1)}, bf16[64,48,128]{2,1,0:T(8,128)(2,1)S(1)}, u32[]{:S(2)}, u32[]{:S(2)}) %collective-permute-start.3) | collective-permute-done | bytes 786464 | tf_op jit(solution)/shard_map/ppermute | solution.py:370
  115.7 2.4 %unpack.1 = (f32[2,64,512]{2,1,0:T(8,128)}, f32[1,512]{1,0:T(1,128)}, f32[2,512,512]{2,1,0:T(8,128)}, f32[1,512]{1,0:T(1,128)}, f32[2,112,512]{2,1,0:T(8,128)}, /*index=5*/f32[1,112]{1,0:T(1,128)}) custom-call(s32[2]{0:T(128)S(1)} %pad_add_fusion.place_ref, bf16[64,48,128]{2,1,0:T(8,128)(2,1)S(1)} %all_to_all.22.own_ref, ...), custom_call_target="tpu_custom_call" | custom-call | tf_op jit(solution)/shard_map/unpack/pallas_call | solution.py:347
  (1 shorter events, 0.0 us)
Async XLA Ops:
  0.6 9.8 %copy-start.13 = (s32[5,4096]{1,0:T(8,128)S(1)}, s32[5,4096]{1,0:T(8,128)}, u32[]{:S(2)}) copy-start(s32[5,4096]{1,0:T(8,128)} %param.17) | copy-start | bytes 245764
  0.6 9.9 %collective-permute-start = (bf16[64,16384]{1,0:T(8,128)(2,1)}, bf16[64,16384]{1,0:T(8,128)(2,1)}, u32[]{:S(2)}, u32[]{:S(2)}) collective-permute-start(bf16[64,16384]{1,0:T(8,128)(2,1)} %own_ref.1), channel_id=1, source_target_pairs={{0,1},{1,0},{2,3},{3,2},{4,5},{5,4},{6,7},{7,6},{8,9},{9,8},{10,11... | collective-permute-start | bytes 6291464 | tf_op jit(solution)/shard_map/ppermute | solution.py:370
  2.1 8.4 %copy-start = (bf16[64,16384]{1,0:T(8,128)(2,1)S(1)}, bf16[64,16384]{1,0:T(8,128)(2,1)}, u32[]{:S(2)}) copy-start(bf16[64,16384]{1,0:T(8,128)(2,1)} %own_ref.1) | copy-start | bytes 6291460
  2.1 8.4 %copy-start.1 = (s32[4096]{0:T(1024)S(1)}, s32[4096]{0:T(1024)}, u32[]{:S(2)}) copy-start(s32[4096]{0:T(1024)} %self_ref.1) | copy-start | bytes 49156
  4.3 22.4 %all-to-all-start = ((bf16[8,128,512]{2,1,0:T(8,128)(2,1)}), bf16[8,128,512]{2,1,0:T(8,128)(2,1)}, u32[]{:S(2)}, u32[]{:S(2)}) async-start(bf16[8,128,512]{2,1,0:T(8,128)(2,1)} %broadcast_in_dim.8), calls=%async_computation | async-start | bytes 2097152 | tf_op jit(solution)/shard_map/all_to_all | solution.py:366
  26.5 21.1 %copy-start.2 = (bf16[2,512,512]{2,1,0:T(8,128)(2,1)S(1)}, bf16[2,512,512]{2,1,0:T(8,128)(2,1)}, u32[]{:S(2)}) copy-start(bf16[2,512,512]{2,1,0:T(8,128)(2,1)} %w_two_ref.1) | copy-start | bytes 3145732
  26.5 21.1 %copy-start.3 = (bf16[2,512,112]{1,2,0:T(8,128)(2,1)S(1)}, bf16[2,512,112]{1,2,0:T(8,128)(2,1)}, u32[]{:S(2)}) copy-start(bf16[2,512,112]{1,2,0:T(8,128)(2,1)} %param.28) | copy-start | bytes 688132
  26.5 21.1 %copy-start.4 = (s32[32,112]{1,0:T(8,128)S(1)}, s32[32,112]{1,0:T(8,128)}, u32[]{:S(2)}) copy-start(s32[32,112]{1,0:T(8,128)} %targets_ref.1) | copy-start | bytes 43012
  26.5 21.1 %copy-start.5 = (s32[10,128]{1,0:T(8,128)S(1)}, s32[10,128]{1,0:T(8,128)}, u32[]{:S(2)}) copy-start(s32[10,128]{1,0:T(8,128)} %near_two_ref.1) | copy-start | bytes 15364
  26.5 21.1 %copy-start.6 = (s32[15,32]{1,0:T(8,128)S(1)}, s32[15,32]{1,0:T(8,128)}, u32[]{:S(2)}) copy-start(s32[15,32]{1,0:T(8,128)} %near_three_ref.1) | copy-start | bytes 5764
  26.6 21.1 %copy-start.7 = (f32[512]{0:T(512)S(1)}, f32[512]{0:T(512)}, u32[]{:S(2)}) copy-start(f32[512]{0:T(512)} %param.25) | copy-start | bytes 6148
  26.6 21.1 %copy-start.8 = (f32[512]{0:T(512)S(1)}, f32[512]{0:T(512)}, u32[]{:S(2)}) copy-start(f32[512]{0:T(512)} %param.27) | copy-start | bytes 6148
  26.6 21.1 %copy-start.9 = (s32[128]{0:T(128)S(1)}, s32[128]{0:T(128)}, u32[]{:S(2)}) copy-start(s32[128]{0:T(128)} %count_ref.1) | copy-start | bytes 1540
  26.6 21.1 %copy-start.10 = (s32[128]{0:T(128)S(1)}, s32[128]{0:T(128)}, u32[]{:S(2)}) copy-start(s32[128]{0:T(128)} %param.18) | copy-start | bytes 1540
  26.6 21.1 %copy-start.11 = (s32[32]{0:T(128)S(1)}, s32[32]{0:T(128)}, u32[]{:S(2)}) copy-start(s32[32]{0:T(128)} %param.20) | copy-start | bytes 388
  26.6 21.1 %copy-start.12 = (f32[112]{0:T(128)S(1)}, f32[112]{0:T(128)}, u32[]{:S(2)}) copy-start(f32[112]{0:T(128)} %param.29) | copy-start | bytes 1348
  26.6 21.0 %collective-permute-start.1 = (bf16[8,128,512]{2,1,0:T(8,128)(2,1)}, bf16[8,128,512]{2,1,0:T(8,128)(2,1)S(1)}, u32[]{:S(2)}, u32[]{:S(2)}) collective-permute-start(bf16[8,128,512]{2,1,0:T(8,128)(2,1)} %all-to-all-done.w_own_ref), channel_id=1, source_target_pairs={{0,1},{1,0},{2,3},{3,2},{4,5},{5,4},{6,7},{7,6},{8,9},{9,8},{10,11... | collective-permute-start | bytes 3145736 | tf_op jit(solution)/shard_map/ppermute | solution.py:370
  54.9 4.7 %collective-permute-start.2 = (bf16[64,104,128]{2,1,0:T(8,128)(2,1)}, bf16[64,104,128]{2,1,0:T(8,128)(2,1)S(1)}, u32[]{:S(2)}, u32[]{:S(2)}) collective-permute-start(bf16[64,104,128]{2,1,0:T(8,128)(2,1)} %get-tuple-element.19), channel_id=1, source_target_pairs={{0,1},{1,0},{2,3},{3,2},{4,5},{5,4},{6,7},{7,6},{8,9},{9,8},{10,11... | collective-permute-start | bytes 5111816 | tf_op jit(solution)/shard_map/ppermute | solution.py:370
  110.4 5.3 %collective-permute-start.3 = (bf16[64,48,128]{2,1,0:T(8,128)(2,1)S(1)}, bf16[64,48,128]{2,1,0:T(8,128)(2,1)S(1)}, u32[]{:S(2)}, u32[]{:S(2)}) collective-permute-start(bf16[64,48,128]{2,1,0:T(8,128)(2,1)S(1)} %all_to_all.22.own_ref), channel_id=1, source_target_pairs={{0,1},{1,0},{2,3},{3,2},{4,5},{5,4},{6,7},{7,6},{8,9},{9,8},{10,11... | collective-permute-start | bytes 2359304 | tf_op jit(solution)/shard_map/ppermute | solution.py:370

commit v4 on v3

--- a/solution.py
+++ b/solution.py
@@ -12,7 +12,7 @@
 
 LANES = 128
 SUB = 8
-GATHER_UNROLL = 16
+GATHER_UNROLL = 32
 TABLE_PIECES = 8
 ONE_ROWS = 64
 TWO_ROWS = 32
@@ -92,8 +92,7 @@
         @pl.loop(0, width // LANES, unroll=4)
         def _(block):
             spot = pl.ds(pl.multiple_of(piece * width + block * LANES, LANES), LANES)
-            part = jnp.concatenate([own[:, spot], other[:, spot]], axis=0).astype(F32)
-            table[spot, :] = part.T
+            table[spot, :] = jnp.concatenate([own[:, spot], other[:, spot]], axis=0).T.astype(F32)
 
     for fetch in id_fetches:
         fetch.wait()
@@ -104,14 +103,15 @@
 
         @pl.loop(0, cap // GATHER_UNROLL)
         def _(group):
+            start = group * GATHER_UNROLL
+            mine = self_ids.at[pl.ds(first + start, GATHER_UNROLL)]
+            others = [near_ids.at[pl.ds(offset * targets + first + start, GATHER_UNROLL)] for offset in range(fan)]
             for step in range(GATHER_UNROLL):
-                line = group * GATHER_UNROLL + step
-                spot = first + line
-                total = table[pl.ds(near_ids[spot], 1), :]
-                for offset in range(1, fan):
-                    total = total + table[pl.ds(near_ids[offset * targets + spot], 1), :]
-                rows[pl.ds(line, 1), :] = table[pl.ds(self_ids[spot], 1), :]
-                rows[pl.ds(cap + line, 1), :] = total
+                total = table[pl.ds(others[0][step], 1), :]
+                for ids in others[1:]:
+                    total = total + table[pl.ds(ids[step], 1), :]
+                rows[pl.ds(start + step, 1), :] = table[pl.ds(mine[step], 1), :]
+                rows[pl.ds(cap + start + step, 1), :] = total
 
         out_ref[chip, pl.ds(0, cap), :] = rows[pl.ds(0, cap), :].astype(BF16)
         out_ref[chip, pl.ds(cap, cap), :] = (rows[pl.ds(cap, cap), :] / fan).astype(BF16)
@@ -138,15 +138,35 @@
             pltpu.SemaphoreType.DMA((2, TABLE_PIECES)),
             pltpu.SemaphoreType.DMA((2,)),
         ],
-        compiler_params=pltpu.CompilerParams(vmem_limit_bytes=48 << 20),
+        compiler_params=pltpu.CompilerParams(vmem_limit_bytes=24 << 20),
         cost_estimate=pl.CostEstimate(flops=1 << 27, bytes_accessed=40 << 20, transcendentals=0),
         name="gather_rows",
     )(place, own_table, other_table, self_one, near_one)
 
 
+def spread_kernel(part_ref, out_ref, sems):
+    copies = [pltpu.make_async_copy(part_ref, out_ref.at[chip], sems.at[chip]) for chip in range(out_ref.shape[0])]
+    for copy in copies:
+        copy.start()
+    for copy in copies:
+        copy.wait()
+
+
+def spread(part, chips):
+    return pl.pallas_call(
+        spread_kernel,
+        out_shape=jax.ShapeDtypeStruct((chips,) + part.shape, part.dtype),
+        in_specs=vmem(1),
+        out_specs=pl.BlockSpec(memory_space=pl.ANY),
+        scratch_shapes=[pltpu.SemaphoreType.DMA((chips,))],
+        name="spread",
+    )(part)
+
+
 def owner_kernel(
     place_ref,
     count_ref,
+    counts_ref,
     rows_ref,
     w_own_ref,
     w_other_ref,
@@ -160,11 +180,14 @@
     bias_two_ref,
     w_three_ref,
     bias_three_ref,
-    keep_ref,
     send_ref,
-    pre_one,
+    one_ref,
+    two_ref,
     mids,
     tops,
+    logit_ref,
+    biases_ref,
+    pre_one,
 ):
     core = place_ref[0]
     owner = place_ref[1]
@@ -211,8 +234,7 @@
     tops[1] = near_top
     logits = back_dot(self_top, w_three_ref[0]) + back_dot(near_top, w_three_ref[1]) + bias_three_ref[...]
 
-    live_total = lax.fori_loop(0, count_ref.shape[0], lambda i, t: t + count_ref[i], jnp.int32(0))
-    scale = 1.0 / jnp.sqrt(jnp.full((1, labels), live_total, jnp.int32).astype(F32))
+    scale = 1.0 / jnp.sqrt(jnp.sum(counts_ref[...].astype(F32), axis=1, keepdims=True))
     live = lax.broadcasted_iota(jnp.int32, (seeds, labels), 0) < count_ref[owner]
     slope = jax.nn.sigmoid(logits) - targets_ref[...].astype(F32)
     logit_grad = jnp.where(live, slope * scale, 0.0).astype(BF16)
@@ -231,7 +253,7 @@
 
     wide_logit = jnp.concatenate([logit_grad, jnp.zeros((seeds, LANES - labels), BF16)], axis=1)
     bias_three = jnp.sum(wide_logit.astype(F32), axis=0, keepdims=True)
-    biases = jnp.concatenate(
+    biases_ref[...] = jnp.concatenate(
         [
             jnp.sum(pre_grad_one.astype(F32), axis=0, keepdims=True),
             jnp.sum(pre_grad_two.astype(F32), axis=0, keepdims=True),
@@ -240,54 +262,80 @@
         ],
         axis=0,
     )
+    one_ref[...] = pre_grad_one
+    two_ref[...] = pre_grad_two
+    logit_ref[...] = wide_logit
+    write_products(send_ref, 1, 1 - core, rows_ref, one_ref, two_ref, mids, tops, logit_ref, biases_ref)
+
+
+def write_products(out_ref, half, side, rows_ref, one_ref, two_ref, mids, tops, logit_ref, biases_ref):
+    chips = rows_ref.shape[0]
+    cap, hidden = one_ref.shape
+    labels = LANES - biases_ref.shape[0]
+    tiles = hidden // LANES
+    width = LANES // 2
     count = hidden // PEERS
-
     for pair in range(chips // 2):
-        sides = []
+        cells = []
         for chip in (2 * pair, 2 * pair + 1):
-            blocks = [lead_dot(rows_ref[chip, pl.ds(line * cap, cap), :], pre_grad_one) for line in (0, 1)]
-            sides.append(
-                [jnp.concatenate([block[start : start + half] for block in blocks], axis=0) for start in (0, half)]
-            )
-        for out_ref, side in ((keep_ref, 0), (send_ref, 1)):
-            for peer in range(PEERS):
-                line, tile = divmod(peer, tiles)
-                cell = [
-                    both[side][line * SUB : (line + 1) * SUB, tile * LANES : (tile + 1) * LANES] for both in sides
-                ]
-                out_ref[peer, pl.ds(pair * 2 * SUB, 2 * SUB), :] = jnp.concatenate(cell, axis=0).astype(BF16)
-    for out_ref, side in ((send_ref, 1 - core), (keep_ref, core)):
-        two = lead_dot(mids[side], pre_grad_two)
-        top = lead_dot(wide_logit, tops[side])
-        top = jnp.concatenate([top[:labels], biases * (side == 0).astype(F32)], axis=0).T
+            blocks = [lead_dot(rows_ref[chip, pl.ds(line * cap, cap), :], one_ref[...]) for line in (0, 1)]
+            cells.append(jnp.concatenate([block[half * width : (half + 1) * width] for block in blocks], axis=0))
         for peer in range(PEERS):
-            late = [
-                two[peer * count : (peer + 1) * count, tile * LANES : (tile + 1) * LANES]
-                for tile in range(tiles)
-            ]
-            late.append(top[peer * count : (peer + 1) * count, :])
-            out_ref[peer, pl.ds(ONE_ROWS, LATE_ROWS), :] = jnp.concatenate(late, axis=0).astype(BF16)
+            line, tile = divmod(peer, tiles)
+            cell = [both[line * SUB : (line + 1) * SUB, tile * LANES : (tile + 1) * LANES] for both in cells]
+            out_ref[peer, pl.ds(pair * 2 * SUB, 2 * SUB), :] = jnp.concatenate(cell, axis=0).astype(BF16)
+    two = lead_dot(mids[side], two_ref[...])
+    top = lead_dot(logit_ref[...], tops[side])
+    top = jnp.concatenate([top[:labels], biases_ref[...]], axis=0).T
+    for peer in range(PEERS):
+        late = [
+            two[peer * count : (peer + 1) * count, tile * LANES : (tile + 1) * LANES] for tile in range(tiles)
+        ]
+        late.append(top[peer * count : (peer + 1) * count, :])
+        out_ref[peer, pl.ds(ONE_ROWS, LATE_ROWS), :] = jnp.concatenate(late, axis=0).astype(BF16)
+
+
+def keep_kernel(place_ref, rows_ref, one_ref, two_ref, mids, tops, logit_ref, biases_ref, keep_ref):
+    write_products(keep_ref, 0, place_ref[0], rows_ref, one_ref, two_ref, mids, tops, logit_ref, biases_ref)
+
+
+def keep_products(place, rows, grads):
+    return pl.pallas_call(
+        keep_kernel,
+        out_shape=jax.ShapeDtypeStruct((PEERS, CHUNK_ROWS, LANES), BF16),
+        in_specs=[pl.BlockSpec(memory_space=SMEM)] + vmem(1 + len(grads)),
+        out_specs=pl.BlockSpec(memory_space=VMEM),
+        compiler_params=pltpu.CompilerParams(vmem_limit_bytes=24 << 20),
+        cost_estimate=pl.CostEstimate(flops=1 << 30, bytes_accessed=8 << 20, transcendentals=0),
+        name="keep_products",
+    )(place, rows, *grads)
 
 
 def owner_pass(place, seed_count, rows, w_own, w_other, bias_one, self_two, near_two, self_three, near_three,
                targets, w_two, bias_two, w_three, bias_three, cap):
     hidden = w_two.shape[2]
-    chunk = jax.ShapeDtypeStruct((PEERS, CHUNK_ROWS, LANES), BF16)
+    labels = w_three.shape[2]
+    mid_rows = self_two.shape[0]
+    seeds = self_three.shape[0]
     return pl.pallas_call(
         owner_kernel,
-        out_shape=(chunk, chunk),
-        in_specs=[pl.BlockSpec(memory_space=SMEM)] * 2 + vmem(13),
-        out_specs=tuple(vmem(2)),
-        scratch_shapes=[
-            VMEM((cap, hidden), F32),
-            VMEM((2, near_two.shape[1], hidden), BF16),
-            VMEM((2, near_three.shape[1], hidden), BF16),
-        ],
-        compiler_params=pltpu.CompilerParams(vmem_limit_bytes=48 << 20),
+        out_shape=(
+            jax.ShapeDtypeStruct((PEERS, CHUNK_ROWS, LANES), BF16),
+            jax.ShapeDtypeStruct((cap, hidden), BF16),
+            jax.ShapeDtypeStruct((mid_rows, hidden), BF16),
+            jax.ShapeDtypeStruct((2, mid_rows, hidden), BF16),
+            jax.ShapeDtypeStruct((2, seeds, hidden), BF16),
+            jax.ShapeDtypeStruct((seeds, LANES), BF16),
+            jax.ShapeDtypeStruct((LANES - labels, hidden), F32),
+        ),
+        in_specs=[pl.BlockSpec(memory_space=SMEM)] * 2 + vmem(14),
+        out_specs=tuple(vmem(7)),
+        scratch_shapes=[VMEM((cap, hidden), F32)],
+        compiler_params=pltpu.CompilerParams(vmem_limit_bytes=24 << 20),
         cost_estimate=pl.CostEstimate(flops=1 << 31, bytes_accessed=10 << 20, transcendentals=1 << 19),
         name="owner_pass",
     )(
-        place, seed_count, rows, w_own, w_other, bias_one.reshape(1, -1), self_two.reshape(1, -1), near_two,
+        place, seed_count, seed_count.reshape(1, -1), rows, w_own, w_other, bias_one.reshape(1, -1), self_two.reshape(1, -1), near_two,
         self_three.reshape(1, -1), near_three, targets, w_two, bias_two.reshape(1, -1),
         jnp.transpose(w_three, (0, 2, 1)), bias_three.reshape(1, -1),
     )
@@ -311,55 +359,134 @@
         out_shape=jax.ShapeDtypeStruct((PEERS, SUB + LATE_ROWS, LANES), BF16),
         in_specs=vmem(1),
         out_specs=pl.BlockSpec(memory_space=VMEM),
-        compiler_params=pltpu.CompilerParams(vmem_limit_bytes=48 << 20),
+        compiler_params=pltpu.CompilerParams(vmem_limit_bytes=24 << 20),
         name="sum_parts",
     )(parts)
 
 
-def unpack_kernel(place_ref, own_ref, other_ref, grad_one, bias_one, grad_two, bias_two, grad_three, bias_three, top):
-    core = place_ref[0]
-    cut_rows, hidden = grad_one.shape[1:]
+def write_late(ref, side, grad_two, grad_three, two, top, three, sems):
+    hidden = two.shape[0]
+    labels = three.shape[0]
+    count = hidden // PEERS
+    pieces = sems.shape[0] - 1
+    step = hidden // pieces
+    copies = []
+    for peer in range(PEERS):
+        cells = ref[peer].astype(F32)
+        for tile in range(hidden // LANES):
+            two[pl.ds(peer * count, count), pl.ds(tile * LANES, LANES)] = cells[
+                SUB + tile * count : SUB + (tile + 1) * count
+            ]
+        top[pl.ds(peer * count, count), :] = cells[SUB + TWO_ROWS :]
+        done = (peer + 1) * count
+        if done % step == 0:
+            spot = pl.ds(done - step, step)
+            copies.append(pltpu.make_async_copy(two.at[spot], grad_two.at[side, spot], sems.at[len(copies)]))
+            copies[-1].start()
+    flipped = top[...].T
+    three[...] = flipped[:labels]
+    copies.append(pltpu.make_async_copy(three, grad_three.at[side], sems.at[pieces]))
+    copies[-1].start()
+    return flipped[labels:], copies
+
+
+def own_kernel(
+    place_ref,
+    own_ref,
+    grad_one,
+    grad_two,
+    grad_three,
+    bias_one,
+    bias_two,
+    bias_three,
+    one,
+    two,
+    top,
+    three,
+    first,
+    second,
+    third,
+    sems,
+    late_sems,
+):
+    cut_rows, hidden = one.shape[1:]
     tiles = hidden // LANES
-    count = hidden // PEERS
-    labels = grad_three.shape[1]
-    for ref, side in ((own_ref, core), (other_ref, 1 - core)):
-        for peer in range(PEERS):
-            cells = ref[peer].astype(F32)
-            if ref is own_ref:
-                line, tile = divmod(peer, tiles)
-                layer, line = divmod(line * SUB, cut_rows)
-                grad_one[layer, pl.ds(line, SUB), pl.ds(tile * LANES, LANES)] = cells[:SUB]
-            for tile in range(tiles):
-                grad_two[side, pl.ds(peer * count, count), pl.ds(tile * LANES, LANES)] = cells[
-                    SUB + tile * count : SUB + (tile + 1) * count
-                ]
-            top[side, pl.ds(peer * count, count), :] = cells[SUB + TWO_ROWS :]
-    for side in (0, 1):
-        flipped = top[side].T
-        grad_three[side] = flipped[:labels]
-        if side == 0:
-            bias_one[...] = flipped[labels : labels + 1]
-            bias_two[...] = flipped[labels + 1 : labels + 2]
-            bias_three[...] = flipped[labels + 2 : labels + 3, :labels]
-
-
-def unpack(place, own, other, cut_rows, hidden, labels):
-    return pl.pallas_call(
-        unpack_kernel,
+    for peer in range(PEERS):
+        line, tile = divmod(peer, tiles)
+        layer, line = divmod(line * SUB, cut_rows)
+        one[layer, pl.ds(line, SUB), pl.ds(tile * LANES, LANES)] = own_ref[peer].astype(F32)[:SUB]
+    one_copy = pltpu.make_async_copy(one, grad_one, late_sems.at[0])
+    one_copy.start()
+    kept, copies = write_late(own_ref, place_ref[0], grad_two, grad_three, two, top, three, sems)
+    first[...] = kept[0:1]
+    second[...] = kept[1:2]
+    third[...] = kept[2:3, : three.shape[0]]
+    for slot, (held, out) in enumerate(((first, bias_one), (second, bias_two), (third, bias_three))):
+        copies.append(pltpu.make_async_copy(held, out, late_sems.at[1 + slot]))
+        copies[-1].start()
+    for copy in [one_copy] + copies:
+        copy.wait()
+
+
+def other_kernel(place_ref, other_ref, two_in, three_in, grad_two, grad_three, two, top, three, sems):
+    _, copies = write_late(other_ref, 1 - place_ref[0], grad_two, grad_three, two, top, three, sems)
+    for copy in copies:
+        copy.wait()
+
+
+def unpack_own(place, own, cut_rows, hidden, labels):
+    anywhere = pl.BlockSpec(memory_space=pl.ANY)
+    return pl.pallas_call(
+        own_kernel,
         out_shape=(
             jax.ShapeDtypeStruct((2, cut_rows, hidden), F32),
+            jax.ShapeDtypeStruct((2, hidden, hidden), F32),
+            jax.ShapeDtypeStruct((2, labels, hidden), F32),
             jax.ShapeDtypeStruct((1, hidden), F32),
-            jax.ShapeDtypeStruct((2, hidden, hidden), F32),
             jax.ShapeDtypeStruct((1, hidden), F32),
-            jax.ShapeDtypeStruct((2, labels, hidden), F32),
             jax.ShapeDtypeStruct((1, labels), F32),
         ),
-        in_specs=[pl.BlockSpec(memory_space=SMEM)] + vmem(2),
-        out_specs=tuple(vmem(6)),
-        scratch_shapes=[VMEM((2, hidden, LANES), F32)],
-        compiler_params=pltpu.CompilerParams(vmem_limit_bytes=48 << 20),
-        name="unpack",
-    )(place, own, other)
+        in_specs=[pl.BlockSpec(memory_space=SMEM)] + vmem(1),
+        out_specs=(anywhere,) * 6,
+        scratch_shapes=[
+            VMEM((2, cut_rows, hidden), F32),
+            VMEM((hidden, hidden), F32),
+            VMEM((hidden, LANES), F32),
+            VMEM((labels, hidden), F32),
+            VMEM((1, hidden), F32),
+            VMEM((1, hidden), F32),
+            VMEM((1, labels), F32),
+            pltpu.SemaphoreType.DMA((9,)),
+            pltpu.SemaphoreType.DMA((4,)),
+        ],
+        compiler_params=pltpu.CompilerParams(vmem_limit_bytes=16 << 20),
+        cost_estimate=pl.CostEstimate(flops=1 << 22, bytes_accessed=4 << 20, transcendentals=0),
+        name="unpack_own",
+    )(place, own)
+
+
+def unpack_other(place, other, grad_two, grad_three):
+    hidden = grad_two.shape[2]
+    labels = grad_three.shape[1]
+    anywhere = pl.BlockSpec(memory_space=pl.ANY)
+    return pl.pallas_call(
+        other_kernel,
+        out_shape=(
+            jax.ShapeDtypeStruct(grad_two.shape, F32),
+            jax.ShapeDtypeStruct(grad_three.shape, F32),
+        ),
+        in_specs=[pl.BlockSpec(memory_space=SMEM)] + vmem(1) + [anywhere] * 2,
+        out_specs=(anywhere, anywhere),
+        scratch_shapes=[
+            VMEM((hidden, hidden), F32),
+            VMEM((hidden, LANES), F32),
+            VMEM((labels, hidden), F32),
+            pltpu.SemaphoreType.DMA((9,)),
+        ],
+        input_output_aliases={2: 0, 3: 1},
+        compiler_params=pltpu.CompilerParams(vmem_limit_bytes=16 << 20),
+        name="unpack_other",
+    )(place, other, grad_two, grad_three)
 
 
 def exchange(values, axes):
@@ -394,22 +521,23 @@
     owner = lax.axis_index(DP) * lax.axis_size(CUTS) + lax.axis_index(CUTS)
     place = jnp.stack([lax.axis_index("core"), owner]).astype(jnp.int32)
     other_table = swap_core(feat_table)
-    w_own = exchange(jnp.broadcast_to(w_one.reshape(1, -1, hidden), (chips, 2 * cut_rows, hidden)), CHIPS)
+    w_own = exchange(spread(w_one.reshape(-1, hidden), chips), CHIPS)
     rows = gather_rows(place, feat_table, other_table, self_one, near_one, chips)
     w_own, rows = lax.optimization_barrier((w_own, rows))
     w_other = swap_core(w_own)
     rows = exchange(rows, CHIPS)
-    keep, send = owner_pass(
+    send, *grads = owner_pass(
         place, seed_count, rows, w_own, w_other, bias_one, self_two, near_two, self_three, near_three,
         targets, w_two, bias_two, w_three, bias_three, cap,
     )
-    parts = (keep.astype(F32) + swap_core(send).astype(F32)).astype(BF16)
+    other = swap_core(send)
+    keep = keep_products(place, rows, grads)
+    parts = (keep.astype(F32) + other.astype(F32)).astype(BF16)
     sums = sum_parts(exchange(parts, SAME_CORE))
     own = exchange(sums, SAME_CORE)
     other = swap_core(own)
-    grad_one, bias_one, grad_two, bias_two, grad_three, bias_three = unpack(
-        place, own, other, cut_rows, hidden, labels
-    )
+    grad_one, grad_two, grad_three, bias_one, bias_two, bias_three = unpack_own(place, own, cut_rows, hidden, labels)
+    grad_two, grad_three = unpack_other(place, other, grad_two, grad_three)
     return (
         grad_one,
         bias_one.reshape(-1),

time: 118 us -> 113 us (0.958)
  blocking collectives: 70.4 us -> 68.1 us
  local copies, waits for them, and re-layouts: 2.24 us -> 0.13 us
    ppermute x4, waiting for transfers between devices: 5.35 us -> 1.8 us  [swap_core(): return lax.ppermute(values, 'core', [(0, 1), (1, 0)])]
    pallas_call x1, Pallas kernels: 15.9 us -> 12.4 us  [gather_rows(): pl.pallas_call(gather_kernel, out_shape=jax.ShapeDtypeStruct((chips, 2 *...]
    all_to_all x1, waiting for transfers between devices: 0.01 us -> 2.96 us  [exchange(): return lax.all_to_all(values, axes, 0, 0, tiled=True)]
    pallas_call x2 -> x5, Pallas kernels: 9.54 us -> 12.2 us  [the longest x1 5.08 us: owner_pass(): pl.pallas_call(owner_kernel, out_shape=(jax.ShapeDtypeStruct((PEERS, CHUN...]
    all_to_all x3, blocking collectives: 70.4 us -> 68.1 us  [exchange(): return lax.all_to_all(values, axes, 0, 0, tiled=True)]
    broadcast_in_dim x1 -> x0, local copies, waits for them, and re-layouts: 2.11 us -> none  [local(): jnp.broadcast_to(w_one.reshape(1, -1, hidden), (chips, 2 * cut_rows, hidd...]
  transfers between devices with their start and end apart: 5 -> 5, of which waited for: 2 -> 3; matrix products, arithmetic and copies ran while one was open for 2% -> 0% of each run, Pallas kernels for 13% -> 16%
where the time goes in v4:
time: 113 us
  blocking collectives  68.1 us (60%)
  Pallas kernels  24.9 us (22%)
  starting transfers between devices  13.3 us (12%)
  waiting for transfers between devices  4.76 us (4%)
    all_to_all x3, blocking collectives, exchange(): return lax.all_to_all(values, axes, 0, 0, tiled=True)  68.1 us
    pallas_call x1, Pallas kernels, gather_rows(): pl.pallas_call(gather_kernel, out_shape=jax.ShapeDtypeStruct((chips, 2 *...  12.4 us
    ppermute x4, starting transfers between devices, swap_core(): return lax.ppermute(values, 'core', [(0, 1), (1, 0)])  7.17 us
    all_to_all x1, starting transfers between devices, exchange(): return lax.all_to_all(values, axes, 0, 0, tiled=True)  6.14 us
    pallas_call x1, Pallas kernels, owner_pass(): pl.pallas_call(owner_kernel, out_shape=(jax.ShapeDtypeStruct((PEERS, CHUN...  5.08 us
    all_to_all x1, waiting for transfers between devices, exchange(): return lax.all_to_all(values, axes, 0, 0, tiled=True)  2.96 us
  transfers between devices with their start and end apart: 5, of which 3 were waited for; matrix products, arithmetic and copies ran while one was open for 0% of the time, Pallas kernels for 16%

profile of v4, /device:TPU:1, one launch (start us, length us, event | category | flops | bytes accessed | tf_op | source)
XLA Modules:
  0.0 112.5 jit_solution(16969872523972496032)
XLA Ops:
  0.6 0.0 copy-start.13
  0.6 1.5 %collective-permute-start = (bf16[64,16384]{1,0:T(8,128)(2,1)}, bf16[64,16384]{1,0:T(8,128)(2,1)}, u32[]{:S(2)}, u32[]{:S(2)}) collective-permute-start(bf16[64,16384]{1,0:T(8,128)(2,1)} %own_ref.1), channel_id=1, source_target_pairs={{0,1},{1,0},{2,3},{3,2},{4,5},{5,4},{6,7},{7,6},{8,9},{9,8},{10,11... | collective-permute-start | bytes 6291464 | tf_op jit(solution)/shard_map/ppermute | solution.py:497
  2.1 0.0 copy-start
  2.1 0.0 copy-start.1
  2.1 2.1 %spread.1 = bf16[8,128,512]{2,1,0:T(8,128)(2,1)} custom-call(bf16[128,512]{1,0:T(8,128)(2,1)} %bitcast.22), custom_call_target="tpu_custom_call" | custom-call | tf_op jit(solution)/shard_map/spread/pallas_call | solution.py:156
  4.2 6.1 %all-to-all-start = ((bf16[8,128,512]{2,1,0:T(8,128)(2,1)}), bf16[8,128,512]{2,1,0:T(8,128)(2,1)}, u32[]{:S(2)}, u32[]{:S(2)}) async-start(bf16[8,128,512]{2,1,0:T(8,128)(2,1)} %spread.1), calls=%async_computation | async-start | bytes 2097152 | tf_op jit(solution)/shard_map/all_to_all | solution.py:493
  10.4 0.0 copy-done.13
  10.4 0.1 pad_add_fusion.place_ref
  10.5 0.0 collective-permute-done.other_ref
  10.5 0.0 copy-done
  10.5 0.0 copy-done.1
  10.5 12.4 %gather_rows.1 = bf16[8,512,128]{2,1,0:T(8,128)(2,1)S(1)} custom-call(s32[2]{0:T(128)S(1)} %pad_add_fusion.place_ref, bf16[64,16384]{1,0:T(8,128)(2,1)S(1)} %copy-done, bf16[64,16384]{1,0:T(8,128)(2,1)} %collective-permute-done.other_ref, s32[4096]{0:T(1024)S(1)} %copy-done.1, s32[20480]{0:T(1024)S(1)} %reshape.46.near_ref), custom_call_target="tpu_custom_call" | custom-call | flops 134217728 | bytes 41943040 | tf_op jit(solution)/shard_map/gather_rows/pallas_call | solution.py:126
  22.9 0.0 copy-start.2
  23.0 0.0 copy-start.3
  23.0 0.0 copy-start.4
  23.0 0.0 copy-start.5
  23.0 0.0 copy-start.6
  23.0 0.0 copy-start.7
  23.0 0.0 copy-start.8
  23.0 0.0 copy-start.9
  23.0 0.0 copy-start.10
  23.1 0.0 copy-start.11
  23.1 0.0 copy-start.12
  23.1 3.0 %all-to-all-done.w_own_ref = bf16[8,128,512]{2,1,0:T(8,128)(2,1)} async-done(((bf16[8,128,512]{2,1,0:T(8,128)(2,1)}), bf16[8,128,512]{2,1,0:T(8,128)(2,1)}, u32[]{:S(2)}, u32[]{:S(2)}) %all-to-all-start) | async-done | bytes 1048608 | tf_op jit(solution)/shard_map/all_to_all | solution.py:493
  26.0 1.1 %collective-permute-start.1 = (bf16[8,128,512]{2,1,0:T(8,128)(2,1)}, bf16[8,128,512]{2,1,0:T(8,128)(2,1)S(1)}, u32[]{:S(2)}, u32[]{:S(2)}) collective-permute-start(bf16[8,128,512]{2,1,0:T(8,128)(2,1)} %all-to-all-done.w_own_ref), channel_id=1, source_target_pairs={{0,1},{1,0},{2,3},{3,2},{4,5},{5,4},{6,7},{7,6},{8,9},{9,8},{10,11... | collective-permute-start | bytes 3145736 | tf_op jit(solution)/shard_map/ppermute | solution.py:497
  27.2 18.1 %all_to_all.20.rows_ref = bf16[8,512,128]{2,1,0:T(8,128)(2,1)S(1)} all-to-all(bf16[8,512,128]{2,1,0:T(8,128)(2,1)S(1)} %gather_rows.1), channel_id=1, replica_groups=mesh['y_hi'=2,'x'=4,'z'=4,'y_lo'=2,'core'=2] {'z','y_lo'}, dimensions={0} | all-to-all | bytes 2097152 | tf_op jit(solution)/shard_map/all_to_all | solution.py:493
  45.2 0.0 collective-permute-done.1.w_other_ref
  45.2 0.0 copy-done.2
  45.2 0.0 copy-done.3
  45.2 0.0 copy-done.4
  45.3 0.0 copy-done.5
  45.3 0.0 copy-done.6
  45.3 0.0 copy-done.7
  45.3 0.0 copy-done.8
  45.3 0.0 copy-done.9
  45.3 0.0 copy-done.10
  45.3 0.0 copy-done.11
  45.3 0.0 copy-done.12
  45.3 5.1 %owner_pass.1 = (bf16[64,104,128]{2,1,0:T(8,128)(2,1)S(1)}, bf16[256,512]{1,0:T(8,128)(2,1)S(1)}, bf16[128,512]{1,0:T(8,128)(2,1)S(1)}, bf16[2,128,512]{2,1,0:T(...) custom-call(s32[2]{0:T(128)S(1)} %pad_add_fusion.place_ref, ...), custom_call_target="tpu_custom_call" | custom-call | flops 2147483648 | bytes 10485760 | tf_op jit(solution)/shard_map/owner_pass/pallas_call | solution.py:320
  50.4 1.1 collective-permute-start.2
  51.5 1.5 %keep_products.1 = bf16[64,104,128]{2,1,0:T(8,128)(2,1)S(1)} custom-call(s32[2]{0:T(128)S(1)} %pad_add_fusion.place_ref, bf16[8,512,128]{2,1,0:T(8,128)(2,1)S(1)} %all_to_all.20.rows_ref, bf16[256,512]{1,0:T(8,128)(2,1)S(1)} %get-tuple-element.25.one_ref, bf16[128,512]{1,0:T(8,128)(2,1)S(1)} %get-tuple-element.26.two_ref, ...), custom_call_target="tpu_custom_call" | custom-call | flops 1073741824 | bytes 8388608 | tf_op jit(solution)/shard_map/keep_products/pallas_call | solution.py:303
  53.1 1.7 %collective-permute-done.2 = bf16[64,104,128]{2,1,0:T(8,128)(2,1)S(1)} collective-permute-done((bf16[64,104,128]{2,1,0:T(8,128)(2,1)S(1)}, bf16[64,104,128]{2,1,0:T(8,128)(2,1)S(1)}, u32[]{:S(2)}, u32[]{:S(2)}) %collective-permute-start.2) | collective-permute-done | bytes 1703968 | tf_op jit(solution)/shard_map/ppermute | solution.py:497
  54.8 0.4 add_convert_fusion
  55.2 31.3 %all_to_all.21.parts_ref = bf16[64,104,128]{2,1,0:T(8,128)(2,1)S(1)} all-to-all(bf16[64,104,128]{2,1,0:T(8,128)(2,1)S(1)} %add_convert_fusion), channel_id=1, replica_groups=mesh['y_hi'=2,'x'=4,'z'=4,'y_lo'=2,'core'=2] {'y_hi','x','z','y_lo'}, dimensions={0} | all-to-all | bytes 3407872 | tf_op jit(solution)/shard_map/all_to_all | solution.py:493
  86.5 0.3 sum_parts.1
  86.8 18.8 %all_to_all.22.own_ref = bf16[64,48,128]{2,1,0:T(8,128)(2,1)S(1)} all-to-all(bf16[64,48,128]{2,1,0:T(8,128)(2,1)S(1)} %sum_parts.1), channel_id=1, replica_groups=mesh['y_hi'=2,'x'=4,'z'=4,'y_lo'=2,'core'=2] {'y_hi','x','z','y_lo'}, dimensions={0} | all-to-all | bytes 1572864 | tf_op jit(solution)/shard_map/all_to_all | solution.py:493
  105.5 3.4 %collective-permute-start.3 = (bf16[64,48,128]{2,1,0:T(8,128)(2,1)S(1)}, bf16[64,48,128]{2,1,0:T(8,128)(2,1)S(1)}, u32[]{:S(2)}, u32[]{:S(2)}) collective-permute-start(bf16[64,48,128]{2,1,0:T(8,128)(2,1)S(1)} %all_to_all.22.own_ref), channel_id=1, source_target_pairs={{0,1},{1,0},{2,3},{3,2},{4,5},{5,4},{6,7},{7,6},{8,9},{9,8},{10,11... | collective-permute-start | bytes 2359304 | tf_op jit(solution)/shard_map/ppermute | solution.py:497
  108.9 1.8 %unpack_own.1 = (f32[2,64,512]{2,1,0:T(8,128)}, f32[2,512,512]{2,1,0:T(8,128)}, f32[2,112,512]{2,1,0:T(8,128)}, f32[1,512]{1,0:T(1,128)}, f32[1,512]{1,0:T(1,128)}, /*index=5*/f32[1,112]{1,0:T(1,128)}) custom-call(s32[2]{0:T(128)S(1)} %pad_add_fusion.place_ref, bf16[64,48,128]{2,1,0:T(8,128)(2,1)S(1)} %all_to_all.22.own_ref), custom_call_target="tpu_custom_call" | custom-call | flops 4194304 | bytes 4194304 | tf_op jit(solution)/shard_map/unpack_own/pallas_call | solution.py:439
  110.8 0.1 collective-permute-done.3.other_ref
  110.8 1.7 %unpack_other.1 = (f32[2,512,512]{2,1,0:T(8,128)}, f32[2,112,512]{2,1,0:T(8,128)}) custom-call(s32[2]{0:T(128)S(1)} %pad_add_fusion.place_ref, bf16[64,48,128]{2,1,0:T(8,128)(2,1)S(1)} %collective-permute-done.3.other_ref, f32[2,512,512]{2,1,0:T(8,128)} %get-tuple-element.34.two_in, ...), custom_call_target="tpu_custom_call", output_to_operand_aliasing={{0}: (2, {}), {1}: (3, {})} | custom-call | tf_op jit(solution)/shard_map/unpack_other/pallas_call | solution.py:472
  (1 shorter events, 0.0 us)
Async XLA Ops:
  0.6 9.7 %copy-start.13 = (s32[5,4096]{1,0:T(8,128)S(1)}, s32[5,4096]{1,0:T(8,128)}, u32[]{:S(2)}) copy-start(s32[5,4096]{1,0:T(8,128)} %param.17) | copy-start | bytes 245764
  0.6 9.9 %collective-permute-start = (bf16[64,16384]{1,0:T(8,128)(2,1)}, bf16[64,16384]{1,0:T(8,128)(2,1)}, u32[]{:S(2)}, u32[]{:S(2)}) collective-permute-start(bf16[64,16384]{1,0:T(8,128)(2,1)} %own_ref.1), channel_id=1, source_target_pairs={{0,1},{1,0},{2,3},{3,2},{4,5},{5,4},{6,7},{7,6},{8,9},{9,8},{10,11... | collective-permute-start | bytes 6291464 | tf_op jit(solution)/shard_map/ppermute | solution.py:497
  2.1 8.4 %copy-start = (bf16[64,16384]{1,0:T(8,128)(2,1)S(1)}, bf16[64,16384]{1,0:T(8,128)(2,1)}, u32[]{:S(2)}) copy-start(bf16[64,16384]{1,0:T(8,128)(2,1)} %own_ref.1) | copy-start | bytes 6291460
  2.1 8.4 %copy-start.1 = (s32[4096]{0:T(1024)S(1)}, s32[4096]{0:T(1024)}, u32[]{:S(2)}) copy-start(s32[4096]{0:T(1024)} %self_ref.1) | copy-start | bytes 49156
  4.2 21.8 %all-to-all-start = ((bf16[8,128,512]{2,1,0:T(8,128)(2,1)}), bf16[8,128,512]{2,1,0:T(8,128)(2,1)}, u32[]{:S(2)}, u32[]{:S(2)}) async-start(bf16[8,128,512]{2,1,0:T(8,128)(2,1)} %spread.1), calls=%async_computation | async-start | bytes 2097152 | tf_op jit(solution)/shard_map/all_to_all | solution.py:493
  22.9 22.3 %copy-start.2 = (bf16[2,512,512]{2,1,0:T(8,128)(2,1)S(1)}, bf16[2,512,512]{2,1,0:T(8,128)(2,1)}, u32[]{:S(2)}) copy-start(bf16[2,512,512]{2,1,0:T(8,128)(2,1)} %w_two_ref.1) | copy-start | bytes 3145732
  23.0 22.3 %copy-start.3 = (bf16[2,512,112]{1,2,0:T(8,128)(2,1)S(1)}, bf16[2,512,112]{1,2,0:T(8,128)(2,1)}, u32[]{:S(2)}) copy-start(bf16[2,512,112]{1,2,0:T(8,128)(2,1)} %param.28) | copy-start | bytes 688132
  23.0 22.3 %copy-start.4 = (s32[32,112]{1,0:T(8,128)S(1)}, s32[32,112]{1,0:T(8,128)}, u32[]{:S(2)}) copy-start(s32[32,112]{1,0:T(8,128)} %targets_ref.1) | copy-start | bytes 43012
  23.0 22.3 %copy-start.5 = (s32[10,128]{1,0:T(8,128)S(1)}, s32[10,128]{1,0:T(8,128)}, u32[]{:S(2)}) copy-start(s32[10,128]{1,0:T(8,128)} %near_two_ref.1) | copy-start | bytes 15364
  23.0 22.3 %copy-start.6 = (s32[15,32]{1,0:T(8,128)S(1)}, s32[15,32]{1,0:T(8,128)}, u32[]{:S(2)}) copy-start(s32[15,32]{1,0:T(8,128)} %near_three_ref.1) | copy-start | bytes 5764
  23.0 22.3 %copy-start.7 = (f32[512]{0:T(512)S(1)}, f32[512]{0:T(512)}, u32[]{:S(2)}) copy-start(f32[512]{0:T(512)} %param.25) | copy-start | bytes 6148
  23.0 22.3 %copy-start.8 = (f32[512]{0:T(512)S(1)}, f32[512]{0:T(512)}, u32[]{:S(2)}) copy-start(f32[512]{0:T(512)} %param.27) | copy-start | bytes 6148
  23.0 22.3 %copy-start.9 = (s32[128]{0:T(128)S(1)}, s32[128]{0:T(128)}, u32[]{:S(2)}) copy-start(s32[128]{0:T(128)} %count_ref.1) | copy-start | bytes 1540
  23.0 22.3 %copy-start.10 = (s32[128]{0:T(128)S(1)}, s32[128]{0:T(128)}, u32[]{:S(2)}) copy-start(s32[128]{0:T(128)} %param.18) | copy-start | bytes 1540
  23.1 22.3 %copy-start.11 = (s32[32]{0:T(128)S(1)}, s32[32]{0:T(128)}, u32[]{:S(2)}) copy-start(s32[32]{0:T(128)} %param.20) | copy-start | bytes 388
  23.1 22.3 %copy-start.12 = (f32[112]{0:T(128)S(1)}, f32[112]{0:T(128)}, u32[]{:S(2)}) copy-start(f32[112]{0:T(128)} %param.29) | copy-start | bytes 1348
  26.0 19.2 %collective-permute-start.1 = (bf16[8,128,512]{2,1,0:T(8,128)(2,1)}, bf16[8,128,512]{2,1,0:T(8,128)(2,1)S(1)}, u32[]{:S(2)}, u32[]{:S(2)}) collective-permute-start(bf16[8,128,512]{2,1,0:T(8,128)(2,1)} %all-to-all-done.w_own_ref), channel_id=1, source_target_pairs={{0,1},{1,0},{2,3},{3,2},{4,5},{5,4},{6,7},{7,6},{8,9},{9,8},{10,11... | collective-permute-start | bytes 3145736 | tf_op jit(solution)/shard_map/ppermute | solution.py:497
  50.4 4.3 %collective-permute-start.2 = (bf16[64,104,128]{2,1,0:T(8,128)(2,1)S(1)}, bf16[64,104,128]{2,1,0:T(8,128)(2,1)S(1)}, u32[]{:S(2)}, u32[]{:S(2)}) collective-permute-start(bf16[64,104,128]{2,1,0:T(8,128)(2,1)S(1)} %get-tuple-element.31), channel_id=1, source_target_pairs={{0,1},{1,0},{2,3},{3,2},{4,5},{5,4},{6,7},{7,6},{8,9},{9,8},{10,11... | collective-permute-start | bytes 5111816 | tf_op jit(solution)/shard_map/ppermute | solution.py:497
  105.5 5.3 %collective-permute-start.3 = (bf16[64,48,128]{2,1,0:T(8,128)(2,1)S(1)}, bf16[64,48,128]{2,1,0:T(8,128)(2,1)S(1)}, u32[]{:S(2)}, u32[]{:S(2)}) collective-permute-start(bf16[64,48,128]{2,1,0:T(8,128)(2,1)S(1)} %all_to_all.22.own_ref), channel_id=1, source_target_pairs={{0,1},{1,0},{2,3},{3,2},{4,5},{5,4},{6,7},{7,6},{8,9},{9,8},{10,11... | collective-permute-start | bytes 2359304 | tf_op jit(solution)/shard_map/ppermute | solution.py:497

commit v5 on v4

v5 whole, which is shorter than its diff:
```python
import functools

import jax
import jax.numpy as jnp
from jax import lax
from jax.experimental import pallas as pl
from jax.experimental.pallas import tpu as pltpu
from jax.sharding import Mesh, PartitionSpec as P

BF16 = jnp.bfloat16
F32 = jnp.float32
VMEM = pltpu.VMEM
SMEM = pltpu.SMEM
HBM = pltpu.MemorySpace.HBM

LANES = 128
SUB = 8
SPARE = 16
GATHER_UNROLL = 32
TABLE_PIECES = 8
ONE_ROWS = 64
TWO_ROWS = 32
TOP_ROWS = 8
LATE_ROWS = TWO_ROWS + TOP_ROWS
CHUNK_ROWS = ONE_ROWS + LATE_ROWS
PEERS = 64

DP = ("y_hi", "x")
CUTS = ("z", "y_lo", "core")
CHIPS = ("z", "y_lo")
SAME_CORE = DP + CHIPS


def dot(first, second, contract=((1,), (0,))):
    return lax.dot_general(first, second, (contract, ((), ())), preferred_element_type=F32)


def lead_dot(first, second):
    return dot(first, second, ((0,), (0,)))


def back_dot(first, second):
    return dot(first, second, ((1,), (1,)))


def exact_dot(picks, values):
    high = values.astype(BF16)
    low = (values - high.astype(F32)).astype(BF16)
    return dot(picks, high) + dot(picks, low)


def gelu_and_slope(values):
    square = values * values
    tanh = jnp.tanh(0.7978845608028654 * (values + 0.044715 * values * square))
    cdf = 0.5 * (1.0 + tanh)
    inner_slope = 0.7978845608028654 * (1.0 + 3.0 * 0.044715 * square)
    return values * cdf, cdf + 0.5 * values * (1.0 - tanh * tanh) * inner_slope


def vmem(count):
    return [pl.BlockSpec(memory_space=VMEM)] * count


def write_picks(self_ref, near_ref, back, pick):
    def counts(ids):
        total = jnp.zeros(spots.shape, F32)
        for offset in range(ids.shape[0]):
            total += (spots == ids[pl.ds(offset, 1), :]).astype(F32)
        return total

    spots = lax.broadcasted_iota(jnp.int32, (back.shape[0], self_ref.shape[1]), 0)
    both = jnp.concatenate([counts(self_ref), counts(near_ref)], axis=1)
    back[...] = both.astype(BF16)
    pick[...] = both.T.astype(BF16)


def gather_kernel(
    place_ref,
    own_ref,
    other_ref,
    self_ref,
    near_ref,
    out_ref,
    own,
    other,
    self_ids,
    near_ids,
    table,
    rows,
    sems,
    id_sems,
):
    core = place_ref[0]
    nodes = own_ref.shape[1]
    targets = self_ref.shape[0]
    fan = near_ref.shape[0] // targets
    chips = out_ref.shape[0]
    cap = targets // (2 * chips)
    width = nodes // TABLE_PIECES

    fetches = []
    for piece in range(TABLE_PIECES):
        spot = pl.ds(piece * width, width)
        for slot, (source, held) in enumerate(((own_ref, own), (other_ref, other))):
            fetch = pltpu.make_async_copy(source.at[:, spot], held.at[:, spot], sems.at[slot, piece])
            fetch.start()
            fetches.append(fetch)
    id_fetches = [
        pltpu.make_async_copy(self_ref, self_ids, id_sems.at[0]),
        pltpu.make_async_copy(near_ref, near_ids, id_sems.at[1]),
    ]
    for fetch in id_fetches:
        fetch.start()

    for piece in range(TABLE_PIECES):
        fetches[2 * piece].wait()
        fetches[2 * piece + 1].wait()

        @pl.loop(0, width // LANES, unroll=4)
        def _(block):
            spot = pl.ds(pl.multiple_of(piece * width + block * LANES, LANES), LANES)
            table[spot, :] = jnp.concatenate([own[:, spot], other[:, spot]], axis=0).T.astype(F32)

    for fetch in id_fetches:
        fetch.wait()

    @pl.loop(0, chips)
    def _(chip):
        first = (2 * chip + core) * cap

        @pl.loop(0, cap // GATHER_UNROLL)
        def _(group):
            start = group * GATHER_UNROLL
            mine = self_ids.at[pl.ds(first + start, GATHER_UNROLL)]
            others = [near_ids.at[pl.ds(offset * targets + first + start, GATHER_UNROLL)] for offset in range(fan)]
            for step in range(GATHER_UNROLL):
                total = table[pl.ds(others[0][step], 1), :]
                for ids in others[1:]:
                    total = total + table[pl.ds(ids[step], 1), :]
                rows[pl.ds(start + step, 1), :] = table[pl.ds(mine[step], 1), :]
                rows[pl.ds(cap + start + step, 1), :] = total

        half = lax.broadcasted_iota(jnp.int32, (cap, LANES), 1) < LANES // 2
        straight = rows[pl.ds(pl.multiple_of(core * cap, cap), cap), :] * jnp.where(core == 0, 1.0, 1.0 / fan)
        turned = rows[pl.ds(pl.multiple_of((1 - core) * cap, cap), cap), :] * jnp.where(core == 0, 1.0 / fan, 1.0)
        turned = pltpu.roll(turned, LANES // 2, 1)
        out_ref[chip, pl.ds(0, cap), :] = jnp.where(half, straight, turned).astype(BF16)
        out_ref[chip, pl.ds(cap, cap), :] = jnp.where(half, turned, straight).astype(BF16)


def gather_rows(place, own_table, other_table, self_one, near_one, chips):
    features, nodes = own_table.shape
    targets = self_one.shape[0]
    near_one = near_one.reshape(-1)
    cap = targets // (2 * chips)
    return pl.pallas_call(
        gather_kernel,
        out_shape=jax.ShapeDtypeStruct((chips, 2 * cap, LANES), BF16),
        in_specs=[pl.BlockSpec(memory_space=SMEM)] + [pl.BlockSpec(memory_space=pl.ANY)] * 4,
        out_specs=pl.BlockSpec(memory_space=VMEM),
        scratch_shapes=[
            VMEM((features, nodes), BF16),
            VMEM((features, nodes), BF16),
            SMEM(self_one.shape, jnp.int32),
            SMEM(near_one.shape, jnp.int32),
            VMEM((nodes, LANES), F32),
            VMEM((2 * cap, LANES), F32),
            pltpu.SemaphoreType.DMA((2, TABLE_PIECES)),
            pltpu.SemaphoreType.DMA((2,)),
        ],
        compiler_params=pltpu.CompilerParams(vmem_limit_bytes=24 << 20),
        cost_estimate=pl.CostEstimate(flops=1 << 27, bytes_accessed=40 << 20, transcendentals=0),
        name="gather_rows",
    )(place, own_table, other_table, self_one, near_one)


def spread_kernel(part_ref, out_ref, sems):
    copies = [pltpu.make_async_copy(part_ref, out_ref.at[chip], sems.at[chip]) for chip in range(out_ref.shape[0])]
    for copy in copies:
        copy.start()
    for copy in copies:
        copy.wait()


def spread(part, chips):
    return pl.pallas_call(
        spread_kernel,
        out_shape=jax.ShapeDtypeStruct((chips,) + part.shape, part.dtype),
        in_specs=vmem(1),
        out_specs=pl.BlockSpec(memory_space=pl.ANY),
        scratch_shapes=[pltpu.SemaphoreType.DMA((chips,))],
        name="spread",
    )(part)


def picks_kernel(self_two_ref, near_two_ref, self_three_ref, near_three_ref, back_two, pick_two, back_three, pick_three):
    write_picks(self_two_ref, near_two_ref, back_two, pick_two)
    write_picks(self_three_ref, near_three_ref, back_three, pick_three)


def make_picks(self_two, near_two, self_three, near_three, cap):
    mid_rows = self_two.shape[0]
    seeds = self_three.shape[0]
    shapes = [(cap, 2 * mid_rows), (2 * mid_rows, cap), (mid_rows, 2 * seeds), (2 * seeds, mid_rows)]
    return pl.pallas_call(
        picks_kernel,
        out_shape=tuple(jax.ShapeDtypeStruct(shape, BF16) for shape in shapes),
        in_specs=vmem(4),
        out_specs=tuple(vmem(4)),
        compiler_params=pltpu.CompilerParams(vmem_limit_bytes=8 << 20),
        name="make_picks",
    )(self_two.reshape(1, -1), near_two, self_three.reshape(1, -1), near_three)


def owner_kernel(
    fan_two,
    fan_three,
    place_ref,
    count_ref,
    counts_ref,
    rows_ref,
    w_own_ref,
    w_other_ref,
    bias_one_ref,
    pick_two,
    back_three,
    pick_three,
    targets_ref,
    w_two_ref,
    bias_two_ref,
    w_three_ref,
    bias_three_ref,
    slope_one,
    two_ref,
    mids,
    tops,
    logit_ref,
    ship_ref,
):
    core = place_ref[0]
    owner = place_ref[1]
    chips = rows_ref.shape[0]
    cap, hidden = slope_one.shape
    labels = w_three_ref.shape[1]
    mid_rows = mids.shape[1]
    seeds = tops.shape[1]
    half = LANES // 2
    front = pl.ds(pl.multiple_of(core * half, half), half)
    back = pl.ds(pl.multiple_of((1 - core) * half, half), half)

    total = None
    for chip in range(chips):
        wide = jnp.concatenate([rows_ref[chip, pl.ds(0, cap), :], rows_ref[chip, pl.ds(cap, cap), :]], axis=1)
        depth = [
            w_own_ref[chip, front, :],
            w_own_ref[chip, back, :],
            w_other_ref[chip, back, :],
            w_other_ref[chip, front, :],
        ]
        part = dot(wide, jnp.concatenate(depth, axis=0))
        total = part if total is None else total + part
    hidden_one, slope = gelu_and_slope(total + bias_one_ref[...])
    slope_one[...] = slope

    mid = dot(pick_two[...], hidden_one.astype(BF16))
    self_mid = mid[:mid_rows].astype(BF16)
    near_mid = (mid[mid_rows:] / fan_two).astype(BF16)
    mids[0] = self_mid
    mids[1] = near_mid
    pre_two = dot(self_mid, w_two_ref[0]) + dot(near_mid, w_two_ref[1]) + bias_two_ref[...]
    hidden_two, slope_two = gelu_and_slope(pre_two)

    top = dot(pick_three[...], hidden_two.astype(BF16))
    self_top = top[:seeds].astype(BF16)
    near_top = (top[seeds:] / fan_three).astype(BF16)
    tops[0] = self_top
    tops[1] = near_top
    logits = back_dot(self_top, w_three_ref[0]) + back_dot(near_top, w_three_ref[1]) + bias_three_ref[...]

    scale = 1.0 / jnp.sqrt(jnp.sum(counts_ref[...].astype(F32), axis=1, keepdims=True))
    live = lax.broadcasted_iota(jnp.int32, (seeds, labels), 0) < count_ref[owner]
    slope = jax.nn.sigmoid(logits) - targets_ref[...].astype(F32)
    logit_grad = jnp.where(live, slope * scale, 0.0).astype(BF16)

    grads = [dot(logit_grad, w_three_ref[0]), dot(logit_grad, w_three_ref[1]) / fan_three]
    upstream = exact_dot(back_three[...], jnp.concatenate(grads, axis=0))
    pre_grad_two = (slope_two * upstream).astype(BF16)

    wide_logit = jnp.concatenate([logit_grad, jnp.zeros((seeds, LANES - labels), BF16)], axis=1)
    two_ref[...] = pre_grad_two
    logit_ref[...] = wide_logit
    ship_ref[pl.ds(0, mid_rows), :] = mids[1 - core]
    ship_ref[pl.ds(mid_rows, mid_rows), :] = pre_grad_two
    ship_ref[pl.ds(2 * mid_rows, seeds), :] = tops[1 - core]
    ship_ref[pl.ds(2 * mid_rows + seeds, seeds), pl.ds(0, LANES)] = wide_logit


def write_one(out_ref, half, one, rows_ref):
    chips = rows_ref.shape[0]
    cap, hidden = one.shape
    count = hidden // PEERS
    spot = pl.ds(half * cap, cap)
    flipped = one.T
    for pair in range(chips // 2):
        wide = jnp.concatenate([rows_ref[2 * pair, spot, :], rows_ref[2 * pair + 1, spot, :]], axis=1)
        block = dot(flipped, wide)
        for peer in range(PEERS):
            line = block[peer * count : (peer + 1) * count]
            cell = jnp.concatenate([line[:, :LANES], line[:, LANES:]], axis=0)
            out_ref[peer, pl.ds(pair * 2 * SUB, 2 * SUB), :] = cell.astype(BF16)


def send_kernel(fan_two, slope_one, two_ref, back_two, w_two_ref, rows_ref, send_ref, one_ref):
    grads = [back_dot(two_ref[...], w_two_ref[0]), back_dot(two_ref[...], w_two_ref[1]) / fan_two]
    upstream = exact_dot(back_two[...], jnp.concatenate(grads, axis=0))
    pre_grad_one = (slope_one[...] * upstream).astype(BF16)
    one_ref[...] = pre_grad_one
    write_one(send_ref, 1, pre_grad_one, rows_ref)


def send_products(slope_one, two, back_two, w_two, rows, fan_two):
    return pl.pallas_call(
        functools.partial(send_kernel, fan_two),
        out_shape=(
            jax.ShapeDtypeStruct((PEERS, ONE_ROWS, LANES), BF16),
            jax.ShapeDtypeStruct(slope_one.shape, BF16),
        ),
        in_specs=vmem(5),
        out_specs=tuple(vmem(2)),
        compiler_params=pltpu.CompilerParams(vmem_limit_bytes=24 << 20),
        cost_estimate=pl.CostEstimate(flops=1 << 29, bytes_accessed=4 << 20, transcendentals=0),
        name="send_products",
    )(slope_one, two, back_two, w_two, rows)


def keep_kernel(place_ref, rows_ref, one_ref, two_ref, mids, tops, logit_ref, ship_ref, keep_ref):
    core = place_ref[0]
    hidden = one_ref.shape[1]
    mid_rows = two_ref.shape[0]
    seeds = logit_ref.shape[0]
    tiles = hidden // LANES
    count = hidden // PEERS
    write_one(keep_ref, 0, one_ref[...], rows_ref)

    other_mid = ship_ref[pl.ds(0, mid_rows), :]
    other_two = ship_ref[pl.ds(mid_rows, mid_rows), :]
    other_top = ship_ref[pl.ds(2 * mid_rows, seeds), :]
    other_logit = ship_ref[pl.ds(2 * mid_rows + seeds, seeds), pl.ds(0, LANES)]
    both_two = jnp.concatenate([two_ref[...], other_two], axis=0)
    two = lead_dot(jnp.concatenate([mids[core], other_mid], axis=0), both_two)
    both_logit = jnp.concatenate([logit_ref[...], other_logit], axis=0)
    top = lead_dot(both_logit, jnp.concatenate([tops[core], other_top], axis=0))
    bias_three = jnp.sum(logit_ref[...].astype(F32), axis=0, keepdims=True)
    biases = [
        jnp.sum(one_ref[...].astype(F32), axis=0, keepdims=True),
        jnp.sum(two_ref[...].astype(F32), axis=0, keepdims=True),
        jnp.concatenate([bias_three, jnp.zeros((1, hidden - LANES), F32)], axis=1),
        jnp.zeros((SPARE - 3, hidden), F32),
    ]
    top = jnp.concatenate([top[: LANES - SPARE]] + biases, axis=0).T
    for peer in range(PEERS):
        late = [
            two[peer * count : (peer + 1) * count, tile * LANES : (tile + 1) * LANES] for tile in range(tiles)
        ]
        late.append(top[peer * count : (peer + 1) * count, :])
        keep_ref[peer, pl.ds(ONE_ROWS, LATE_ROWS), :] = jnp.concatenate(late, axis=0).astype(BF16)


def keep_products(place, rows, one, grads):
    return pl.pallas_call(
        keep_kernel,
        out_shape=jax.ShapeDtypeStruct((PEERS, CHUNK_ROWS, LANES), BF16),
        in_specs=[pl.BlockSpec(memory_space=SMEM)] + vmem(2 + len(grads)),
        out_specs=pl.BlockSpec(memory_space=VMEM),
        compiler_params=pltpu.CompilerParams(vmem_limit_bytes=24 << 20),
        cost_estimate=pl.CostEstimate(flops=1 << 30, bytes_accessed=8 << 20, transcendentals=0),
        name="keep_products",
    )(place, rows, one, *grads)


def merge_kernel(keep_ref, other_ref, out_ref):
    spot = pl.ds(0, ONE_ROWS)
    out_ref[:, spot, :] = keep_ref[:, spot, :] + other_ref[...]


def merge(keep, other):
    return pl.pallas_call(
        merge_kernel,
        out_shape=jax.ShapeDtypeStruct(keep.shape, BF16),
        in_specs=vmem(2),
        out_specs=pl.BlockSpec(memory_space=VMEM),
        input_output_aliases={0: 0},
        compiler_params=pltpu.CompilerParams(vmem_limit_bytes=24 << 20),
        name="merge",
    )(keep, other)


def owner_pass(place, seed_count, rows, w_own, w_other, bias_one, picks, targets, w_two, bias_two, w_three, bias_three,
               fans):
    hidden = w_two.shape[2]
    labels = w_three.shape[2]
    cap = picks[1].shape[1]
    mid_rows = picks[2].shape[0]
    seeds = targets.shape[0]
    return pl.pallas_call(
        functools.partial(owner_kernel, *fans),
        out_shape=(
            jax.ShapeDtypeStruct((cap, hidden), F32),
            jax.ShapeDtypeStruct((mid_rows, hidden), BF16),
            jax.ShapeDtypeStruct((2, mid_rows, hidden), BF16),
            jax.ShapeDtypeStruct((2, seeds, hidden), BF16),
            jax.ShapeDtypeStruct((seeds, LANES), BF16),
            jax.ShapeDtypeStruct((2 * (mid_rows + seeds), hidden), BF16),
        ),
        in_specs=[pl.BlockSpec(memory_space=SMEM)] * 2 + vmem(13),
        out_specs=tuple(vmem(6)),
        compiler_params=pltpu.CompilerParams(vmem_limit_bytes=24 << 20),
        cost_estimate=pl.CostEstimate(flops=1 << 31, bytes_accessed=10 << 20, transcendentals=1 << 19),
        name="owner_pass",
    )(
        place, seed_count, seed_count.reshape(1, -1), rows, w_own, w_other, bias_one.reshape(1, -1), *picks[1:],
        targets, w_two, bias_two.reshape(1, -1), jnp.transpose(w_three, (0, 2, 1)), bias_three.reshape(1, -1),
    )


def sum_kernel(parts_ref, out_ref):
    total = parts_ref[0].astype(F32)
    for peer in range(1, PEERS):
        total = total + parts_ref[peer].astype(F32)
    late = total[ONE_ROWS:]
    chips = ONE_ROWS // SUB
    for chip in range(chips):
        block = jnp.concatenate([total[chip * SUB : (chip + 1) * SUB], late], axis=0).astype(BF16)
        for group in range(PEERS // chips):
            out_ref[group * chips + chip] = block


def sum_parts(parts):
    return pl.pallas_call(
        sum_kernel,
        out_shape=jax.ShapeDtypeStruct((PEERS, SUB + LATE_ROWS, LANES), BF16),
        in_specs=vmem(1),
        out_specs=pl.BlockSpec(memory_space=VMEM),
        compiler_params=pltpu.CompilerParams(vmem_limit_bytes=24 << 20),
        name="sum_parts",
    )(parts)


def write_late(ref, side, grad_two, grad_three, two, top, three, sems):
    hidden = two.shape[0]
    labels = three.shape[0]
    count = hidden // PEERS
    pieces = sems.shape[0] - 1
    step = hidden // pieces
    copies = []
    for peer in range(PEERS):
        cells = ref[peer].astype(F32)
        for tile in range(hidden // LANES):
            two[pl.ds(peer * count, count), pl.ds(tile * LANES, LANES)] = cells[
                SUB + tile * count : SUB + (tile + 1) * count
            ]
        top[pl.ds(peer * count, count), :] = cells[SUB + TWO_ROWS :]
        done = (peer + 1) * count
        if done % step == 0:
            spot = pl.ds(done - step, step)
            copies.append(pltpu.make_async_copy(two.at[spot], grad_two.at[side, spot], sems.at[len(copies)]))
            copies[-1].start()
    flipped = top[...].T
    three[...] = flipped[:labels]
    copies.append(pltpu.make_async_copy(three, grad_three.at[side], sems.at[pieces]))
    copies[-1].start()
    return flipped[labels:], copies


def own_kernel(
    place_ref,
    own_ref,
    grad_one,
    grad_two,
    grad_three,
    biases,
    flat,
    one,
    two,
    top,
    three,
    sems,
    one_sem,
):
    cut_rows, hidden = one.shape[1:]
    count = hidden // PEERS
    for peer in range(PEERS):
        flat[pl.ds(peer * count, count), :] = own_ref[peer].astype(F32)[:SUB]
    turned = flat[...].T
    one[place_ref[0]] = turned[:cut_rows]
    one[1 - place_ref[0]] = turned[cut_rows:]
    one_copy = pltpu.make_async_copy(one, grad_one, one_sem)
    one_copy.start()
    kept, copies = write_late(own_ref, place_ref[0], grad_two, grad_three, two, top, three, sems)
    biases[...] = kept
    for copy in [one_copy] + copies:
        copy.wait()


def other_kernel(
    place_ref,
    other_ref,
    biases,
    two_in,
    three_in,
    grad_two,
    grad_three,
    bias_one,
    bias_two,
    bias_three,
    two,
    top,
    three,
    first,
    second,
    third,
    sems,
    bias_sems,
):
    kept, copies = write_late(other_ref, 1 - place_ref[0], grad_two, grad_three, two, top, three, sems)
    kept = kept + biases[...]
    first[...] = kept[0:1]
    second[...] = kept[1:2]
    third[...] = kept[2:3, : three.shape[0]]
    for slot, (held, out) in enumerate(((first, bias_one), (second, bias_two), (third, bias_three))):
        copies.append(pltpu.make_async_copy(held, out, bias_sems.at[slot]))
        copies[-1].start()
    for copy in copies:
        copy.wait()


def unpack_own(place, own, cut_rows, hidden, labels):
    anywhere = pl.BlockSpec(memory_space=pl.ANY)
    return pl.pallas_call(
        own_kernel,
        out_shape=(
            jax.ShapeDtypeStruct((2, cut_rows, hidden), F32),
            jax.ShapeDtypeStruct((2, hidden, hidden), F32),
            jax.ShapeDtypeStruct((2, labels, hidden), F32),
            jax.ShapeDtypeStruct((SPARE, hidden), F32),
        ),
        in_specs=[pl.BlockSpec(memory_space=SMEM)] + vmem(1),
        out_specs=(anywhere,) * 3 + tuple(vmem(1)),
        scratch_shapes=[
            VMEM((hidden, LANES), F32),
            VMEM((2, cut_rows, hidden), F32),
            VMEM((hidden, hidden), F32),
            VMEM((hidden, LANES), F32),
            VMEM((labels, hidden), F32),
            pltpu.SemaphoreType.DMA((9,)),
            pltpu.SemaphoreType.DMA,
        ],
        compiler_params=pltpu.CompilerParams(vmem_limit_bytes=16 << 20),
        cost_estimate=pl.CostEstimate(flops=1 << 22, bytes_accessed=4 << 20, transcendentals=0),
        name="unpack_own",
    )(place, own)


def unpack_other(place, other, biases, grad_two, grad_three):
    hidden = grad_two.shape[2]
    labels = grad_three.shape[1]
    anywhere = pl.BlockSpec(memory_space=pl.ANY)
    return pl.pallas_call(
        other_kernel,
        out_shape=(
            jax.ShapeDtypeStruct(grad_two.shape, F32),
            jax.ShapeDtypeStruct(grad_three.shape, F32),
            jax.ShapeDtypeStruct((1, hidden), F32),
            jax.ShapeDtypeStruct((1, hidden), F32),
            jax.ShapeDtypeStruct((1, labels), F32),
        ),
        in_specs=[pl.BlockSpec(memory_space=SMEM)] + vmem(2) + [anywhere] * 2,
        out_specs=(anywhere,) * 5,
        scratch_shapes=[
            VMEM((hidden, hidden), F32),
            VMEM((hidden, LANES), F32),
            VMEM((labels, hidden), F32),
            VMEM((1, hidden), F32),
            VMEM((1, hidden), F32),
            VMEM((1, labels), F32),
            pltpu.SemaphoreType.DMA((9,)),
            pltpu.SemaphoreType.DMA((3,)),
        ],
        input_output_aliases={3: 0, 4: 1},
        compiler_params=pltpu.CompilerParams(vmem_limit_bytes=16 << 20),
        name="unpack_other",
    )(place, other, biases, grad_two, grad_three)


def exchange(values, axes):
    return lax.all_to_all(values, axes, 0, 0, tiled=True)


def swap_core(values):
    return lax.ppermute(values, "core", [(0, 1), (1, 0)])


def local(
    feat_table,
    self_one,
    near_one,
    self_two,
    near_two,
    self_three,
    near_three,
    targets,
    seed_count,
    w_one,
    bias_one,
    w_two,
    bias_two,
    w_three,
    bias_three,
):
    cut_rows, hidden = w_one.shape[1:]
    labels = w_three.shape[2]
    chips = lax.axis_size(CHIPS)
    cap = self_one.shape[0] // (2 * chips)
    owner = lax.axis_index(DP) * lax.axis_size(CUTS) + lax.axis_index(CUTS)
    place = jnp.stack([lax.axis_index("core"), owner]).astype(jnp.int32)
    other_table = swap_core(feat_table)
    w_own = exchange(spread(w_one.reshape(-1, hidden), chips), CHIPS)
    rows = gather_rows(place, feat_table, other_table, self_one, near_one, chips)
    self_two, rows = lax.optimization_barrier((self_two, rows))
    picks = make_picks(self_two, near_two, self_three, near_three, cap)
    w_own, rows, picks = lax.optimization_barrier((w_own, rows, picks))
    w_other = swap_core(w_own)
    rows = exchange(rows, CHIPS)
    fans = (near_two.shape[0], near_three.shape[0])
    slope_one, *grads, ship = owner_pass(
        place, seed_count, rows, w_own, w_other, bias_one, picks, targets, w_two, bias_two, w_three, bias_three, fans
    )
    ship = swap_core(ship)
    send, one = send_products(slope_one, grads[0], picks[0], w_two, rows, fans[0])
    send, ship = lax.optimization_barrier((send, ship))
    other = swap_core(send)
    keep = keep_products(place, rows, one, (*grads, ship))
    parts = merge(keep, other)
    sums = sum_parts(exchange(parts, SAME_CORE))
    own = exchange(sums, SAME_CORE)
    other = swap_core(own)
    grad_one, grad_two, grad_three, biases = unpack_own(place, own, cut_rows, hidden, labels)
    grad_two, grad_three, bias_one, bias_two, bias_three = unpack_other(place, other, biases, grad_two, grad_three)
    return (
        grad_one,
        bias_one.reshape(-1),
        grad_two,
        bias_two.reshape(-1),
        jnp.transpose(grad_three, (0, 2, 1)),
        bias_three.reshape(-1),
    )


def solution(mesh):
    fine = Mesh(mesh.devices.reshape(2, 4, 4, 2, 2), ("y_hi", "x", "z", "y_lo", "core"))
    both = DP + CUTS
    return jax.shard_map(
        local,
        mesh=fine,
        in_specs=(
            P(CUTS, DP),
            P(DP),
            P(None, DP),
            P(both),
            P(None, both),
            P(both),
            P(None, both),
            P(both, None),
            P(),
            P(None, CUTS, None),
            P(),
            P(),
            P(),
            P(),
            P(),
        ),
        out_specs=(P(None, CUTS, None), P(), P(), P(), P(), P()),
        check_vma=False,
    )
```

time: 113 us -> 112 us (level)
  waiting for transfers between devices: 4.76 us -> 3.11 us
    ppermute x4 -> x5, starting transfers between devices: 7.17 us -> 7.62 us  [swap_core(): return lax.ppermute(values, 'core', [(0, 1), (1, 0)])]
    pallas_call x1 -> x4, Pallas kernels: 5.08 us -> 5.44 us  [the longest x1 3.4 us: owner_pass(): pl.pallas_call(functools.partial(owner_kernel, *fans), out_shape=(jax.Sha...]
  transfers between devices with their start and end apart: 5 -> 6, of which waited for: 3 -> 3; matrix products, arithmetic and copies ran while one was open for 0% -> 0% of each run, Pallas kernels for 16% -> 17%
where the time goes in v5:
time: 112 us
  blocking collectives  68.4 us (61%)
  Pallas kernels  25.4 us (23%)
  starting transfers between devices  13.8 us (12%)
  waiting for transfers between devices  3.11 us (3%)
    all_to_all x3, blocking collectives, exchange(): return lax.all_to_all(values, axes, 0, 0, tiled=True)  68.4 us
    pallas_call x1, Pallas kernels, gather_rows(): pl.pallas_call(gather_kernel, out_shape=jax.ShapeDtypeStruct((chips, 2 *...  13 us
    ppermute x5, starting transfers between devices, swap_core(): return lax.ppermute(values, 'core', [(0, 1), (1, 0)])  7.62 us
    all_to_all x1, starting transfers between devices, exchange(): return lax.all_to_all(values, axes, 0, 0, tiled=True)  6.14 us
    pallas_call x1, Pallas kernels, owner_pass(): pl.pallas_call(functools.partial(owner_kernel, *fans), out_shape=(jax.Sha...  3.4 us
  transfers between devices with their start and end apart: 6, of which 3 were waited for; matrix products, arithmetic and copies ran while one was open for 0% of the time, Pallas kernels for 17%

profile of v5, /device:TPU:1, one launch (start us, length us, event | category | flops | bytes accessed | tf_op | source)
XLA Modules:
  0.0 111.7 jit_solution(2077927481787658171)
XLA Ops:
  0.6 0.0 copy-start
  0.6 0.0 copy-start.13
  0.7 0.0 copy-start.2
  0.7 1.5 %collective-permute-start = (bf16[64,16384]{1,0:T(8,128)(2,1)}, bf16[64,16384]{1,0:T(8,128)(2,1)}, u32[]{:S(2)}, u32[]{:S(2)}) collective-permute-start(bf16[64,16384]{1,0:T(8,128)(2,1)} %own_ref.1), channel_id=1, source_target_pairs={{0,1},{1,0},{2,3},{3,2},{4,5},{5,4},{6,7},{7,6},{8,9},{9,8},{10,11... | collective-permute-start | bytes 6291464 | tf_op jit(solution)/shard_map/ppermute | solution.py:600
  2.2 1.9 %spread.1 = bf16[8,128,512]{2,1,0:T(8,128)(2,1)} custom-call(bf16[128,512]{1,0:T(8,128)(2,1)} %bitcast.22), custom_call_target="tpu_custom_call" | custom-call | tf_op jit(solution)/shard_map/spread/pallas_call | solution.py:186
  4.1 6.1 %all-to-all-start = ((bf16[8,128,512]{2,1,0:T(8,128)(2,1)}), bf16[8,128,512]{2,1,0:T(8,128)(2,1)}, u32[]{:S(2)}, u32[]{:S(2)}) async-start(bf16[8,128,512]{2,1,0:T(8,128)(2,1)} %spread.1), calls=%async_computation | async-start | bytes 2097152 | tf_op jit(solution)/shard_map/all_to_all | solution.py:596
  10.2 0.0 copy-done.13
  10.3 0.1 pad_add_fusion.place_ref
  10.4 0.0 copy-start.3
  10.4 0.0 copy-start.4
  10.4 0.0 copy-start.5
  10.4 0.0 copy-start.6
  10.4 0.0 collective-permute-done.other_ref
  10.4 0.0 copy-done
  10.4 0.0 copy-done.2
  10.4 13.0 %gather_rows.1 = bf16[8,512,128]{2,1,0:T(8,128)(2,1)S(1)} custom-call(s32[2]{0:T(128)S(1)} %pad_add_fusion.place_ref, bf16[64,16384]{1,0:T(8,128)(2,1)S(1)} %copy-done, bf16[64,16384]{1,0:T(8,128)(2,1)} %collective-permute-done.other_ref, s32[4096]{0:T(1024)S(1)} %copy-done.2, s32[20480]{0:T(1024)S(1)} %reshape.46.near_ref), custom_call_target="tpu_custom_call" | custom-call | flops 134217728 | bytes 41943040 | tf_op jit(solution)/shard_map/gather_rows/pallas_call | solution.py:156
  23.4 0.0 copy-start.1
  23.4 0.0 copy-start.7
  23.4 0.0 copy-start.8
  23.4 0.0 copy-start.9
  23.4 0.0 copy-start.10
  23.5 0.0 copy-start.11
  23.5 0.0 copy-start.12
  23.5 0.0 copy-done.3
  23.5 0.0 copy-done.4
  23.5 0.0 copy-done.5
  23.5 0.0 copy-done.6
  23.5 0.4 make_picks.1
  23.9 1.9 %all-to-all-done.w_own_ref = bf16[8,128,512]{2,1,0:T(8,128)(2,1)} async-done(((bf16[8,128,512]{2,1,0:T(8,128)(2,1)}), bf16[8,128,512]{2,1,0:T(8,128)(2,1)}, u32[]{:S(2)}, u32[]{:S(2)}) %all-to-all-start) | async-done | bytes 1048608 | tf_op jit(solution)/shard_map/all_to_all | solution.py:596
  25.8 1.3 %collective-permute-start.1 = (bf16[8,128,512]{2,1,0:T(8,128)(2,1)}, bf16[8,128,512]{2,1,0:T(8,128)(2,1)S(1)}, u32[]{:S(2)}, u32[]{:S(2)}) collective-permute-start(bf16[8,128,512]{2,1,0:T(8,128)(2,1)} %all-to-all-done.w_own_ref), channel_id=1, source_target_pairs={{0,1},{1,0},{2,3},{3,2},{4,5},{5,4},{6,7},{7,6},{8,9},{9,8},{10,11... | collective-permute-start | bytes 3145736 | tf_op jit(solution)/shard_map/ppermute | solution.py:600
  27.0 18.1 %all_to_all.20.rows_ref = bf16[8,512,128]{2,1,0:T(8,128)(2,1)S(1)} all-to-all(bf16[8,512,128]{2,1,0:T(8,128)(2,1)S(1)} %gather_rows.1), channel_id=1, replica_groups=mesh['y_hi'=2,'x'=4,'z'=4,'y_lo'=2,'core'=2] {'z','y_lo'}, dimensions={0} | all-to-all | bytes 2097152 | tf_op jit(solution)/shard_map/all_to_all | solution.py:596
  45.1 0.0 collective-permute-done.1.w_other_ref
  45.1 0.0 copy-done.1
  45.1 0.0 copy-done.7
  45.1 0.0 copy-done.8
  45.2 0.0 copy-done.9
  45.2 0.0 copy-done.10
  45.2 0.0 copy-done.11
  45.2 0.0 copy-done.12
  45.2 3.4 %owner_pass.1 = (f32[256,512]{1,0:T(8,128)S(1)}, bf16[128,512]{1,0:T(8,128)(2,1)S(1)}, bf16[2,128,512]{2,1,0:T(8,128)(2,1)S(1)}, bf16[2,32,512]{2,1,0:T(8,128)(2...) custom-call(s32[2]{0:T(128)S(1)} %pad_add_fusion.place_ref, s32[128]{0:T(128)S(1)} %copy-done.11, ...), custom_call_target="tpu_custom_call" | custom-call | flops 2147483648 | bytes 10485760 | tf_op jit(solution)/shard_map/owner_pass/pallas_call | solution.py:405
  48.6 1.2 %collective-permute-start.2 = (bf16[320,512]{1,0:T(8,128)(2,1)S(1)}, bf16[320,512]{1,0:T(8,128)(2,1)S(1)}, u32[]{:S(2)}, u32[]{:S(2)}) collective-permute-start(bf16[320,512]{1,0:T(8,128)(2,1)S(1)} %get-tuple-element.56), channel_id=1, source_target_pairs={{0,1},{1,0},{2,3},{3,2},{4,5},{5,4},{6,7},{7,6},{8,9},{9,8},{10,11... | collective-permute-start | bytes 983048 | tf_op jit(solution)/shard_map/ppermute | solution.py:600
  49.8 1.2 %send_products.1 = (bf16[64,64,128]{2,1,0:T(8,128)(2,1)S(1)}, bf16[256,512]{1,0:T(8,128)(2,1)S(1)}) custom-call(f32[256,512]{1,0:T(8,128)S(1)} %get-tuple-element.48.slope_one, bf16[128,512]{1,0:T(8,128)(2,1)S(1)} %get-tuple-element.49.two_ref, bf16[256,256]{1,0:T(8,128)(2,1)S(1)} %get-tuple-element.50.back_two, bf16[2,512,512]{2,1,0:T(8,128)(2,1)S(1)} %copy-done.1, ...), custom_call_target="tpu_custom_call" | custom-call | flops 536870912 | bytes 4194304 | tf_op jit(solution)/shard_map/send_products/pallas_call | solution.py:322
  51.0 0.0 collective-permute-done.2.ship_ref
  51.1 0.4 collective-permute-start.3
  51.4 1.2 %keep_products.1.keep_ref = bf16[64,104,128]{2,1,0:T(8,128)(2,1)S(1)} custom-call(s32[2]{0:T(128)S(1)} %pad_add_fusion.place_ref, bf16[8,512,128]{2,1,0:T(8,128)(2,1)S(1)} %all_to_all.20.rows_ref, bf16[256,512]{1,0:T(8,128)(2,1)S(1)} %get-tuple-element.51.one_ref, bf16[128,512]{1,0:T(8,128)(2,1)S(1)} %get-tuple-element.49.two_ref, ...), custom_call_target="tpu_custom_call" | custom-call | flops 1073741824 | bytes 8388608 | tf_op jit(solution)/shard_map/keep_products/pallas_call | solution.py:370
  52.7 1.1 collective-permute-done.3.other_ref
  53.8 0.5 merge.1
  54.3 31.3 %all_to_all.21.parts_ref = bf16[64,104,128]{2,1,0:T(8,128)(2,1)S(1)} all-to-all(bf16[64,104,128]{2,1,0:T(8,128)(2,1)S(1)} %merge.1), channel_id=1, replica_groups=mesh['y_hi'=2,'x'=4,'z'=4,'y_lo'=2,'core'=2] {'y_hi','x','z','y_lo'}, dimensions={0} | all-to-all | bytes 3407872 | tf_op jit(solution)/shard_map/all_to_all | solution.py:596
  85.5 0.3 sum_parts.1
  85.8 19.0 %all_to_all.22.own_ref = bf16[64,48,128]{2,1,0:T(8,128)(2,1)S(1)} all-to-all(bf16[64,48,128]{2,1,0:T(8,128)(2,1)S(1)} %sum_parts.1), channel_id=1, replica_groups=mesh['y_hi'=2,'x'=4,'z'=4,'y_lo'=2,'core'=2] {'y_hi','x','z','y_lo'}, dimensions={0} | all-to-all | bytes 1572864 | tf_op jit(solution)/shard_map/all_to_all | solution.py:596
  104.8 3.3 %collective-permute-start.4 = (bf16[64,48,128]{2,1,0:T(8,128)(2,1)S(1)}, bf16[64,48,128]{2,1,0:T(8,128)(2,1)S(1)}, u32[]{:S(2)}, u32[]{:S(2)}) collective-permute-start(bf16[64,48,128]{2,1,0:T(8,128)(2,1)S(1)} %all_to_all.22.own_ref), channel_id=1, source_target_pairs={{0,1},{1,0},{2,3},{3,2},{4,5},{5,4},{6,7},{7,6},{8,9},{9,8},{10,11... | collective-permute-start | bytes 2359304 | tf_op jit(solution)/shard_map/ppermute | solution.py:600
  108.1 1.8 %unpack_own.1 = (f32[2,64,512]{2,1,0:T(8,128)}, f32[2,512,512]{2,1,0:T(8,128)}, f32[2,112,512]{2,1,0:T(8,128)}, f32[16,512]{1,0:T(8,128)S(1)}) custom-call(s32[2]{0:T(128)S(1)} %pad_add_fusion.place_ref, bf16[64,48,128]{2,1,0:T(8,128)(2,1)S(1)} %all_to_all.22.own_ref), custom_call_target="tpu_custom_call" | custom-call | flops 4194304 | bytes 4194304 | tf_op jit(solution)/shard_map/unpack_own/pallas_call | solution.py:539
  109.9 0.1 collective-permute-done.4.other_ref
  110.0 1.7 %unpack_other.1 = (f32[2,512,512]{2,1,0:T(8,128)}, f32[2,112,512]{2,1,0:T(8,128)}, f32[1,512]{1,0:T(1,128)}, f32[1,512]{1,0:T(1,128)}, f32[1,112]{1,0:T(1,128)}) custom-call(s32[2]{0:T(128)S(1)} %pad_add_fusion.place_ref, bf16[64,48,128]{2,1,0:T(8,128)(2,1)S(1)} %collective-permute-done.4.other_ref, ...), custom_call_target="tpu_custom_call", output_to_operand_aliasing={{0}: (3, {}), {1}: (4, {})} | custom-call | tf_op jit(solution)/shard_map/unpack_other/pallas_call | solution.py:568
  (1 shorter events, 0.0 us)
Async XLA Ops:
  0.6 9.8 %copy-start = (bf16[64,16384]{1,0:T(8,128)(2,1)S(1)}, bf16[64,16384]{1,0:T(8,128)(2,1)}, u32[]{:S(2)}) copy-start(bf16[64,16384]{1,0:T(8,128)(2,1)} %own_ref.1) | copy-start | bytes 6291460
  0.6 9.6 %copy-start.13 = (s32[5,4096]{1,0:T(8,128)S(1)}, s32[5,4096]{1,0:T(8,128)}, u32[]{:S(2)}) copy-start(s32[5,4096]{1,0:T(8,128)} %param.17) | copy-start | bytes 245764
  0.7 9.8 %copy-start.2 = (s32[4096]{0:T(1024)S(1)}, s32[4096]{0:T(1024)}, u32[]{:S(2)}) copy-start(s32[4096]{0:T(1024)} %self_ref.1) | copy-start | bytes 49156
  0.7 9.7 %collective-permute-start = (bf16[64,16384]{1,0:T(8,128)(2,1)}, bf16[64,16384]{1,0:T(8,128)(2,1)}, u32[]{:S(2)}, u32[]{:S(2)}) collective-permute-start(bf16[64,16384]{1,0:T(8,128)(2,1)} %own_ref.1), channel_id=1, source_target_pairs={{0,1},{1,0},{2,3},{3,2},{4,5},{5,4},{6,7},{7,6},{8,9},{9,8},{10,11... | collective-permute-start | bytes 6291464 | tf_op jit(solution)/shard_map/ppermute | solution.py:600
  4.1 21.7 %all-to-all-start = ((bf16[8,128,512]{2,1,0:T(8,128)(2,1)}), bf16[8,128,512]{2,1,0:T(8,128)(2,1)}, u32[]{:S(2)}, u32[]{:S(2)}) async-start(bf16[8,128,512]{2,1,0:T(8,128)(2,1)} %spread.1), calls=%async_computation | async-start | bytes 2097152 | tf_op jit(solution)/shard_map/all_to_all | solution.py:596
  10.4 13.1 %copy-start.3 = (s32[10,128]{1,0:T(8,128)S(1)}, s32[10,128]{1,0:T(8,128)}, u32[]{:S(2)}) copy-start(s32[10,128]{1,0:T(8,128)} %near_two_ref.1) | copy-start | bytes 15364
  10.4 13.1 %copy-start.4 = (s32[15,32]{1,0:T(8,128)S(1)}, s32[15,32]{1,0:T(8,128)}, u32[]{:S(2)}) copy-start(s32[15,32]{1,0:T(8,128)} %near_three_ref.1) | copy-start | bytes 5764
  10.4 13.1 %copy-start.5 = (s32[128]{0:T(128)S(1)}, s32[128]{0:T(128)}, u32[]{:S(2)}) copy-start(s32[128]{0:T(128)} %param.18) | copy-start | bytes 1540
  10.4 13.1 %copy-start.6 = (s32[32]{0:T(128)S(1)}, s32[32]{0:T(128)}, u32[]{:S(2)}) copy-start(s32[32]{0:T(128)} %param.20) | copy-start | bytes 388
  23.4 21.7 %copy-start.1 = (bf16[2,512,512]{2,1,0:T(8,128)(2,1)S(1)}, bf16[2,512,512]{2,1,0:T(8,128)(2,1)}, u32[]{:S(2)}) copy-start(bf16[2,512,512]{2,1,0:T(8,128)(2,1)} %w_two_ref.3) | copy-start | bytes 3145732
  23.4 21.7 %copy-start.7 = (bf16[2,512,112]{1,2,0:T(8,128)(2,1)S(1)}, bf16[2,512,112]{1,2,0:T(8,128)(2,1)}, u32[]{:S(2)}) copy-start(bf16[2,512,112]{1,2,0:T(8,128)(2,1)} %param.28) | copy-start | bytes 688132
  23.4 21.7 %copy-start.8 = (s32[32,112]{1,0:T(8,128)S(1)}, s32[32,112]{1,0:T(8,128)}, u32[]{:S(2)}) copy-start(s32[32,112]{1,0:T(8,128)} %targets_ref.1) | copy-start | bytes 43012
  23.4 21.7 %copy-start.9 = (f32[512]{0:T(512)S(1)}, f32[512]{0:T(512)}, u32[]{:S(2)}) copy-start(f32[512]{0:T(512)} %param.25) | copy-start | bytes 6148
  23.4 21.7 %copy-start.10 = (f32[512]{0:T(512)S(1)}, f32[512]{0:T(512)}, u32[]{:S(2)}) copy-start(f32[512]{0:T(512)} %param.27) | copy-start | bytes 6148
  23.5 21.7 %copy-start.11 = (s32[128]{0:T(128)S(1)}, s32[128]{0:T(128)}, u32[]{:S(2)}) copy-start(s32[128]{0:T(128)} %count_ref.1) | copy-start | bytes 1540
  23.5 21.7 %copy-start.12 = (f32[112]{0:T(128)S(1)}, f32[112]{0:T(128)}, u32[]{:S(2)}) copy-start(f32[112]{0:T(128)} %param.29) | copy-start | bytes 1348
  25.8 19.4 %collective-permute-start.1 = (bf16[8,128,512]{2,1,0:T(8,128)(2,1)}, bf16[8,128,512]{2,1,0:T(8,128)(2,1)S(1)}, u32[]{:S(2)}, u32[]{:S(2)}) collective-permute-start(bf16[8,128,512]{2,1,0:T(8,128)(2,1)} %all-to-all-done.w_own_ref), channel_id=1, source_target_pairs={{0,1},{1,0},{2,3},{3,2},{4,5},{5,4},{6,7},{7,6},{8,9},{9,8},{10,11... | collective-permute-start | bytes 3145736 | tf_op jit(solution)/shard_map/ppermute | solution.py:600
  48.6 2.5 %collective-permute-start.2 = (bf16[320,512]{1,0:T(8,128)(2,1)S(1)}, bf16[320,512]{1,0:T(8,128)(2,1)S(1)}, u32[]{:S(2)}, u32[]{:S(2)}) collective-permute-start(bf16[320,512]{1,0:T(8,128)(2,1)S(1)} %get-tuple-element.56), channel_id=1, source_target_pairs={{0,1},{1,0},{2,3},{3,2},{4,5},{5,4},{6,7},{7,6},{8,9},{9,8},{10,11... | collective-permute-start | bytes 983048 | tf_op jit(solution)/shard_map/ppermute | solution.py:600
  51.1 2.7 %collective-permute-start.3 = (bf16[64,64,128]{2,1,0:T(8,128)(2,1)S(1)}, bf16[64,64,128]{2,1,0:T(8,128)(2,1)S(1)}, u32[]{:S(2)}, u32[]{:S(2)}) collective-permute-start(bf16[64,64,128]{2,1,0:T(8,128)(2,1)S(1)} %get-tuple-element.58), channel_id=1, source_target_pairs={{0,1},{1,0},{2,3},{3,2},{4,5},{5,4},{6,7},{7,6},{8,9},{9,8},{10,11... | collective-permute-start | bytes 3145736 | tf_op jit(solution)/shard_map/ppermute | solution.py:600
  104.8 5.2 %collective-permute-start.4 = (bf16[64,48,128]{2,1,0:T(8,128)(2,1)S(1)}, bf16[64,48,128]{2,1,0:T(8,128)(2,1)S(1)}, u32[]{:S(2)}, u32[]{:S(2)}) collective-permute-start(bf16[64,48,128]{2,1,0:T(8,128)(2,1)S(1)} %all_to_all.22.own_ref), channel_id=1, source_target_pairs={{0,1},{1,0},{2,3},{3,2},{4,5},{5,4},{6,7},{7,6},{8,9},{9,8},{10,11... | collective-permute-start | bytes 2359304 | tf_op jit(solution)/shard_map/ppermute | solution.py:600

commit v6 on v5

--- a/solution.py
+++ b/solution.py
@@ -295,53 +295,31 @@
     ship_ref[pl.ds(2 * mid_rows + seeds, seeds), pl.ds(0, LANES)] = wide_logit
 
 
-def write_one(out_ref, half, one, rows_ref):
-    chips = rows_ref.shape[0]
-    cap, hidden = one.shape
-    count = hidden // PEERS
-    spot = pl.ds(half * cap, cap)
-    flipped = one.T
-    for pair in range(chips // 2):
-        wide = jnp.concatenate([rows_ref[2 * pair, spot, :], rows_ref[2 * pair + 1, spot, :]], axis=1)
-        block = dot(flipped, wide)
-        for peer in range(PEERS):
-            line = block[peer * count : (peer + 1) * count]
-            cell = jnp.concatenate([line[:, :LANES], line[:, LANES:]], axis=0)
-            out_ref[peer, pl.ds(pair * 2 * SUB, 2 * SUB), :] = cell.astype(BF16)
-
-
-def send_kernel(fan_two, slope_one, two_ref, back_two, w_two_ref, rows_ref, send_ref, one_ref):
+def first_kernel(fan_two, slope_one, two_ref, back_two, w_two_ref, one_ref):
     grads = [back_dot(two_ref[...], w_two_ref[0]), back_dot(two_ref[...], w_two_ref[1]) / fan_two]
     upstream = exact_dot(back_two[...], jnp.concatenate(grads, axis=0))
-    pre_grad_one = (slope_one[...] * upstream).astype(BF16)
-    one_ref[...] = pre_grad_one
-    write_one(send_ref, 1, pre_grad_one, rows_ref)
-
-
-def send_products(slope_one, two, back_two, w_two, rows, fan_two):
-    return pl.pallas_call(
-        functools.partial(send_kernel, fan_two),
-        out_shape=(
-            jax.ShapeDtypeStruct((PEERS, ONE_ROWS, LANES), BF16),
-            jax.ShapeDtypeStruct(slope_one.shape, BF16),
-        ),
-        in_specs=vmem(5),
-        out_specs=tuple(vmem(2)),
+    one_ref[...] = (slope_one[...] * upstream).astype(BF16)
+
+
+def first_grad(slope_one, two, back_two, w_two, fan_two):
+    return pl.pallas_call(
+        functools.partial(first_kernel, fan_two),
+        out_shape=jax.ShapeDtypeStruct(slope_one.shape, BF16),
+        in_specs=vmem(4),
+        out_specs=pl.BlockSpec(memory_space=VMEM),
         compiler_params=pltpu.CompilerParams(vmem_limit_bytes=24 << 20),
         cost_estimate=pl.CostEstimate(flops=1 << 29, bytes_accessed=4 << 20, transcendentals=0),
-        name="send_products",
-    )(slope_one, two, back_two, w_two, rows)
-
-
-def keep_kernel(place_ref, rows_ref, one_ref, two_ref, mids, tops, logit_ref, ship_ref, keep_ref):
+        name="first_grad",
+    )(slope_one, two, back_two, w_two)
+
+
+def late_kernel(place_ref, two_ref, mids, tops, logit_ref, ship_ref, one_ref, parts_ref):
     core = place_ref[0]
     hidden = one_ref.shape[1]
     mid_rows = two_ref.shape[0]
     seeds = logit_ref.shape[0]
     tiles = hidden // LANES
     count = hidden // PEERS
-    write_one(keep_ref, 0, one_ref[...], rows_ref)
-
     other_mid = ship_ref[pl.ds(0, mid_rows), :]
     other_two = ship_ref[pl.ds(mid_rows, mid_rows), :]
     other_top = ship_ref[pl.ds(2 * mid_rows, seeds), :]
@@ -363,36 +341,51 @@
             two[peer * count : (peer + 1) * count, tile * LANES : (tile + 1) * LANES] for tile in range(tiles)
         ]
         late.append(top[peer * count : (peer + 1) * count, :])
-        keep_ref[peer, pl.ds(ONE_ROWS, LATE_ROWS), :] = jnp.concatenate(late, axis=0).astype(BF16)
-
-
-def keep_products(place, rows, one, grads):
-    return pl.pallas_call(
-        keep_kernel,
+        parts_ref[peer, pl.ds(ONE_ROWS, LATE_ROWS), :] = jnp.concatenate(late, axis=0).astype(BF16)
+
+
+def late_products(place, one, grads):
+    return pl.pallas_call(
+        late_kernel,
         out_shape=jax.ShapeDtypeStruct((PEERS, CHUNK_ROWS, LANES), BF16),
-        in_specs=[pl.BlockSpec(memory_space=SMEM)] + vmem(2 + len(grads)),
+        in_specs=[pl.BlockSpec(memory_space=SMEM)] + vmem(1 + len(grads)),
         out_specs=pl.BlockSpec(memory_space=VMEM),
         compiler_params=pltpu.CompilerParams(vmem_limit_bytes=24 << 20),
+        cost_estimate=pl.CostEstimate(flops=1 << 29, bytes_accessed=4 << 20, transcendentals=0),
+        name="late_products",
+    )(place, *grads, one)
+
+
+def one_kernel(rows_ref, other_rows_ref, one_ref, other_one_ref, late_ref, parts_ref):
+    chips = rows_ref.shape[0]
+    cap, hidden = one_ref.shape
+    count = hidden // PEERS
+    mine = pl.ds(0, cap)
+    theirs = pl.ds(cap, cap)
+    flipped = jnp.concatenate([one_ref[...].T, other_one_ref[...].T], axis=1)
+    for pair in range(chips // 2):
+        blocks = [
+            jnp.concatenate([rows_ref[chip, mine, :], other_rows_ref[chip, theirs, :]], axis=0)
+            for chip in (2 * pair, 2 * pair + 1)
+        ]
+        block = dot(flipped, jnp.concatenate(blocks, axis=1))
+        for peer in range(PEERS):
+            line = block[peer * count : (peer + 1) * count]
+            cell = jnp.concatenate([line[:, :LANES], line[:, LANES:]], axis=0)
+            parts_ref[peer, pl.ds(pair * 2 * SUB, 2 * SUB), :] = cell.astype(BF16)
+
+
+def one_products(rows, other_rows, one, other_one, late):
+    return pl.pallas_call(
+        one_kernel,
+        out_shape=jax.ShapeDtypeStruct(late.shape, BF16),
+        in_specs=vmem(5),
+        out_specs=pl.BlockSpec(memory_space=VMEM),
+        input_output_aliases={4: 0},
+        compiler_params=pltpu.CompilerParams(vmem_limit_bytes=24 << 20),
         cost_estimate=pl.CostEstimate(flops=1 << 30, bytes_accessed=8 << 20, transcendentals=0),
-        name="keep_products",
-    )(place, rows, one, *grads)
-
-
-def merge_kernel(keep_ref, other_ref, out_ref):
-    spot = pl.ds(0, ONE_ROWS)
-    out_ref[:, spot, :] = keep_ref[:, spot, :] + other_ref[...]
-
-
-def merge(keep, other):
-    return pl.pallas_call(
-        merge_kernel,
-        out_shape=jax.ShapeDtypeStruct(keep.shape, BF16),
-        in_specs=vmem(2),
-        out_specs=pl.BlockSpec(memory_space=VMEM),
-        input_output_aliases={0: 0},
-        compiler_params=pltpu.CompilerParams(vmem_limit_bytes=24 << 20),
-        name="merge",
-    )(keep, other)
+        name="one_products",
+    )(rows, other_rows, one, other_one, late)
 
 
 def owner_pass(place, seed_count, rows, w_own, w_other, bias_one, picks, targets, w_two, bias_two, w_three, bias_three,
@@ -452,23 +445,23 @@
     count = hidden // PEERS
     pieces = sems.shape[0] - 1
     step = hidden // pieces
-    copies = []
+    for peer in range(PEERS):
+        top[pl.ds(peer * count, count), :] = ref[peer].astype(F32)[SUB + TWO_ROWS :]
+    flipped = top[...].T
+    three[...] = flipped[:labels]
+    copies = [pltpu.make_async_copy(three, grad_three.at[side], sems.at[pieces])]
+    copies[0].start()
     for peer in range(PEERS):
         cells = ref[peer].astype(F32)
         for tile in range(hidden // LANES):
             two[pl.ds(peer * count, count), pl.ds(tile * LANES, LANES)] = cells[
                 SUB + tile * count : SUB + (tile + 1) * count
             ]
-        top[pl.ds(peer * count, count), :] = cells[SUB + TWO_ROWS :]
         done = (peer + 1) * count
         if done % step == 0:
             spot = pl.ds(done - step, step)
-            copies.append(pltpu.make_async_copy(two.at[spot], grad_two.at[side, spot], sems.at[len(copies)]))
+            copies.append(pltpu.make_async_copy(two.at[spot], grad_two.at[side, spot], sems.at[len(copies) - 1]))
             copies[-1].start()
-    flipped = top[...].T
-    three[...] = flipped[:labels]
-    copies.append(pltpu.make_async_copy(three, grad_three.at[side], sems.at[pieces]))
-    copies[-1].start()
     return flipped[labels:], copies
 
 
@@ -635,12 +628,13 @@
     slope_one, *grads, ship = owner_pass(
         place, seed_count, rows, w_own, w_other, bias_one, picks, targets, w_two, bias_two, w_three, bias_three, fans
     )
+    rows, ship = lax.optimization_barrier((rows, ship))
     ship = swap_core(ship)
-    send, one = send_products(slope_one, grads[0], picks[0], w_two, rows, fans[0])
-    send, ship = lax.optimization_barrier((send, ship))
-    other = swap_core(send)
-    keep = keep_products(place, rows, one, (*grads, ship))
-    parts = merge(keep, other)
+    other_rows = swap_core(rows)
+    one = first_grad(slope_one, grads[0], picks[0], w_two, fans[0])
+    other_one = swap_core(one)
+    late = late_products(place, one, (*grads, ship))
+    parts = one_products(rows, other_rows, one, other_one, late)
     sums = sum_parts(exchange(parts, SAME_CORE))
     own = exchange(sums, SAME_CORE)
     other = swap_core(own)

time: 112 us -> 112 us (level)
    ppermute x5 -> x6, starting transfers between devices: 7.62 us -> 8.02 us  [swap_core(): return lax.ppermute(values, 'core', [(0, 1), (1, 0)])]
  transfers between devices with their start and end apart: 6 -> 7, of which waited for: 3 -> 3; matrix products, arithmetic and copies ran while one was open for 0% -> 0% of each run, Pallas kernels for 17% -> 17%
where the time goes in v6:
time: 112 us
  blocking collectives  68.1 us (61%)
  Pallas kernels  25 us (22%)
  starting transfers between devices  14.2 us (13%)
  waiting for transfers between devices  3.35 us (3%)
    all_to_all x3, blocking collectives, exchange(): return lax.all_to_all(values, axes, 0, 0, tiled=True)  68.1 us
    pallas_call x1, Pallas kernels, gather_rows(): pl.pallas_call(gather_kernel, out_shape=jax.ShapeDtypeStruct((chips, 2 *...  13 us
    ppermute x6, starting transfers between devices, swap_core(): return lax.ppermute(values, 'core', [(0, 1), (1, 0)])  8.02 us
    all_to_all x1, starting transfers between devices, exchange(): return lax.all_to_all(values, axes, 0, 0, tiled=True)  6.14 us
    pallas_call x1, Pallas kernels, owner_pass(): pl.pallas_call(functools.partial(owner_kernel, *fans), out_shape=(jax.Sha...  3.39 us
  transfers between devices with their start and end apart: 7, of which 3 were waited for; matrix products, arithmetic and copies ran while one was open for 0% of the time, Pallas kernels for 17%

profile of v6, /device:TPU:1, one launch (start us, length us, event | category | flops | bytes accessed | tf_op | source)
XLA Modules:
  0.0 111.7 jit_solution(4116670988028946436)
XLA Ops:
  0.6 0.0 copy-start
  0.6 0.0 copy-start.13
  0.7 0.0 copy-start.2
  0.7 1.5 %collective-permute-start = (bf16[64,16384]{1,0:T(8,128)(2,1)}, bf16[64,16384]{1,0:T(8,128)(2,1)}, u32[]{:S(2)}, u32[]{:S(2)}) collective-permute-start(bf16[64,16384]{1,0:T(8,128)(2,1)} %own_ref.1), channel_id=1, source_target_pairs={{0,1},{1,0},{2,3},{3,2},{4,5},{5,4},{6,7},{7,6},{8,9},{9,8},{10,11... | collective-permute-start | bytes 6291464 | tf_op jit(solution)/shard_map/ppermute | solution.py:593
  2.2 1.9 %spread.1 = bf16[8,128,512]{2,1,0:T(8,128)(2,1)} custom-call(bf16[128,512]{1,0:T(8,128)(2,1)} %bitcast.22), custom_call_target="tpu_custom_call" | custom-call | tf_op jit(solution)/shard_map/spread/pallas_call | solution.py:186
  4.1 6.1 %all-to-all-start = ((bf16[8,128,512]{2,1,0:T(8,128)(2,1)}), bf16[8,128,512]{2,1,0:T(8,128)(2,1)}, u32[]{:S(2)}, u32[]{:S(2)}) async-start(bf16[8,128,512]{2,1,0:T(8,128)(2,1)} %spread.1), calls=%async_computation | async-start | bytes 2097152 | tf_op jit(solution)/shard_map/all_to_all | solution.py:589
  10.2 0.0 copy-done.13
  10.3 0.1 pad_add_fusion.place_ref
  10.4 0.0 copy-start.3
  10.4 0.0 copy-start.4
  10.4 0.0 copy-start.5
  10.4 0.0 copy-start.6
  10.4 0.0 collective-permute-done.other_ref
  10.4 0.0 copy-done
  10.4 0.0 copy-done.2
  10.4 13.0 %gather_rows.1 = bf16[8,512,128]{2,1,0:T(8,128)(2,1)S(1)} custom-call(s32[2]{0:T(128)S(1)} %pad_add_fusion.place_ref, bf16[64,16384]{1,0:T(8,128)(2,1)S(1)} %copy-done, bf16[64,16384]{1,0:T(8,128)(2,1)} %collective-permute-done.other_ref, s32[4096]{0:T(1024)S(1)} %copy-done.2, s32[20480]{0:T(1024)S(1)} %reshape.46.near_ref), custom_call_target="tpu_custom_call" | custom-call | flops 134217728 | bytes 41943040 | tf_op jit(solution)/shard_map/gather_rows/pallas_call | solution.py:156
  23.4 0.0 copy-start.1
  23.4 0.0 copy-start.7
  23.4 0.0 copy-start.8
  23.4 0.0 copy-start.9
  23.4 0.0 copy-start.10
  23.5 0.0 copy-start.11
  23.5 0.0 copy-start.12
  23.5 0.0 copy-done.3
  23.5 0.0 copy-done.4
  23.5 0.0 copy-done.5
  23.5 0.0 copy-done.6
  23.5 0.4 make_picks.1
  23.9 1.9 %all-to-all-done.w_own_ref = bf16[8,128,512]{2,1,0:T(8,128)(2,1)} async-done(((bf16[8,128,512]{2,1,0:T(8,128)(2,1)}), bf16[8,128,512]{2,1,0:T(8,128)(2,1)}, u32[]{:S(2)}, u32[]{:S(2)}) %all-to-all-start) | async-done | bytes 1048608 | tf_op jit(solution)/shard_map/all_to_all | solution.py:589
  25.8 1.3 %collective-permute-start.1 = (bf16[8,128,512]{2,1,0:T(8,128)(2,1)}, bf16[8,128,512]{2,1,0:T(8,128)(2,1)S(1)}, u32[]{:S(2)}, u32[]{:S(2)}) collective-permute-start(bf16[8,128,512]{2,1,0:T(8,128)(2,1)} %all-to-all-done.w_own_ref), channel_id=1, source_target_pairs={{0,1},{1,0},{2,3},{3,2},{4,5},{5,4},{6,7},{7,6},{8,9},{9,8},{10,11... | collective-permute-start | bytes 3145736 | tf_op jit(solution)/shard_map/ppermute | solution.py:593
  27.0 18.1 %all_to_all.20.rows_ref = bf16[8,512,128]{2,1,0:T(8,128)(2,1)S(1)} all-to-all(bf16[8,512,128]{2,1,0:T(8,128)(2,1)S(1)} %gather_rows.1), channel_id=1, replica_groups=mesh['y_hi'=2,'x'=4,'z'=4,'y_lo'=2,'core'=2] {'z','y_lo'}, dimensions={0} | all-to-all | bytes 2097152 | tf_op jit(solution)/shard_map/all_to_all | solution.py:589
  45.1 0.0 collective-permute-done.1.w_other_ref
  45.1 0.0 copy-done.1
  45.1 0.0 copy-done.7
  45.1 0.0 copy-done.8
  45.2 0.0 copy-done.9
  45.2 0.0 copy-done.10
  45.2 0.0 copy-done.11
  45.2 0.0 copy-done.12
  45.2 3.4 %owner_pass.1 = (f32[256,512]{1,0:T(8,128)S(1)}, bf16[128,512]{1,0:T(8,128)(2,1)S(1)}, bf16[2,128,512]{2,1,0:T(8,128)(2,1)S(1)}, bf16[2,32,512]{2,1,0:T(8,128)(2...) custom-call(s32[2]{0:T(128)S(1)} %pad_add_fusion.place_ref, s32[128]{0:T(128)S(1)} %copy-done.11, ...), custom_call_target="tpu_custom_call" | custom-call | flops 2147483648 | bytes 10485760 | tf_op jit(solution)/shard_map/owner_pass/pallas_call | solution.py:398
  48.6 1.2 %collective-permute-start.2 = (bf16[8,512,128]{2,1,0:T(8,128)(2,1)S(1)}, bf16[8,512,128]{2,1,0:T(8,128)(2,1)S(1)}, u32[]{:S(2)}, u32[]{:S(2)}) collective-permute-start(bf16[8,512,128]{2,1,0:T(8,128)(2,1)S(1)} %all_to_all.20.rows_ref), channel_id=1, source_target_pairs={{0,1},{1,0},{2,3},{3,2},{4,5},{5,4},{6,7},{7,6},{8,9},{9,8},{10,11... | collective-permute-start | bytes 3145736 | tf_op jit(solution)/shard_map/ppermute | solution.py:593
  49.8 0.1 collective-permute-start.4
  49.9 0.7 first_grad.1.one_ref
  50.6 0.5 collective-permute-start.3
  51.2 1.4 %collective-permute-done.4.ship_ref = bf16[320,512]{1,0:T(8,128)(2,1)S(1)} collective-permute-done((bf16[320,512]{1,0:T(8,128)(2,1)S(1)}, bf16[320,512]{1,0:T(8,128)(2,1)S(1)}, u32[]{:S(2)}, u32[]{:S(2)}) %collective-permute-start.4) | collective-permute-done | bytes 327712 | tf_op jit(solution)/shard_map/ppermute | solution.py:593
  52.6 1.0 late_products.1.late_ref
  53.5 0.0 collective-permute-done.3.other_one_ref
  53.6 0.0 collective-permute-done.2.other_rows_ref
  53.6 0.7 one_products.1
  54.3 31.3 %all_to_all.21.parts_ref = bf16[64,104,128]{2,1,0:T(8,128)(2,1)S(1)} all-to-all(bf16[64,104,128]{2,1,0:T(8,128)(2,1)S(1)} %one_products.1), channel_id=1, replica_groups=mesh['y_hi'=2,'x'=4,'z'=4,'y_lo'=2,'core'=2] {'y_hi','x','z','y_lo'}, dimensions={0} | all-to-all | bytes 3407872 | tf_op jit(solution)/shard_map/all_to_all | solution.py:589
  85.6 0.3 sum_parts.1
  85.9 18.7 %all_to_all.22.own_ref = bf16[64,48,128]{2,1,0:T(8,128)(2,1)S(1)} all-to-all(bf16[64,48,128]{2,1,0:T(8,128)(2,1)S(1)} %sum_parts.1), channel_id=1, replica_groups=mesh['y_hi'=2,'x'=4,'z'=4,'y_lo'=2,'core'=2] {'y_hi','x','z','y_lo'}, dimensions={0} | all-to-all | bytes 1572864 | tf_op jit(solution)/shard_map/all_to_all | solution.py:589
  104.6 3.4 %collective-permute-start.5 = (bf16[64,48,128]{2,1,0:T(8,128)(2,1)S(1)}, bf16[64,48,128]{2,1,0:T(8,128)(2,1)S(1)}, u32[]{:S(2)}, u32[]{:S(2)}) collective-permute-start(bf16[64,48,128]{2,1,0:T(8,128)(2,1)S(1)} %all_to_all.22.own_ref), channel_id=1, source_target_pairs={{0,1},{1,0},{2,3},{3,2},{4,5},{5,4},{6,7},{7,6},{8,9},{9,8},{10,11... | collective-permute-start | bytes 2359304 | tf_op jit(solution)/shard_map/ppermute | solution.py:593
  108.0 1.8 %unpack_own.1 = (f32[2,64,512]{2,1,0:T(8,128)}, f32[2,512,512]{2,1,0:T(8,128)}, f32[2,112,512]{2,1,0:T(8,128)}, f32[16,512]{1,0:T(8,128)S(1)}) custom-call(s32[2]{0:T(128)S(1)} %pad_add_fusion.place_ref, bf16[64,48,128]{2,1,0:T(8,128)(2,1)S(1)} %all_to_all.22.own_ref), custom_call_target="tpu_custom_call" | custom-call | flops 4194304 | bytes 4194304 | tf_op jit(solution)/shard_map/unpack_own/pallas_call | solution.py:532
  109.9 0.1 collective-permute-done.5.other_ref
  110.0 1.8 %unpack_other.1 = (f32[2,512,512]{2,1,0:T(8,128)}, f32[2,112,512]{2,1,0:T(8,128)}, f32[1,512]{1,0:T(1,128)}, f32[1,512]{1,0:T(1,128)}, f32[1,112]{1,0:T(1,128)}) custom-call(s32[2]{0:T(128)S(1)} %pad_add_fusion.place_ref, bf16[64,48,128]{2,1,0:T(8,128)(2,1)S(1)} %collective-permute-done.5.other_ref, ...), custom_call_target="tpu_custom_call", output_to_operand_aliasing={{0}: (3, {}), {1}: (4, {})} | custom-call | tf_op jit(solution)/shard_map/unpack_other/pallas_call | solution.py:561
  (1 shorter events, 0.0 us)
Async XLA Ops:
  0.6 9.8 %copy-start = (bf16[64,16384]{1,0:T(8,128)(2,1)S(1)}, bf16[64,16384]{1,0:T(8,128)(2,1)}, u32[]{:S(2)}) copy-start(bf16[64,16384]{1,0:T(8,128)(2,1)} %own_ref.1) | copy-start | bytes 6291460
  0.6 9.6 %copy-start.13 = (s32[5,4096]{1,0:T(8,128)S(1)}, s32[5,4096]{1,0:T(8,128)}, u32[]{:S(2)}) copy-start(s32[5,4096]{1,0:T(8,128)} %param.17) | copy-start | bytes 245764
  0.7 9.8 %copy-start.2 = (s32[4096]{0:T(1024)S(1)}, s32[4096]{0:T(1024)}, u32[]{:S(2)}) copy-start(s32[4096]{0:T(1024)} %self_ref.1) | copy-start | bytes 49156
  0.7 9.7 %collective-permute-start = (bf16[64,16384]{1,0:T(8,128)(2,1)}, bf16[64,16384]{1,0:T(8,128)(2,1)}, u32[]{:S(2)}, u32[]{:S(2)}) collective-permute-start(bf16[64,16384]{1,0:T(8,128)(2,1)} %own_ref.1), channel_id=1, source_target_pairs={{0,1},{1,0},{2,3},{3,2},{4,5},{5,4},{6,7},{7,6},{8,9},{9,8},{10,11... | collective-permute-start | bytes 6291464 | tf_op jit(solution)/shard_map/ppermute | solution.py:593
  4.1 21.7 %all-to-all-start = ((bf16[8,128,512]{2,1,0:T(8,128)(2,1)}), bf16[8,128,512]{2,1,0:T(8,128)(2,1)}, u32[]{:S(2)}, u32[]{:S(2)}) async-start(bf16[8,128,512]{2,1,0:T(8,128)(2,1)} %spread.1), calls=%async_computation | async-start | bytes 2097152 | tf_op jit(solution)/shard_map/all_to_all | solution.py:589
  10.4 13.1 %copy-start.3 = (s32[10,128]{1,0:T(8,128)S(1)}, s32[10,128]{1,0:T(8,128)}, u32[]{:S(2)}) copy-start(s32[10,128]{1,0:T(8,128)} %near_two_ref.1) | copy-start | bytes 15364
  10.4 13.1 %copy-start.4 = (s32[15,32]{1,0:T(8,128)S(1)}, s32[15,32]{1,0:T(8,128)}, u32[]{:S(2)}) copy-start(s32[15,32]{1,0:T(8,128)} %near_three_ref.1) | copy-start | bytes 5764
  10.4 13.1 %copy-start.5 = (s32[128]{0:T(128)S(1)}, s32[128]{0:T(128)}, u32[]{:S(2)}) copy-start(s32[128]{0:T(128)} %param.18) | copy-start | bytes 1540
  10.4 13.1 %copy-start.6 = (s32[32]{0:T(128)S(1)}, s32[32]{0:T(128)}, u32[]{:S(2)}) copy-start(s32[32]{0:T(128)} %param.20) | copy-start | bytes 388
  23.4 21.7 %copy-start.1 = (bf16[2,512,512]{2,1,0:T(8,128)(2,1)S(1)}, bf16[2,512,512]{2,1,0:T(8,128)(2,1)}, u32[]{:S(2)}) copy-start(bf16[2,512,512]{2,1,0:T(8,128)(2,1)} %w_two_ref.3) | copy-start | bytes 3145732
  23.4 21.7 %copy-start.7 = (bf16[2,512,112]{1,2,0:T(8,128)(2,1)S(1)}, bf16[2,512,112]{1,2,0:T(8,128)(2,1)}, u32[]{:S(2)}) copy-start(bf16[2,512,112]{1,2,0:T(8,128)(2,1)} %param.28) | copy-start | bytes 688132
  23.4 21.7 %copy-start.8 = (s32[32,112]{1,0:T(8,128)S(1)}, s32[32,112]{1,0:T(8,128)}, u32[]{:S(2)}) copy-start(s32[32,112]{1,0:T(8,128)} %targets_ref.1) | copy-start | bytes 43012
  23.4 21.7 %copy-start.9 = (f32[512]{0:T(512)S(1)}, f32[512]{0:T(512)}, u32[]{:S(2)}) copy-start(f32[512]{0:T(512)} %param.25) | copy-start | bytes 6148
  23.4 21.7 %copy-start.10 = (f32[512]{0:T(512)S(1)}, f32[512]{0:T(512)}, u32[]{:S(2)}) copy-start(f32[512]{0:T(512)} %param.27) | copy-start | bytes 6148
  23.5 21.7 %copy-start.11 = (s32[128]{0:T(128)S(1)}, s32[128]{0:T(128)}, u32[]{:S(2)}) copy-start(s32[128]{0:T(128)} %count_ref.1) | copy-start | bytes 1540
  23.5 21.7 %copy-start.12 = (f32[112]{0:T(128)S(1)}, f32[112]{0:T(128)}, u32[]{:S(2)}) copy-start(f32[112]{0:T(128)} %param.29) | copy-start | bytes 1348
  25.8 19.4 %collective-permute-start.1 = (bf16[8,128,512]{2,1,0:T(8,128)(2,1)}, bf16[8,128,512]{2,1,0:T(8,128)(2,1)S(1)}, u32[]{:S(2)}, u32[]{:S(2)}) collective-permute-start(bf16[8,128,512]{2,1,0:T(8,128)(2,1)} %all-to-all-done.w_own_ref), channel_id=1, source_target_pairs={{0,1},{1,0},{2,3},{3,2},{4,5},{5,4},{6,7},{7,6},{8,9},{9,8},{10,11... | collective-permute-start | bytes 3145736 | tf_op jit(solution)/shard_map/ppermute | solution.py:593
  48.6 5.0 %collective-permute-start.2 = (bf16[8,512,128]{2,1,0:T(8,128)(2,1)S(1)}, bf16[8,512,128]{2,1,0:T(8,128)(2,1)S(1)}, u32[]{:S(2)}, u32[]{:S(2)}) collective-permute-start(bf16[8,512,128]{2,1,0:T(8,128)(2,1)S(1)} %all_to_all.20.rows_ref), channel_id=1, source_target_pairs={{0,1},{1,0},{2,3},{3,2},{4,5},{5,4},{6,7},{7,6},{8,9},{9,8},{10,11... | collective-permute-start | bytes 3145736 | tf_op jit(solution)/shard_map/ppermute | solution.py:593
  49.8 2.8 %collective-permute-start.4 = (bf16[320,512]{1,0:T(8,128)(2,1)S(1)}, bf16[320,512]{1,0:T(8,128)(2,1)S(1)}, u32[]{:S(2)}, u32[]{:S(2)}) collective-permute-start(bf16[320,512]{1,0:T(8,128)(2,1)S(1)} %get-tuple-element.54), channel_id=1, source_target_pairs={{0,1},{1,0},{2,3},{3,2},{4,5},{5,4},{6,7},{7,6},{8,9},{9,8},{10,11... | collective-permute-start | bytes 983048 | tf_op jit(solution)/shard_map/ppermute | solution.py:593
  50.6 2.9 %collective-permute-start.3 = (bf16[256,512]{1,0:T(8,128)(2,1)S(1)}, bf16[256,512]{1,0:T(8,128)(2,1)S(1)}, u32[]{:S(2)}, u32[]{:S(2)}) collective-permute-start(bf16[256,512]{1,0:T(8,128)(2,1)S(1)} %first_grad.1.one_ref), channel_id=1, source_target_pairs={{0,1},{1,0},{2,3},{3,2},{4,5},{5,4},{6,7},{7,6},{8,9},{9,8},{10,11... | collective-permute-start | bytes 786440 | tf_op jit(solution)/shard_map/ppermute | solution.py:593
  104.6 5.3 %collective-permute-start.5 = (bf16[64,48,128]{2,1,0:T(8,128)(2,1)S(1)}, bf16[64,48,128]{2,1,0:T(8,128)(2,1)S(1)}, u32[]{:S(2)}, u32[]{:S(2)}) collective-permute-start(bf16[64,48,128]{2,1,0:T(8,128)(2,1)S(1)} %all_to_all.22.own_ref), channel_id=1, source_target_pairs={{0,1},{1,0},{2,3},{3,2},{4,5},{5,4},{6,7},{7,6},{8,9},{9,8},{10,11... | collective-permute-start | bytes 2359304 | tf_op jit(solution)/shard_map/ppermute | solution.py:593

commit v7 on v6

--- a/solution.py
+++ b/solution.py
@@ -16,8 +16,8 @@
 LANES = 128
 SUB = 8
 SPARE = 16
-GATHER_UNROLL = 32
-TABLE_PIECES = 8
+GATHER_UNROLL = 64
+TABLE_PIECES = 16
 ONE_ROWS = 64
 TWO_ROWS = 32
 TOP_ROWS = 8
@@ -624,13 +624,13 @@
     w_own, rows, picks = lax.optimization_barrier((w_own, rows, picks))
     w_other = swap_core(w_own)
     rows = exchange(rows, CHIPS)
+    rows, w_own, w_other = lax.optimization_barrier((rows, w_own, w_other))
+    other_rows = swap_core(rows)
     fans = (near_two.shape[0], near_three.shape[0])
     slope_one, *grads, ship = owner_pass(
         place, seed_count, rows, w_own, w_other, bias_one, picks, targets, w_two, bias_two, w_three, bias_three, fans
     )
-    rows, ship = lax.optimization_barrier((rows, ship))
     ship = swap_core(ship)
-    other_rows = swap_core(rows)
     one = first_grad(slope_one, grads[0], picks[0], w_two, fans[0])
     other_one = swap_core(one)
     late = late_products(place, one, (*grads, ship))

time: 112 us -> 111 us (level)
  transfers between devices with their start and end apart: 7 -> 7, of which waited for: 3 -> 3; matrix products, arithmetic and copies ran while one was open for 0% -> 0% of each run, Pallas kernels for 17% -> 20%
where the time goes in v7:
time: 111 us
  blocking collectives  68.8 us (62%)
  Pallas kernels  24.8 us (22%)
  starting transfers between devices  13.7 us (12%)
  waiting for transfers between devices  2.43 us (2%)
    all_to_all x3, blocking collectives, exchange(): return lax.all_to_all(values, axes, 0, 0, tiled=True)  68.8 us
    pallas_call x1, Pallas kernels, gather_rows(): pl.pallas_call(gather_kernel, out_shape=jax.ShapeDtypeStruct((chips, 2 *...  12.8 us
    ppermute x6, starting transfers between devices, swap_core(): return lax.ppermute(values, 'core', [(0, 1), (1, 0)])  7.53 us
    all_to_all x1, starting transfers between devices, exchange(): return lax.all_to_all(values, axes, 0, 0, tiled=True)  6.14 us
    pallas_call x1, Pallas kernels, owner_pass(): pl.pallas_call(functools.partial(owner_kernel, *fans), out_shape=(jax.Sha...  3.39 us
  transfers between devices with their start and end apart: 7, of which 3 were waited for; matrix products, arithmetic and copies ran while one was open for 0% of the time, Pallas kernels for 20%

profile of v7, /device:TPU:1, one launch (start us, length us, event | category | flops | bytes accessed | tf_op | source)
XLA Modules:
  0.0 110.8 jit_solution(5034065522352550957)
XLA Ops:
  0.6 0.0 copy-start
  0.6 0.0 copy-start.13
  0.7 0.0 copy-start.2
  0.7 1.5 %collective-permute-start = (bf16[64,16384]{1,0:T(8,128)(2,1)}, bf16[64,16384]{1,0:T(8,128)(2,1)}, u32[]{:S(2)}, u32[]{:S(2)}) collective-permute-start(bf16[64,16384]{1,0:T(8,128)(2,1)} %own_ref.1), channel_id=1, source_target_pairs={{0,1},{1,0},{2,3},{3,2},{4,5},{5,4},{6,7},{7,6},{8,9},{9,8},{10,11... | collective-permute-start | bytes 6291464 | tf_op jit(solution)/shard_map/ppermute | solution.py:593
  2.2 1.9 %spread.1 = bf16[8,128,512]{2,1,0:T(8,128)(2,1)} custom-call(bf16[128,512]{1,0:T(8,128)(2,1)} %bitcast.22), custom_call_target="tpu_custom_call" | custom-call | tf_op jit(solution)/shard_map/spread/pallas_call | solution.py:186
  4.1 6.1 %all-to-all-start = ((bf16[8,128,512]{2,1,0:T(8,128)(2,1)}), bf16[8,128,512]{2,1,0:T(8,128)(2,1)}, u32[]{:S(2)}, u32[]{:S(2)}) async-start(bf16[8,128,512]{2,1,0:T(8,128)(2,1)} %spread.1), calls=%async_computation | async-start | bytes 2097152 | tf_op jit(solution)/shard_map/all_to_all | solution.py:589
  10.2 0.0 copy-done.13
  10.3 0.1 pad_add_fusion.place_ref
  10.4 0.0 copy-start.3
  10.4 0.0 copy-start.4
  10.4 0.0 copy-start.5
  10.4 0.0 copy-start.6
  10.4 0.0 collective-permute-done.other_ref
  10.4 0.0 copy-done
  10.4 0.0 copy-done.2
  10.4 12.8 %gather_rows.1 = bf16[8,512,128]{2,1,0:T(8,128)(2,1)S(1)} custom-call(s32[2]{0:T(128)S(1)} %pad_add_fusion.place_ref, bf16[64,16384]{1,0:T(8,128)(2,1)S(1)} %copy-done, bf16[64,16384]{1,0:T(8,128)(2,1)} %collective-permute-done.other_ref, s32[4096]{0:T(1024)S(1)} %copy-done.2, s32[20480]{0:T(1024)S(1)} %reshape.46.near_ref), custom_call_target="tpu_custom_call" | custom-call | flops 134217728 | bytes 41943040 | tf_op jit(solution)/shard_map/gather_rows/pallas_call | solution.py:156
  23.2 0.0 copy-start.1
  23.2 0.0 copy-start.7
  23.2 0.0 copy-start.8
  23.2 0.0 copy-start.9
  23.2 0.0 copy-start.10
  23.3 0.0 copy-start.11
  23.3 0.0 copy-start.12
  23.3 0.0 copy-done.3
  23.3 0.0 copy-done.4
  23.3 0.0 copy-done.5
  23.3 0.0 copy-done.6
  23.3 0.4 make_picks.1
  23.7 2.1 %all-to-all-done.w_own_ref = bf16[8,128,512]{2,1,0:T(8,128)(2,1)} async-done(((bf16[8,128,512]{2,1,0:T(8,128)(2,1)}), bf16[8,128,512]{2,1,0:T(8,128)(2,1)}, u32[]{:S(2)}, u32[]{:S(2)}) %all-to-all-start) | async-done | bytes 1048608 | tf_op jit(solution)/shard_map/all_to_all | solution.py:589
  25.8 1.3 %collective-permute-start.1 = (bf16[8,128,512]{2,1,0:T(8,128)(2,1)}, bf16[8,128,512]{2,1,0:T(8,128)(2,1)S(1)}, u32[]{:S(2)}, u32[]{:S(2)}) collective-permute-start(bf16[8,128,512]{2,1,0:T(8,128)(2,1)} %all-to-all-done.w_own_ref), channel_id=1, source_target_pairs={{0,1},{1,0},{2,3},{3,2},{4,5},{5,4},{6,7},{7,6},{8,9},{9,8},{10,11... | collective-permute-start | bytes 3145736 | tf_op jit(solution)/shard_map/ppermute | solution.py:593
  27.0 18.0 %all_to_all.20.rows_ref = bf16[8,512,128]{2,1,0:T(8,128)(2,1)S(1)} all-to-all(bf16[8,512,128]{2,1,0:T(8,128)(2,1)S(1)} %gather_rows.1), channel_id=1, replica_groups=mesh['y_hi'=2,'x'=4,'z'=4,'y_lo'=2,'core'=2] {'z','y_lo'}, dimensions={0} | all-to-all | bytes 2097152 | tf_op jit(solution)/shard_map/all_to_all | solution.py:589
  45.0 0.0 collective-permute-done.1.w_other_ref
  45.0 1.1 collective-permute-start.2
  46.1 0.0 copy-done.1
  46.1 0.0 copy-done.7
  46.1 0.0 copy-done.8
  46.1 0.0 copy-done.9
  46.1 0.0 copy-done.10
  46.1 0.0 copy-done.11
  46.1 0.0 copy-done.12
  46.2 3.4 %owner_pass.1 = (f32[256,512]{1,0:T(8,128)S(1)}, bf16[128,512]{1,0:T(8,128)(2,1)S(1)}, bf16[2,128,512]{2,1,0:T(8,128)(2,1)S(1)}, bf16[2,32,512]{2,1,0:T(8,128)(2...) custom-call(s32[2]{0:T(128)S(1)} %pad_add_fusion.place_ref, s32[128]{0:T(128)S(1)} %copy-done.11, ...), custom_call_target="tpu_custom_call" | custom-call | flops 2147483648 | bytes 10485760 | tf_op jit(solution)/shard_map/owner_pass/pallas_call | solution.py:398
  49.6 0.1 collective-permute-start.4
  49.7 0.7 first_grad.1.one_ref
  50.4 0.6 collective-permute-start.3
  51.0 0.3 collective-permute-done.4.ship_ref
  51.3 1.0 late_products.1.late_ref
  52.2 0.0 collective-permute-done.3.other_one_ref
  52.3 0.0 collective-permute-done.2.other_rows_ref
  52.3 0.8 one_products.1
  53.0 31.3 %all_to_all.21.parts_ref = bf16[64,104,128]{2,1,0:T(8,128)(2,1)S(1)} all-to-all(bf16[64,104,128]{2,1,0:T(8,128)(2,1)S(1)} %one_products.1), channel_id=1, replica_groups=mesh['y_hi'=2,'x'=4,'z'=4,'y_lo'=2,'core'=2] {'y_hi','x','z','y_lo'}, dimensions={0} | all-to-all | bytes 3407872 | tf_op jit(solution)/shard_map/all_to_all | solution.py:589
  84.3 0.3 sum_parts.1
  84.6 19.5 %all_to_all.22.own_ref = bf16[64,48,128]{2,1,0:T(8,128)(2,1)S(1)} all-to-all(bf16[64,48,128]{2,1,0:T(8,128)(2,1)S(1)} %sum_parts.1), channel_id=1, replica_groups=mesh['y_hi'=2,'x'=4,'z'=4,'y_lo'=2,'core'=2] {'y_hi','x','z','y_lo'}, dimensions={0} | all-to-all | bytes 1572864 | tf_op jit(solution)/shard_map/all_to_all | solution.py:589
  104.1 3.0 %collective-permute-start.5 = (bf16[64,48,128]{2,1,0:T(8,128)(2,1)S(1)}, bf16[64,48,128]{2,1,0:T(8,128)(2,1)S(1)}, u32[]{:S(2)}, u32[]{:S(2)}) collective-permute-start(bf16[64,48,128]{2,1,0:T(8,128)(2,1)S(1)} %all_to_all.22.own_ref), channel_id=1, source_target_pairs={{0,1},{1,0},{2,3},{3,2},{4,5},{5,4},{6,7},{7,6},{8,9},{9,8},{10,11... | collective-permute-start | bytes 2359304 | tf_op jit(solution)/shard_map/ppermute | solution.py:593
  107.1 1.8 %unpack_own.1 = (f32[2,64,512]{2,1,0:T(8,128)}, f32[2,512,512]{2,1,0:T(8,128)}, f32[2,112,512]{2,1,0:T(8,128)}, f32[16,512]{1,0:T(8,128)S(1)}) custom-call(s32[2]{0:T(128)S(1)} %pad_add_fusion.place_ref, bf16[64,48,128]{2,1,0:T(8,128)(2,1)S(1)} %all_to_all.22.own_ref), custom_call_target="tpu_custom_call" | custom-call | flops 4194304 | bytes 4194304 | tf_op jit(solution)/shard_map/unpack_own/pallas_call | solution.py:532
  109.0 0.1 collective-permute-done.5.other_ref
  109.0 1.8 %unpack_other.1 = (f32[2,512,512]{2,1,0:T(8,128)}, f32[2,112,512]{2,1,0:T(8,128)}, f32[1,512]{1,0:T(1,128)}, f32[1,512]{1,0:T(1,128)}, f32[1,112]{1,0:T(1,128)}) custom-call(s32[2]{0:T(128)S(1)} %pad_add_fusion.place_ref, bf16[64,48,128]{2,1,0:T(8,128)(2,1)S(1)} %collective-permute-done.5.other_ref, ...), custom_call_target="tpu_custom_call", output_to_operand_aliasing={{0}: (3, {}), {1}: (4, {})} | custom-call | tf_op jit(solution)/shard_map/unpack_other/pallas_call | solution.py:561
  (1 shorter events, 0.0 us)
Async XLA Ops:
  0.6 9.8 %copy-start = (bf16[64,16384]{1,0:T(8,128)(2,1)S(1)}, bf16[64,16384]{1,0:T(8,128)(2,1)}, u32[]{:S(2)}) copy-start(bf16[64,16384]{1,0:T(8,128)(2,1)} %own_ref.1) | copy-start | bytes 6291460
  0.6 9.6 %copy-start.13 = (s32[5,4096]{1,0:T(8,128)S(1)}, s32[5,4096]{1,0:T(8,128)}, u32[]{:S(2)}) copy-start(s32[5,4096]{1,0:T(8,128)} %param.17) | copy-start | bytes 245764
  0.7 9.8 %copy-start.2 = (s32[4096]{0:T(1024)S(1)}, s32[4096]{0:T(1024)}, u32[]{:S(2)}) copy-start(s32[4096]{0:T(1024)} %self_ref.1) | copy-start | bytes 49156
  0.7 9.7 %collective-permute-start = (bf16[64,16384]{1,0:T(8,128)(2,1)}, bf16[64,16384]{1,0:T(8,128)(2,1)}, u32[]{:S(2)}, u32[]{:S(2)}) collective-permute-start(bf16[64,16384]{1,0:T(8,128)(2,1)} %own_ref.1), channel_id=1, source_target_pairs={{0,1},{1,0},{2,3},{3,2},{4,5},{5,4},{6,7},{7,6},{8,9},{9,8},{10,11... | collective-permute-start | bytes 6291464 | tf_op jit(solution)/shard_map/ppermute | solution.py:593
  4.1 21.7 %all-to-all-start = ((bf16[8,128,512]{2,1,0:T(8,128)(2,1)}), bf16[8,128,512]{2,1,0:T(8,128)(2,1)}, u32[]{:S(2)}, u32[]{:S(2)}) async-start(bf16[8,128,512]{2,1,0:T(8,128)(2,1)} %spread.1), calls=%async_computation | async-start | bytes 2097152 | tf_op jit(solution)/shard_map/all_to_all | solution.py:589
  10.4 12.9 %copy-start.3 = (s32[10,128]{1,0:T(8,128)S(1)}, s32[10,128]{1,0:T(8,128)}, u32[]{:S(2)}) copy-start(s32[10,128]{1,0:T(8,128)} %near_two_ref.1) | copy-start | bytes 15364
  10.4 12.9 %copy-start.4 = (s32[15,32]{1,0:T(8,128)S(1)}, s32[15,32]{1,0:T(8,128)}, u32[]{:S(2)}) copy-start(s32[15,32]{1,0:T(8,128)} %near_three_ref.1) | copy-start | bytes 5764
  10.4 12.9 %copy-start.5 = (s32[128]{0:T(128)S(1)}, s32[128]{0:T(128)}, u32[]{:S(2)}) copy-start(s32[128]{0:T(128)} %param.18) | copy-start | bytes 1540
  10.4 12.9 %copy-start.6 = (s32[32]{0:T(128)S(1)}, s32[32]{0:T(128)}, u32[]{:S(2)}) copy-start(s32[32]{0:T(128)} %param.20) | copy-start | bytes 388
  23.2 22.9 %copy-start.1 = (bf16[2,512,512]{2,1,0:T(8,128)(2,1)S(1)}, bf16[2,512,512]{2,1,0:T(8,128)(2,1)}, u32[]{:S(2)}) copy-start(bf16[2,512,512]{2,1,0:T(8,128)(2,1)} %w_two_ref.3) | copy-start | bytes 3145732
  23.2 22.9 %copy-start.7 = (bf16[2,512,112]{1,2,0:T(8,128)(2,1)S(1)}, bf16[2,512,112]{1,2,0:T(8,128)(2,1)}, u32[]{:S(2)}) copy-start(bf16[2,512,112]{1,2,0:T(8,128)(2,1)} %param.28) | copy-start | bytes 688132
  23.2 22.9 %copy-start.8 = (s32[32,112]{1,0:T(8,128)S(1)}, s32[32,112]{1,0:T(8,128)}, u32[]{:S(2)}) copy-start(s32[32,112]{1,0:T(8,128)} %targets_ref.1) | copy-start | bytes 43012
  23.2 22.9 %copy-start.9 = (f32[512]{0:T(512)S(1)}, f32[512]{0:T(512)}, u32[]{:S(2)}) copy-start(f32[512]{0:T(512)} %param.25) | copy-start | bytes 6148
  23.2 22.9 %copy-start.10 = (f32[512]{0:T(512)S(1)}, f32[512]{0:T(512)}, u32[]{:S(2)}) copy-start(f32[512]{0:T(512)} %param.27) | copy-start | bytes 6148
  23.3 22.9 %copy-start.11 = (s32[128]{0:T(128)S(1)}, s32[128]{0:T(128)}, u32[]{:S(2)}) copy-start(s32[128]{0:T(128)} %count_ref.1) | copy-start | bytes 1540
  23.3 22.9 %copy-start.12 = (f32[112]{0:T(128)S(1)}, f32[112]{0:T(128)}, u32[]{:S(2)}) copy-start(f32[112]{0:T(128)} %param.29) | copy-start | bytes 1348
  25.8 19.3 %collective-permute-start.1 = (bf16[8,128,512]{2,1,0:T(8,128)(2,1)}, bf16[8,128,512]{2,1,0:T(8,128)(2,1)S(1)}, u32[]{:S(2)}, u32[]{:S(2)}) collective-permute-start(bf16[8,128,512]{2,1,0:T(8,128)(2,1)} %all-to-all-done.w_own_ref), channel_id=1, source_target_pairs={{0,1},{1,0},{2,3},{3,2},{4,5},{5,4},{6,7},{7,6},{8,9},{9,8},{10,11... | collective-permute-start | bytes 3145736 | tf_op jit(solution)/shard_map/ppermute | solution.py:593
  45.0 7.2 %collective-permute-start.2 = (bf16[8,512,128]{2,1,0:T(8,128)(2,1)S(1)}, bf16[8,512,128]{2,1,0:T(8,128)(2,1)S(1)}, u32[]{:S(2)}, u32[]{:S(2)}) collective-permute-start(bf16[8,512,128]{2,1,0:T(8,128)(2,1)S(1)} %all_to_all.20.rows_ref), channel_id=1, source_target_pairs={{0,1},{1,0},{2,3},{3,2},{4,5},{5,4},{6,7},{7,6},{8,9},{9,8},{10,11... | collective-permute-start | bytes 3145736 | tf_op jit(solution)/shard_map/ppermute | solution.py:593
  49.6 1.7 %collective-permute-start.4 = (bf16[320,512]{1,0:T(8,128)(2,1)S(1)}, bf16[320,512]{1,0:T(8,128)(2,1)S(1)}, u32[]{:S(2)}, u32[]{:S(2)}) collective-permute-start(bf16[320,512]{1,0:T(8,128)(2,1)S(1)} %get-tuple-element.56), channel_id=1, source_target_pairs={{0,1},{1,0},{2,3},{3,2},{4,5},{5,4},{6,7},{7,6},{8,9},{9,8},{10,11... | collective-permute-start | bytes 983048 | tf_op jit(solution)/shard_map/ppermute | solution.py:593
  50.4 1.8 %collective-permute-start.3 = (bf16[256,512]{1,0:T(8,128)(2,1)S(1)}, bf16[256,512]{1,0:T(8,128)(2,1)S(1)}, u32[]{:S(2)}, u32[]{:S(2)}) collective-permute-start(bf16[256,512]{1,0:T(8,128)(2,1)S(1)} %first_grad.1.one_ref), channel_id=1, source_target_pairs={{0,1},{1,0},{2,3},{3,2},{4,5},{5,4},{6,7},{7,6},{8,9},{9,8},{10,11... | collective-permute-start | bytes 786440 | tf_op jit(solution)/shard_map/ppermute | solution.py:593
  104.1 4.9 %collective-permute-start.5 = (bf16[64,48,128]{2,1,0:T(8,128)(2,1)S(1)}, bf16[64,48,128]{2,1,0:T(8,128)(2,1)S(1)}, u32[]{:S(2)}, u32[]{:S(2)}) collective-permute-start(bf16[64,48,128]{2,1,0:T(8,128)(2,1)S(1)} %all_to_all.22.own_ref), channel_id=1, source_target_pairs={{0,1},{1,0},{2,3},{3,2},{4,5},{5,4},{6,7},{7,6},{8,9},{9,8},{10,11... | collective-permute-start | bytes 2359304 | tf_op jit(solution)/shard_map/ppermute | solution.py:593

commit v8 on v7

--- a/solution.py
+++ b/solution.py
@@ -46,7 +46,7 @@
 def exact_dot(picks, values):
     high = values.astype(BF16)
     low = (values - high.astype(F32)).astype(BF16)
-    return dot(picks, high) + dot(picks, low)
+    return dot(jnp.concatenate([picks, picks], axis=1), jnp.concatenate([high, low], axis=0))
 
 
 def gelu_and_slope(values):
@@ -248,17 +248,13 @@
     front = pl.ds(pl.multiple_of(core * half, half), half)
     back = pl.ds(pl.multiple_of((1 - core) * half, half), half)
 
-    total = None
-    for chip in range(chips):
-        wide = jnp.concatenate([rows_ref[chip, pl.ds(0, cap), :], rows_ref[chip, pl.ds(cap, cap), :]], axis=1)
-        depth = [
-            w_own_ref[chip, front, :],
-            w_own_ref[chip, back, :],
-            w_other_ref[chip, back, :],
-            w_other_ref[chip, front, :],
-        ]
-        part = dot(wide, jnp.concatenate(depth, axis=0))
-        total = part if total is None else total + part
+    wides = [rows_ref[chip, pl.ds(start, cap), :] for chip in range(chips) for start in (0, cap)]
+    depths = [
+        weights[chip, spot, :]
+        for chip in range(chips)
+        for weights, spot in ((w_own_ref, front), (w_own_ref, back), (w_other_ref, back), (w_other_ref, front))
+    ]
+    total = dot(jnp.concatenate(wides, axis=1), jnp.concatenate(depths, axis=0))
     hidden_one, slope = gelu_and_slope(total + bias_one_ref[...])
     slope_one[...] = slope
 
@@ -267,7 +263,8 @@
     near_mid = (mid[mid_rows:] / fan_two).astype(BF16)
     mids[0] = self_mid
     mids[1] = near_mid
-    pre_two = dot(self_mid, w_two_ref[0]) + dot(near_mid, w_two_ref[1]) + bias_two_ref[...]
+    both = jnp.concatenate([self_mid, near_mid], axis=1)
+    pre_two = dot(both, jnp.concatenate([w_two_ref[0], w_two_ref[1]], axis=0)) + bias_two_ref[...]
     hidden_two, slope_two = gelu_and_slope(pre_two)
 
     top = dot(pick_three[...], hidden_two.astype(BF16))

time: 111 us -> 111 us (level)
  no operation moved by 1% of the time
where the time goes in v8:
time: 111 us
  blocking collectives  68.7 us (62%)
  Pallas kernels  24.8 us (22%)
  starting transfers between devices  13.7 us (12%)
  waiting for transfers between devices  2.42 us (2%)
    all_to_all x3, blocking collectives, exchange(): return lax.all_to_all(values, axes, 0, 0, tiled=True)  68.7 us
    pallas_call x1, Pallas kernels, gather_rows(): pl.pallas_call(gather_kernel, out_shape=jax.ShapeDtypeStruct((chips, 2 *...  12.8 us
    ppermute x6, starting transfers between devices, swap_core(): return lax.ppermute(values, 'core', [(0, 1), (1, 0)])  7.55 us
    all_to_all x1, starting transfers between devices, exchange(): return lax.all_to_all(values, axes, 0, 0, tiled=True)  6.14 us
    pallas_call x1, Pallas kernels, owner_pass(): pl.pallas_call(functools.partial(owner_kernel, *fans), out_shape=(jax.Sha...  3.32 us
  transfers between devices with their start and end apart: 7, of which 3 were waited for; matrix products, arithmetic and copies ran while one was open for 0% of the time, Pallas kernels for 20%

profile of v8, /device:TPU:1, one launch (start us, length us, event | category | flops | bytes accessed | tf_op | source)
XLA Modules:
  0.0 110.7 jit_solution(16290939996626870045)
XLA Ops:
  0.6 0.0 copy-start
  0.6 0.0 copy-start.13
  0.7 0.0 copy-start.2
  0.7 1.5 %collective-permute-start = (bf16[64,16384]{1,0:T(8,128)(2,1)}, bf16[64,16384]{1,0:T(8,128)(2,1)}, u32[]{:S(2)}, u32[]{:S(2)}) collective-permute-start(bf16[64,16384]{1,0:T(8,128)(2,1)} %own_ref.1), channel_id=1, source_target_pairs={{0,1},{1,0},{2,3},{3,2},{4,5},{5,4},{6,7},{7,6},{8,9},{9,8},{10,11... | collective-permute-start | bytes 6291464 | tf_op jit(solution)/shard_map/ppermute | solution.py:590
  2.2 1.9 %spread.1 = bf16[8,128,512]{2,1,0:T(8,128)(2,1)} custom-call(bf16[128,512]{1,0:T(8,128)(2,1)} %bitcast.22), custom_call_target="tpu_custom_call" | custom-call | tf_op jit(solution)/shard_map/spread/pallas_call | solution.py:186
  4.1 6.1 %all-to-all-start = ((bf16[8,128,512]{2,1,0:T(8,128)(2,1)}), bf16[8,128,512]{2,1,0:T(8,128)(2,1)}, u32[]{:S(2)}, u32[]{:S(2)}) async-start(bf16[8,128,512]{2,1,0:T(8,128)(2,1)} %spread.1), calls=%async_computation | async-start | bytes 2097152 | tf_op jit(solution)/shard_map/all_to_all | solution.py:586
  10.2 0.0 copy-done.13
  10.3 0.1 pad_add_fusion.place_ref
  10.4 0.0 copy-start.3
  10.4 0.0 copy-start.4
  10.4 0.0 copy-start.5
  10.4 0.0 copy-start.6
  10.4 0.0 collective-permute-done.other_ref
  10.4 0.0 copy-done
  10.4 0.0 copy-done.2
  10.4 12.8 %gather_rows.1 = bf16[8,512,128]{2,1,0:T(8,128)(2,1)S(1)} custom-call(s32[2]{0:T(128)S(1)} %pad_add_fusion.place_ref, bf16[64,16384]{1,0:T(8,128)(2,1)S(1)} %copy-done, bf16[64,16384]{1,0:T(8,128)(2,1)} %collective-permute-done.other_ref, s32[4096]{0:T(1024)S(1)} %copy-done.2, s32[20480]{0:T(1024)S(1)} %reshape.46.near_ref), custom_call_target="tpu_custom_call" | custom-call | flops 134217728 | bytes 41943040 | tf_op jit(solution)/shard_map/gather_rows/pallas_call | solution.py:156
  23.2 0.0 copy-start.1
  23.2 0.0 copy-start.7
  23.2 0.0 copy-start.8
  23.2 0.0 copy-start.9
  23.2 0.0 copy-start.10
  23.3 0.0 copy-start.11
  23.3 0.0 copy-start.12
  23.3 0.0 copy-done.3
  23.3 0.0 copy-done.4
  23.3 0.0 copy-done.5
  23.3 0.0 copy-done.6
  23.3 0.4 make_picks.1
  23.7 2.1 %all-to-all-done.w_own_ref = bf16[8,128,512]{2,1,0:T(8,128)(2,1)} async-done(((bf16[8,128,512]{2,1,0:T(8,128)(2,1)}), bf16[8,128,512]{2,1,0:T(8,128)(2,1)}, u32[]{:S(2)}, u32[]{:S(2)}) %all-to-all-start) | async-done | bytes 1048608 | tf_op jit(solution)/shard_map/all_to_all | solution.py:586
  25.8 1.3 %collective-permute-start.1 = (bf16[8,128,512]{2,1,0:T(8,128)(2,1)}, bf16[8,128,512]{2,1,0:T(8,128)(2,1)S(1)}, u32[]{:S(2)}, u32[]{:S(2)}) collective-permute-start(bf16[8,128,512]{2,1,0:T(8,128)(2,1)} %all-to-all-done.w_own_ref), channel_id=1, source_target_pairs={{0,1},{1,0},{2,3},{3,2},{4,5},{5,4},{6,7},{7,6},{8,9},{9,8},{10,11... | collective-permute-start | bytes 3145736 | tf_op jit(solution)/shard_map/ppermute | solution.py:590
  27.0 18.0 %all_to_all.20.rows_ref = bf16[8,512,128]{2,1,0:T(8,128)(2,1)S(1)} all-to-all(bf16[8,512,128]{2,1,0:T(8,128)(2,1)S(1)} %gather_rows.1), channel_id=1, replica_groups=mesh['y_hi'=2,'x'=4,'z'=4,'y_lo'=2,'core'=2] {'z','y_lo'}, dimensions={0} | all-to-all | bytes 2097152 | tf_op jit(solution)/shard_map/all_to_all | solution.py:586
  45.0 0.0 collective-permute-done.1.w_other_ref
  45.0 1.1 collective-permute-start.2
  46.1 0.0 copy-done.1
  46.1 0.0 copy-done.7
  46.1 0.0 copy-done.8
  46.1 0.0 copy-done.9
  46.1 0.0 copy-done.10
  46.1 0.0 copy-done.11
  46.1 0.0 copy-done.12
  46.2 3.3 %owner_pass.1 = (f32[256,512]{1,0:T(8,128)S(1)}, bf16[128,512]{1,0:T(8,128)(2,1)S(1)}, bf16[2,128,512]{2,1,0:T(8,128)(2,1)S(1)}, bf16[2,32,512]{2,1,0:T(8,128)(2...) custom-call(s32[2]{0:T(128)S(1)} %pad_add_fusion.place_ref, s32[128]{0:T(128)S(1)} %copy-done.11, ...), custom_call_target="tpu_custom_call" | custom-call | flops 2147483648 | bytes 10485760 | tf_op jit(solution)/shard_map/owner_pass/pallas_call | solution.py:395
  49.5 0.1 collective-permute-start.4
  49.6 0.7 first_grad.1.one_ref
  50.4 0.6 collective-permute-start.3
  50.9 0.3 collective-permute-done.4.ship_ref
  51.2 1.0 late_products.1.late_ref
  52.2 0.0 collective-permute-done.3.other_one_ref
  52.2 0.0 collective-permute-done.2.other_rows_ref
  52.2 0.8 one_products.1
  53.0 31.3 %all_to_all.21.parts_ref = bf16[64,104,128]{2,1,0:T(8,128)(2,1)S(1)} all-to-all(bf16[64,104,128]{2,1,0:T(8,128)(2,1)S(1)} %one_products.1), channel_id=1, replica_groups=mesh['y_hi'=2,'x'=4,'z'=4,'y_lo'=2,'core'=2] {'y_hi','x','z','y_lo'}, dimensions={0} | all-to-all | bytes 3407872 | tf_op jit(solution)/shard_map/all_to_all | solution.py:586
  84.3 0.3 sum_parts.1
  84.5 19.5 %all_to_all.22.own_ref = bf16[64,48,128]{2,1,0:T(8,128)(2,1)S(1)} all-to-all(bf16[64,48,128]{2,1,0:T(8,128)(2,1)S(1)} %sum_parts.1), channel_id=1, replica_groups=mesh['y_hi'=2,'x'=4,'z'=4,'y_lo'=2,'core'=2] {'y_hi','x','z','y_lo'}, dimensions={0} | all-to-all | bytes 1572864 | tf_op jit(solution)/shard_map/all_to_all | solution.py:586
  104.0 3.0 %collective-permute-start.5 = (bf16[64,48,128]{2,1,0:T(8,128)(2,1)S(1)}, bf16[64,48,128]{2,1,0:T(8,128)(2,1)S(1)}, u32[]{:S(2)}, u32[]{:S(2)}) collective-permute-start(bf16[64,48,128]{2,1,0:T(8,128)(2,1)S(1)} %all_to_all.22.own_ref), channel_id=1, source_target_pairs={{0,1},{1,0},{2,3},{3,2},{4,5},{5,4},{6,7},{7,6},{8,9},{9,8},{10,11... | collective-permute-start | bytes 2359304 | tf_op jit(solution)/shard_map/ppermute | solution.py:590
  107.0 1.8 %unpack_own.1 = (f32[2,64,512]{2,1,0:T(8,128)}, f32[2,512,512]{2,1,0:T(8,128)}, f32[2,112,512]{2,1,0:T(8,128)}, f32[16,512]{1,0:T(8,128)S(1)}) custom-call(s32[2]{0:T(128)S(1)} %pad_add_fusion.place_ref, bf16[64,48,128]{2,1,0:T(8,128)(2,1)S(1)} %all_to_all.22.own_ref), custom_call_target="tpu_custom_call" | custom-call | flops 4194304 | bytes 4194304 | tf_op jit(solution)/shard_map/unpack_own/pallas_call | solution.py:529
  108.9 0.1 collective-permute-done.5.other_ref
  108.9 1.8 %unpack_other.1 = (f32[2,512,512]{2,1,0:T(8,128)}, f32[2,112,512]{2,1,0:T(8,128)}, f32[1,512]{1,0:T(1,128)}, f32[1,512]{1,0:T(1,128)}, f32[1,112]{1,0:T(1,128)}) custom-call(s32[2]{0:T(128)S(1)} %pad_add_fusion.place_ref, bf16[64,48,128]{2,1,0:T(8,128)(2,1)S(1)} %collective-permute-done.5.other_ref, ...), custom_call_target="tpu_custom_call", output_to_operand_aliasing={{0}: (3, {}), {1}: (4, {})} | custom-call | tf_op jit(solution)/shard_map/unpack_other/pallas_call | solution.py:558
  (1 shorter events, 0.0 us)
Async XLA Ops:
  0.6 9.8 %copy-start = (bf16[64,16384]{1,0:T(8,128)(2,1)S(1)}, bf16[64,16384]{1,0:T(8,128)(2,1)}, u32[]{:S(2)}) copy-start(bf16[64,16384]{1,0:T(8,128)(2,1)} %own_ref.1) | copy-start | bytes 6291460
  0.6 9.6 %copy-start.13 = (s32[5,4096]{1,0:T(8,128)S(1)}, s32[5,4096]{1,0:T(8,128)}, u32[]{:S(2)}) copy-start(s32[5,4096]{1,0:T(8,128)} %param.17) | copy-start | bytes 245764
  0.7 9.8 %copy-start.2 = (s32[4096]{0:T(1024)S(1)}, s32[4096]{0:T(1024)}, u32[]{:S(2)}) copy-start(s32[4096]{0:T(1024)} %self_ref.1) | copy-start | bytes 49156
  0.7 9.7 %collective-permute-start = (bf16[64,16384]{1,0:T(8,128)(2,1)}, bf16[64,16384]{1,0:T(8,128)(2,1)}, u32[]{:S(2)}, u32[]{:S(2)}) collective-permute-start(bf16[64,16384]{1,0:T(8,128)(2,1)} %own_ref.1), channel_id=1, source_target_pairs={{0,1},{1,0},{2,3},{3,2},{4,5},{5,4},{6,7},{7,6},{8,9},{9,8},{10,11... | collective-permute-start | bytes 6291464 | tf_op jit(solution)/shard_map/ppermute | solution.py:590
  4.1 21.7 %all-to-all-start = ((bf16[8,128,512]{2,1,0:T(8,128)(2,1)}), bf16[8,128,512]{2,1,0:T(8,128)(2,1)}, u32[]{:S(2)}, u32[]{:S(2)}) async-start(bf16[8,128,512]{2,1,0:T(8,128)(2,1)} %spread.1), calls=%async_computation | async-start | bytes 2097152 | tf_op jit(solution)/shard_map/all_to_all | solution.py:586
  10.4 12.9 %copy-start.3 = (s32[10,128]{1,0:T(8,128)S(1)}, s32[10,128]{1,0:T(8,128)}, u32[]{:S(2)}) copy-start(s32[10,128]{1,0:T(8,128)} %near_two_ref.1) | copy-start | bytes 15364
  10.4 12.9 %copy-start.4 = (s32[15,32]{1,0:T(8,128)S(1)}, s32[15,32]{1,0:T(8,128)}, u32[]{:S(2)}) copy-start(s32[15,32]{1,0:T(8,128)} %near_three_ref.1) | copy-start | bytes 5764
  10.4 12.9 %copy-start.5 = (s32[128]{0:T(128)S(1)}, s32[128]{0:T(128)}, u32[]{:S(2)}) copy-start(s32[128]{0:T(128)} %param.18) | copy-start | bytes 1540
  10.4 12.9 %copy-start.6 = (s32[32]{0:T(128)S(1)}, s32[32]{0:T(128)}, u32[]{:S(2)}) copy-start(s32[32]{0:T(128)} %param.20) | copy-start | bytes 388
  23.2 22.9 %copy-start.1 = (bf16[2,512,512]{2,1,0:T(8,128)(2,1)S(1)}, bf16[2,512,512]{2,1,0:T(8,128)(2,1)}, u32[]{:S(2)}) copy-start(bf16[2,512,512]{2,1,0:T(8,128)(2,1)} %w_two_ref.3) | copy-start | bytes 3145732
  23.2 22.9 %copy-start.7 = (bf16[2,512,112]{1,2,0:T(8,128)(2,1)S(1)}, bf16[2,512,112]{1,2,0:T(8,128)(2,1)}, u32[]{:S(2)}) copy-start(bf16[2,512,112]{1,2,0:T(8,128)(2,1)} %param.28) | copy-start | bytes 688132
  23.2 22.9 %copy-start.8 = (s32[32,112]{1,0:T(8,128)S(1)}, s32[32,112]{1,0:T(8,128)}, u32[]{:S(2)}) copy-start(s32[32,112]{1,0:T(8,128)} %targets_ref.1) | copy-start | bytes 43012
  23.2 22.9 %copy-start.9 = (f32[512]{0:T(512)S(1)}, f32[512]{0:T(512)}, u32[]{:S(2)}) copy-start(f32[512]{0:T(512)} %param.25) | copy-start | bytes 6148
  23.2 22.9 %copy-start.10 = (f32[512]{0:T(512)S(1)}, f32[512]{0:T(512)}, u32[]{:S(2)}) copy-start(f32[512]{0:T(512)} %param.27) | copy-start | bytes 6148
  23.3 22.9 %copy-start.11 = (s32[128]{0:T(128)S(1)}, s32[128]{0:T(128)}, u32[]{:S(2)}) copy-start(s32[128]{0:T(128)} %count_ref.1) | copy-start | bytes 1540
  23.3 22.9 %copy-start.12 = (f32[112]{0:T(128)S(1)}, f32[112]{0:T(128)}, u32[]{:S(2)}) copy-start(f32[112]{0:T(128)} %param.29) | copy-start | bytes 1348
  25.8 19.3 %collective-permute-start.1 = (bf16[8,128,512]{2,1,0:T(8,128)(2,1)}, bf16[8,128,512]{2,1,0:T(8,128)(2,1)S(1)}, u32[]{:S(2)}, u32[]{:S(2)}) collective-permute-start(bf16[8,128,512]{2,1,0:T(8,128)(2,1)} %all-to-all-done.w_own_ref), channel_id=1, source_target_pairs={{0,1},{1,0},{2,3},{3,2},{4,5},{5,4},{6,7},{7,6},{8,9},{9,8},{10,11... | collective-permute-start | bytes 3145736 | tf_op jit(solution)/shard_map/ppermute | solution.py:590
  45.0 7.2 %collective-permute-start.2 = (bf16[8,512,128]{2,1,0:T(8,128)(2,1)S(1)}, bf16[8,512,128]{2,1,0:T(8,128)(2,1)S(1)}, u32[]{:S(2)}, u32[]{:S(2)}) collective-permute-start(bf16[8,512,128]{2,1,0:T(8,128)(2,1)S(1)} %all_to_all.20.rows_ref), channel_id=1, source_target_pairs={{0,1},{1,0},{2,3},{3,2},{4,5},{5,4},{6,7},{7,6},{8,9},{9,8},{10,11... | collective-permute-start | bytes 3145736 | tf_op jit(solution)/shard_map/ppermute | solution.py:590
  49.5 1.7 %collective-permute-start.4 = (bf16[320,512]{1,0:T(8,128)(2,1)S(1)}, bf16[320,512]{1,0:T(8,128)(2,1)S(1)}, u32[]{:S(2)}, u32[]{:S(2)}) collective-permute-start(bf16[320,512]{1,0:T(8,128)(2,1)S(1)} %get-tuple-element.56), channel_id=1, source_target_pairs={{0,1},{1,0},{2,3},{3,2},{4,5},{5,4},{6,7},{7,6},{8,9},{9,8},{10,11... | collective-permute-start | bytes 983048 | tf_op jit(solution)/shard_map/ppermute | solution.py:590
  50.4 1.8 %collective-permute-start.3 = (bf16[256,512]{1,0:T(8,128)(2,1)S(1)}, bf16[256,512]{1,0:T(8,128)(2,1)S(1)}, u32[]{:S(2)}, u32[]{:S(2)}) collective-permute-start(bf16[256,512]{1,0:T(8,128)(2,1)S(1)} %first_grad.1.one_ref), channel_id=1, source_target_pairs={{0,1},{1,0},{2,3},{3,2},{4,5},{5,4},{6,7},{7,6},{8,9},{9,8},{10,11... | collective-permute-start | bytes 786440 | tf_op jit(solution)/shard_map/ppermute | solution.py:590
  104.0 4.9 %collective-permute-start.5 = (bf16[64,48,128]{2,1,0:T(8,128)(2,1)S(1)}, bf16[64,48,128]{2,1,0:T(8,128)(2,1)S(1)}, u32[]{:S(2)}, u32[]{:S(2)}) collective-permute-start(bf16[64,48,128]{2,1,0:T(8,128)(2,1)S(1)} %all_to_all.22.own_ref), channel_id=1, source_target_pairs={{0,1},{1,0},{2,3},{3,2},{4,5},{5,4},{6,7},{7,6},{8,9},{9,8},{10,11... | collective-permute-start | bytes 2359304 | tf_op jit(solution)/shard_map/ppermute | solution.py:590

commit v9 on v8

--- a/solution.py
+++ b/solution.py
@@ -442,23 +442,23 @@
     count = hidden // PEERS
     pieces = sems.shape[0] - 1
     step = hidden // pieces
-    for peer in range(PEERS):
-        top[pl.ds(peer * count, count), :] = ref[peer].astype(F32)[SUB + TWO_ROWS :]
-    flipped = top[...].T
-    three[...] = flipped[:labels]
-    copies = [pltpu.make_async_copy(three, grad_three.at[side], sems.at[pieces])]
-    copies[0].start()
+    copies = []
     for peer in range(PEERS):
         cells = ref[peer].astype(F32)
         for tile in range(hidden // LANES):
             two[pl.ds(peer * count, count), pl.ds(tile * LANES, LANES)] = cells[
                 SUB + tile * count : SUB + (tile + 1) * count
             ]
+        top[pl.ds(peer * count, count), :] = cells[SUB + TWO_ROWS :]
         done = (peer + 1) * count
         if done % step == 0:
             spot = pl.ds(done - step, step)
-            copies.append(pltpu.make_async_copy(two.at[spot], grad_two.at[side, spot], sems.at[len(copies) - 1]))
+            copies.append(pltpu.make_async_copy(two.at[spot], grad_two.at[side, spot], sems.at[len(copies)]))
             copies[-1].start()
+    flipped = top[...].T
+    three[...] = flipped[:labels]
+    copies.append(pltpu.make_async_copy(three, grad_three.at[side], sems.at[pieces]))
+    copies[-1].start()
     return flipped[labels:], copies
 
 

time: 111 us -> 111 us (level)
  no operation moved by 1% of the time
where the time goes in v9:
time: 111 us
  blocking collectives  68.7 us (62%)
  Pallas kernels  24.7 us (22%)
  starting transfers between devices  13.7 us (12%)
  waiting for transfers between devices  2.46 us (2%)
    all_to_all x3, blocking collectives, exchange(): return lax.all_to_all(values, axes, 0, 0, tiled=True)  68.7 us
    pallas_call x1, Pallas kernels, gather_rows(): pl.pallas_call(gather_kernel, out_shape=jax.ShapeDtypeStruct((chips, 2 *...  12.8 us
    ppermute x6, starting transfers between devices, swap_core(): return lax.ppermute(values, 'core', [(0, 1), (1, 0)])  7.55 us
    all_to_all x1, starting transfers between devices, exchange(): return lax.all_to_all(values, axes, 0, 0, tiled=True)  6.14 us
    pallas_call x1, Pallas kernels, owner_pass(): pl.pallas_call(functools.partial(owner_kernel, *fans), out_shape=(jax.Sha...  3.32 us
  transfers between devices with their start and end apart: 7, of which 3 were waited for; matrix products, arithmetic and copies ran while one was open for 0% of the time, Pallas kernels for 20%

profile of v9, /device:TPU:1, one launch (start us, length us, event | category | flops | bytes accessed | tf_op | source)
XLA Modules:
  0.0 110.6 jit_solution(3512684269207631049)
XLA Ops:
  0.6 0.0 copy-start
  0.6 0.0 copy-start.13
  0.7 0.0 copy-start.2
  0.7 1.5 %collective-permute-start = (bf16[64,16384]{1,0:T(8,128)(2,1)}, bf16[64,16384]{1,0:T(8,128)(2,1)}, u32[]{:S(2)}, u32[]{:S(2)}) collective-permute-start(bf16[64,16384]{1,0:T(8,128)(2,1)} %own_ref.1), channel_id=1, source_target_pairs={{0,1},{1,0},{2,3},{3,2},{4,5},{5,4},{6,7},{7,6},{8,9},{9,8},{10,11... | collective-permute-start | bytes 6291464 | tf_op jit(solution)/shard_map/ppermute | solution.py:590
  2.2 1.9 %spread.1 = bf16[8,128,512]{2,1,0:T(8,128)(2,1)} custom-call(bf16[128,512]{1,0:T(8,128)(2,1)} %bitcast.22), custom_call_target="tpu_custom_call" | custom-call | tf_op jit(solution)/shard_map/spread/pallas_call | solution.py:186
  4.1 6.1 %all-to-all-start = ((bf16[8,128,512]{2,1,0:T(8,128)(2,1)}), bf16[8,128,512]{2,1,0:T(8,128)(2,1)}, u32[]{:S(2)}, u32[]{:S(2)}) async-start(bf16[8,128,512]{2,1,0:T(8,128)(2,1)} %spread.1), calls=%async_computation | async-start | bytes 2097152 | tf_op jit(solution)/shard_map/all_to_all | solution.py:586
  10.2 0.0 copy-done.13
  10.3 0.1 pad_add_fusion.place_ref
  10.4 0.0 copy-start.3
  10.4 0.0 copy-start.4
  10.4 0.0 copy-start.5
  10.4 0.0 copy-start.6
  10.4 0.0 collective-permute-done.other_ref
  10.4 0.0 copy-done
  10.4 0.0 copy-done.2
  10.4 12.8 %gather_rows.1 = bf16[8,512,128]{2,1,0:T(8,128)(2,1)S(1)} custom-call(s32[2]{0:T(128)S(1)} %pad_add_fusion.place_ref, bf16[64,16384]{1,0:T(8,128)(2,1)S(1)} %copy-done, bf16[64,16384]{1,0:T(8,128)(2,1)} %collective-permute-done.other_ref, s32[4096]{0:T(1024)S(1)} %copy-done.2, s32[20480]{0:T(1024)S(1)} %reshape.46.near_ref), custom_call_target="tpu_custom_call" | custom-call | flops 134217728 | bytes 41943040 | tf_op jit(solution)/shard_map/gather_rows/pallas_call | solution.py:156
  23.2 0.0 copy-start.1
  23.2 0.0 copy-start.7
  23.2 0.0 copy-start.8
  23.2 0.0 copy-start.9
  23.2 0.0 copy-start.10
  23.3 0.0 copy-start.11
  23.3 0.0 copy-start.12
  23.3 0.0 copy-done.3
  23.3 0.0 copy-done.4
  23.3 0.0 copy-done.5
  23.3 0.0 copy-done.6
  23.3 0.4 make_picks.1
  23.7 2.1 %all-to-all-done.w_own_ref = bf16[8,128,512]{2,1,0:T(8,128)(2,1)} async-done(((bf16[8,128,512]{2,1,0:T(8,128)(2,1)}), bf16[8,128,512]{2,1,0:T(8,128)(2,1)}, u32[]{:S(2)}, u32[]{:S(2)}) %all-to-all-start) | async-done | bytes 1048608 | tf_op jit(solution)/shard_map/all_to_all | solution.py:586
  25.8 1.3 %collective-permute-start.1 = (bf16[8,128,512]{2,1,0:T(8,128)(2,1)}, bf16[8,128,512]{2,1,0:T(8,128)(2,1)S(1)}, u32[]{:S(2)}, u32[]{:S(2)}) collective-permute-start(bf16[8,128,512]{2,1,0:T(8,128)(2,1)} %all-to-all-done.w_own_ref), channel_id=1, source_target_pairs={{0,1},{1,0},{2,3},{3,2},{4,5},{5,4},{6,7},{7,6},{8,9},{9,8},{10,11... | collective-permute-start | bytes 3145736 | tf_op jit(solution)/shard_map/ppermute | solution.py:590
  27.0 18.0 %all_to_all.20.rows_ref = bf16[8,512,128]{2,1,0:T(8,128)(2,1)S(1)} all-to-all(bf16[8,512,128]{2,1,0:T(8,128)(2,1)S(1)} %gather_rows.1), channel_id=1, replica_groups=mesh['y_hi'=2,'x'=4,'z'=4,'y_lo'=2,'core'=2] {'z','y_lo'}, dimensions={0} | all-to-all | bytes 2097152 | tf_op jit(solution)/shard_map/all_to_all | solution.py:586
  45.0 0.0 collective-permute-done.1.w_other_ref
  45.0 1.1 collective-permute-start.2
  46.1 0.0 copy-done.1
  46.1 0.0 copy-done.7
  46.1 0.0 copy-done.8
  46.1 0.0 copy-done.9
  46.1 0.0 copy-done.10
  46.1 0.0 copy-done.11
  46.1 0.0 copy-done.12
  46.2 3.3 %owner_pass.1 = (f32[256,512]{1,0:T(8,128)S(1)}, bf16[128,512]{1,0:T(8,128)(2,1)S(1)}, bf16[2,128,512]{2,1,0:T(8,128)(2,1)S(1)}, bf16[2,32,512]{2,1,0:T(8,128)(2...) custom-call(s32[2]{0:T(128)S(1)} %pad_add_fusion.place_ref, s32[128]{0:T(128)S(1)} %copy-done.11, ...), custom_call_target="tpu_custom_call" | custom-call | flops 2147483648 | bytes 10485760 | tf_op jit(solution)/shard_map/owner_pass/pallas_call | solution.py:395
  49.5 0.1 collective-permute-start.4
  49.6 0.7 first_grad.1.one_ref
  50.4 0.6 collective-permute-start.3
  50.9 0.3 collective-permute-done.4.ship_ref
  51.2 1.0 late_products.1.late_ref
  52.2 0.0 collective-permute-done.3.other_one_ref
  52.2 0.0 collective-permute-done.2.other_rows_ref
  52.2 0.8 one_products.1
  53.0 31.3 %all_to_all.21.parts_ref = bf16[64,104,128]{2,1,0:T(8,128)(2,1)S(1)} all-to-all(bf16[64,104,128]{2,1,0:T(8,128)(2,1)S(1)} %one_products.1), channel_id=1, replica_groups=mesh['y_hi'=2,'x'=4,'z'=4,'y_lo'=2,'core'=2] {'y_hi','x','z','y_lo'}, dimensions={0} | all-to-all | bytes 3407872 | tf_op jit(solution)/shard_map/all_to_all | solution.py:586
  84.3 0.3 sum_parts.1
  84.5 19.5 %all_to_all.22.own_ref = bf16[64,48,128]{2,1,0:T(8,128)(2,1)S(1)} all-to-all(bf16[64,48,128]{2,1,0:T(8,128)(2,1)S(1)} %sum_parts.1), channel_id=1, replica_groups=mesh['y_hi'=2,'x'=4,'z'=4,'y_lo'=2,'core'=2] {'y_hi','x','z','y_lo'}, dimensions={0} | all-to-all | bytes 1572864 | tf_op jit(solution)/shard_map/all_to_all | solution.py:586
  104.0 3.0 %collective-permute-start.5 = (bf16[64,48,128]{2,1,0:T(8,128)(2,1)S(1)}, bf16[64,48,128]{2,1,0:T(8,128)(2,1)S(1)}, u32[]{:S(2)}, u32[]{:S(2)}) collective-permute-start(bf16[64,48,128]{2,1,0:T(8,128)(2,1)S(1)} %all_to_all.22.own_ref), channel_id=1, source_target_pairs={{0,1},{1,0},{2,3},{3,2},{4,5},{5,4},{6,7},{7,6},{8,9},{9,8},{10,11... | collective-permute-start | bytes 2359304 | tf_op jit(solution)/shard_map/ppermute | solution.py:590
  107.0 1.8 %unpack_own.1 = (f32[2,64,512]{2,1,0:T(8,128)}, f32[2,512,512]{2,1,0:T(8,128)}, f32[2,112,512]{2,1,0:T(8,128)}, f32[16,512]{1,0:T(8,128)S(1)}) custom-call(s32[2]{0:T(128)S(1)} %pad_add_fusion.place_ref, bf16[64,48,128]{2,1,0:T(8,128)(2,1)S(1)} %all_to_all.22.own_ref), custom_call_target="tpu_custom_call" | custom-call | flops 4194304 | bytes 4194304 | tf_op jit(solution)/shard_map/unpack_own/pallas_call | solution.py:529
  108.8 0.1 collective-permute-done.5.other_ref
  108.9 1.7 %unpack_other.1 = (f32[2,512,512]{2,1,0:T(8,128)}, f32[2,112,512]{2,1,0:T(8,128)}, f32[1,512]{1,0:T(1,128)}, f32[1,512]{1,0:T(1,128)}, f32[1,112]{1,0:T(1,128)}) custom-call(s32[2]{0:T(128)S(1)} %pad_add_fusion.place_ref, bf16[64,48,128]{2,1,0:T(8,128)(2,1)S(1)} %collective-permute-done.5.other_ref, ...), custom_call_target="tpu_custom_call", output_to_operand_aliasing={{0}: (3, {}), {1}: (4, {})} | custom-call | tf_op jit(solution)/shard_map/unpack_other/pallas_call | solution.py:558
  (1 shorter events, 0.0 us)
Async XLA Ops:
  0.6 9.8 %copy-start = (bf16[64,16384]{1,0:T(8,128)(2,1)S(1)}, bf16[64,16384]{1,0:T(8,128)(2,1)}, u32[]{:S(2)}) copy-start(bf16[64,16384]{1,0:T(8,128)(2,1)} %own_ref.1) | copy-start | bytes 6291460
  0.6 9.6 %copy-start.13 = (s32[5,4096]{1,0:T(8,128)S(1)}, s32[5,4096]{1,0:T(8,128)}, u32[]{:S(2)}) copy-start(s32[5,4096]{1,0:T(8,128)} %param.17) | copy-start | bytes 245764
  0.7 9.8 %copy-start.2 = (s32[4096]{0:T(1024)S(1)}, s32[4096]{0:T(1024)}, u32[]{:S(2)}) copy-start(s32[4096]{0:T(1024)} %self_ref.1) | copy-start | bytes 49156
  0.7 9.7 %collective-permute-start = (bf16[64,16384]{1,0:T(8,128)(2,1)}, bf16[64,16384]{1,0:T(8,128)(2,1)}, u32[]{:S(2)}, u32[]{:S(2)}) collective-permute-start(bf16[64,16384]{1,0:T(8,128)(2,1)} %own_ref.1), channel_id=1, source_target_pairs={{0,1},{1,0},{2,3},{3,2},{4,5},{5,4},{6,7},{7,6},{8,9},{9,8},{10,11... | collective-permute-start | bytes 6291464 | tf_op jit(solution)/shard_map/ppermute | solution.py:590
  4.1 21.7 %all-to-all-start = ((bf16[8,128,512]{2,1,0:T(8,128)(2,1)}), bf16[8,128,512]{2,1,0:T(8,128)(2,1)}, u32[]{:S(2)}, u32[]{:S(2)}) async-start(bf16[8,128,512]{2,1,0:T(8,128)(2,1)} %spread.1), calls=%async_computation | async-start | bytes 2097152 | tf_op jit(solution)/shard_map/all_to_all | solution.py:586
  10.4 12.9 %copy-start.3 = (s32[10,128]{1,0:T(8,128)S(1)}, s32[10,128]{1,0:T(8,128)}, u32[]{:S(2)}) copy-start(s32[10,128]{1,0:T(8,128)} %near_two_ref.1) | copy-start | bytes 15364
  10.4 12.9 %copy-start.4 = (s32[15,32]{1,0:T(8,128)S(1)}, s32[15,32]{1,0:T(8,128)}, u32[]{:S(2)}) copy-start(s32[15,32]{1,0:T(8,128)} %near_three_ref.1) | copy-start | bytes 5764
  10.4 12.9 %copy-start.5 = (s32[128]{0:T(128)S(1)}, s32[128]{0:T(128)}, u32[]{:S(2)}) copy-start(s32[128]{0:T(128)} %param.18) | copy-start | bytes 1540
  10.4 12.9 %copy-start.6 = (s32[32]{0:T(128)S(1)}, s32[32]{0:T(128)}, u32[]{:S(2)}) copy-start(s32[32]{0:T(128)} %param.20) | copy-start | bytes 388
  23.2 22.9 %copy-start.1 = (bf16[2,512,512]{2,1,0:T(8,128)(2,1)S(1)}, bf16[2,512,512]{2,1,0:T(8,128)(2,1)}, u32[]{:S(2)}) copy-start(bf16[2,512,512]{2,1,0:T(8,128)(2,1)} %w_two_ref.3) | copy-start | bytes 3145732
  23.2 22.9 %copy-start.7 = (bf16[2,512,112]{1,2,0:T(8,128)(2,1)S(1)}, bf16[2,512,112]{1,2,0:T(8,128)(2,1)}, u32[]{:S(2)}) copy-start(bf16[2,512,112]{1,2,0:T(8,128)(2,1)} %param.28) | copy-start | bytes 688132
  23.2 22.9 %copy-start.8 = (s32[32,112]{1,0:T(8,128)S(1)}, s32[32,112]{1,0:T(8,128)}, u32[]{:S(2)}) copy-start(s32[32,112]{1,0:T(8,128)} %targets_ref.1) | copy-start | bytes 43012
  23.2 22.9 %copy-start.9 = (f32[512]{0:T(512)S(1)}, f32[512]{0:T(512)}, u32[]{:S(2)}) copy-start(f32[512]{0:T(512)} %param.25) | copy-start | bytes 6148
  23.2 22.9 %copy-start.10 = (f32[512]{0:T(512)S(1)}, f32[512]{0:T(512)}, u32[]{:S(2)}) copy-start(f32[512]{0:T(512)} %param.27) | copy-start | bytes 6148
  23.3 22.9 %copy-start.11 = (s32[128]{0:T(128)S(1)}, s32[128]{0:T(128)}, u32[]{:S(2)}) copy-start(s32[128]{0:T(128)} %count_ref.1) | copy-start | bytes 1540
  23.3 22.9 %copy-start.12 = (f32[112]{0:T(128)S(1)}, f32[112]{0:T(128)}, u32[]{:S(2)}) copy-start(f32[112]{0:T(128)} %param.29) | copy-start | bytes 1348
  25.8 19.3 %collective-permute-start.1 = (bf16[8,128,512]{2,1,0:T(8,128)(2,1)}, bf16[8,128,512]{2,1,0:T(8,128)(2,1)S(1)}, u32[]{:S(2)}, u32[]{:S(2)}) collective-permute-start(bf16[8,128,512]{2,1,0:T(8,128)(2,1)} %all-to-all-done.w_own_ref), channel_id=1, source_target_pairs={{0,1},{1,0},{2,3},{3,2},{4,5},{5,4},{6,7},{7,6},{8,9},{9,8},{10,11... | collective-permute-start | bytes 3145736 | tf_op jit(solution)/shard_map/ppermute | solution.py:590
  45.0 7.2 %collective-permute-start.2 = (bf16[8,512,128]{2,1,0:T(8,128)(2,1)S(1)}, bf16[8,512,128]{2,1,0:T(8,128)(2,1)S(1)}, u32[]{:S(2)}, u32[]{:S(2)}) collective-permute-start(bf16[8,512,128]{2,1,0:T(8,128)(2,1)S(1)} %all_to_all.20.rows_ref), channel_id=1, source_target_pairs={{0,1},{1,0},{2,3},{3,2},{4,5},{5,4},{6,7},{7,6},{8,9},{9,8},{10,11... | collective-permute-start | bytes 3145736 | tf_op jit(solution)/shard_map/ppermute | solution.py:590
  49.5 1.7 %collective-permute-start.4 = (bf16[320,512]{1,0:T(8,128)(2,1)S(1)}, bf16[320,512]{1,0:T(8,128)(2,1)S(1)}, u32[]{:S(2)}, u32[]{:S(2)}) collective-permute-start(bf16[320,512]{1,0:T(8,128)(2,1)S(1)} %get-tuple-element.56), channel_id=1, source_target_pairs={{0,1},{1,0},{2,3},{3,2},{4,5},{5,4},{6,7},{7,6},{8,9},{9,8},{10,11... | collective-permute-start | bytes 983048 | tf_op jit(solution)/shard_map/ppermute | solution.py:590
  50.4 1.8 %collective-permute-start.3 = (bf16[256,512]{1,0:T(8,128)(2,1)S(1)}, bf16[256,512]{1,0:T(8,128)(2,1)S(1)}, u32[]{:S(2)}, u32[]{:S(2)}) collective-permute-start(bf16[256,512]{1,0:T(8,128)(2,1)S(1)} %first_grad.1.one_ref), channel_id=1, source_target_pairs={{0,1},{1,0},{2,3},{3,2},{4,5},{5,4},{6,7},{7,6},{8,9},{9,8},{10,11... | collective-permute-start | bytes 786440 | tf_op jit(solution)/shard_map/ppermute | solution.py:590
  104.0 4.9 %collective-permute-start.5 = (bf16[64,48,128]{2,1,0:T(8,128)(2,1)S(1)}, bf16[64,48,128]{2,1,0:T(8,128)(2,1)S(1)}, u32[]{:S(2)}, u32[]{:S(2)}) collective-permute-start(bf16[64,48,128]{2,1,0:T(8,128)(2,1)S(1)} %all_to_all.22.own_ref), channel_id=1, source_target_pairs={{0,1},{1,0},{2,3},{3,2},{4,5},{5,4},{6,7},{7,6},{8,9},{9,8},{10,11... | collective-permute-start | bytes 2359304 | tf_op jit(solution)/shard_map/ppermute | solution.py:590
